TPU v7x, 512 devices: a whole 4x8x8 slice. The times are simulated.
512 devices in a mesh: shell: 8 (over y), lat: 64 (over x, z, core).
Axes of the slice: x: 4, y: 8, z: 8, core: 2. Of those that a mesh axis runs over, the one named last changes fastest.
Arguments:
- solution: float32 [3, 64, 4096, 128], P(None, 'shell', 'lat'), may hold values from -6 to 6
- right_side: float32 [3, 64, 4096, 128], P(None, 'shell', 'lat'), may hold values from -20000 to 20000
- viscosity: float32 [64, 4096, 128], P('shell', 'lat'), may hold values from 3e-05 to 30000, as said below
- stencil_weights: float32 [7], replicated, may hold values from 0.3 to 3
Outputs:
- smoothed: float32 [3, 64, 4096, 128], P(None, 'shell', 'lat')
- coarse: float32 [3, 32, 2048, 64], P(None, 'shell', 'lat')
Inputs may be any that keep to these rules, and one draw needn't show every extreme that they name: `viscosity`: positive.
All inputs are finite; a program needn't handle non-finite values.
Results may differ from a plain program's by a relative error of at most 0.00002.
Values sent between devices are 32-bit elements; how exact they have to be, the bound alone decides.
No kernel may reach another device: no remote copies, remote signals or barrier semaphores. Data moves between devices by JAX's collectives and lax.ppermute only.
A program may use at most 64 MiB of HBM per device.

v0:
```python
import jax
import jax.numpy as jnp
from jax import lax
from jax.sharding import PartitionSpec as P

OFFSETS = ((1, 0, 0), (0, 1, 0), (0, 0, 1), (1, 1, 0), (1, 0, 1), (0, 1, 1), (1, 1, 1))
OMEGA = 0.6


def padded_2(array, sides, width):
    for axis, dim in sides:
        size, length = (lax.axis_size(axis), array.shape[dim])
        up = [(i, (i + 1) % size) for i in range(size - 1)]
        down = [(j, i) for i, j in up]
        last = lax.slice_in_dim(array, length - width, length, axis=dim)
        initial = lax.slice_in_dim(array, 0, width, axis=dim)
        before = lax.ppermute(last, axis, up)
        after = lax.ppermute(initial, axis, down)
        array = jnp.concatenate([before, array, after], axis=dim)
    return array


def from_behind(value, axis, steps):
    count = lax.axis_size(axis)
    initial, last = (max(0, -steps), min(count, count - steps))
    return lax.ppermute(value, axis, [(source, source + steps) for source in range(initial, last)])


def moved(field, first, second, third):
    size_a, size_b, size_c = field.shape[-3:]
    return field[
        ...,
        1 + first : size_a - 1 + first,
        1 + second : size_b - 1 + second,
        1 + third : size_c - 1 + third,
    ]


def stencil(upad, npad, weights):
    uz = jnp.pad(upad, ((0, 0), (0, 0), (0, 0), (1, 1)))
    nz = jnp.pad(npad, ((0, 0), (0, 0), (1, 1)))
    ucenter = moved(uz, 0, 0, 0)
    ncenter = moved(nz, 0, 0, 0)
    diag = jnp.zeros_like(ncenter)
    offsum = jnp.zeros_like(ucenter)
    for index, step in enumerate(OFFSETS):
        for sign in (1, -1):
            coef = (
                weights[index]
                * 0.5
                * (ncenter + moved(nz, sign * step[0], sign * step[1], sign * step[2]))
            )
            diag = diag + coef
            offsum = offsum + coef * moved(uz, sign * step[0], sign * step[1], sign * step[2])
    return (diag * ucenter - offsum, diag, ucenter)


def halve(field, axis, following):
    count = field.shape[axis]
    joined = jnp.concatenate([field, following], axis)
    first = lax.slice_in_dim(joined, 0, count, 2, axis)
    middle = lax.slice_in_dim(joined, 1, count, 2, axis)
    last = lax.slice_in_dim(joined, 2, count + 1, 2, axis)
    return 0.25 * first + 0.5 * middle + 0.25 * last


def refresh(field):
    return padded_2(field, (("shell", 1), ("lat", 2)), 1)


def per_device(solution, right_side, viscosity, stencil_weights):
    stacked = jnp.concatenate([solution, viscosity[None]], 0)
    padded = padded_2(stacked, (("shell", 1), ("lat", 2)), 1)
    npad = padded[3]
    upad = padded[:3]
    current = solution
    for turn in range(3):
        if turn > 0:
            upad = refresh(current)
        image, diag, ucenter = stencil(upad, npad, stencil_weights)
        if turn < 2:
            current = current + OMEGA * (right_side - image) / diag
    scaled = (right_side - image) / diag
    upper = from_behind(scaled[:, 0:1], "shell", -1)
    radial = halve(scaled, 1, upper)
    beside = from_behind(radial[:, :, 0:1], "lat", -1)
    lateral = halve(radial, 2, beside)
    tail = jnp.zeros_like(lateral[:, :, :, 0:1])
    return (current, halve(lateral, 3, tail))


def solution(mesh):
    in_specs = (
        P(None, "shell", "lat", None),
        P(None, "shell", "lat", None),
        P("shell", "lat", None),
        P(),
    )
    out_specs = (P(None, "shell", "lat", None), P(None, "shell", "lat", None))
    return jax.shard_map(
        per_device, mesh=mesh, in_specs=in_specs, out_specs=out_specs, check_vma=False
    )
```

profile of v0, /device:TPU:30, one launch (start us, length us, event | category | flops | bytes accessed | tf_op | source)
XLA Modules:
  0.0 106.2 jit_solution(14839335242404385653)
XLA Ops:
  0.6 0.0 copy-start
  0.6 0.0 copy-start.2
  0.7 0.0 copy-start.4
  0.7 1.1 %pad_maximum_fusion.14 = (f32[4,1,64,128]{3,2,1,0:T(8,128)S(1)}, f32[4,1,64,128]{3,2,1,0:T(8,128)S(1)}) fusion(f32[1,8,64,128]{3,2,1,0:T(8,128)} %bitcast.10, f32[3,8,64,128]{3,2,1,0:T(8,128)} %param.4), kind=kLoop, calls=%fused_computation.168 | loop fusion | flops 65536 | bytes 1310720 | tf_op jit(solution)/shard_map/slice | solution.py:15
  1.8 4.7 %collective-permute-start = (f32[4,1,64,128]{3,2,1,0:T(8,128)S(1)}, f32[4,1,64,128]{3,2,1,0:T(8,128)S(1)}, u32[]{:S(2)}, u32[]{:S(2)}) collective-permute-start(f32[4,1,64,128]{3,2,1,0:T(8,128)S(1)} %get-tuple-element.21), channel_id=1, source_target_pairs={{0,64},{64,128},{128,192},{192,256},{256,320},{320,384},{384,448},... | collective-permute-start | bytes 393224 | tf_op jit(solution)/shard_map/ppermute | solution.py:17
  6.5 1.9 %collective-permute-start.1 = (f32[4,1,64,128]{3,2,1,0:T(8,128)S(1)}, f32[4,1,64,128]{3,2,1,0:T(8,128)S(1)}, u32[]{:S(2)}, u32[]{:S(2)}) collective-permute-start(f32[4,1,64,128]{3,2,1,0:T(8,128)S(1)} %get-tuple-element.22), channel_id=1, source_target_pairs={{64,0},{128,64},{192,128},{256,192},{320,256},{384,320},{448,384},... | collective-permute-start | bytes 393224 | tf_op jit(solution)/shard_map/ppermute | solution.py:18
  8.4 0.8 collective-permute-done
  9.2 5.3 %collective-permute-done.1 = f32[4,1,64,128]{3,2,1,0:T(8,128)S(1)} collective-permute-done((f32[4,1,64,128]{3,2,1,0:T(8,128)S(1)}, f32[4,1,64,128]{3,2,1,0:T(8,128)S(1)}, u32[]{:S(2)}, u32[]{:S(2)}) %collective-permute-start.1) | collective-permute-done | bytes 131104 | tf_op jit(solution)/shard_map/ppermute | solution.py:18
  14.5 1.0 pad_maximum_fusion.18
  15.5 1.9 %collective-permute-start.2 = (f32[4,10,1,128]{3,2,1,0:T(1,128)S(1)}, f32[4,10,1,128]{3,2,1,0:T(1,128)S(1)}, u32[]{:S(2)}, u32[]{:S(2)}) collective-permute-start(f32[4,10,1,128]{3,2,1,0:T(1,128)S(1)} %get-tuple-element.19), channel_id=1, source_target_pairs={{0,1},{1,2},{2,3},{3,4},{4,5},{5,6},{6,7},{7,8},{8,9},{9,10},{10,1... | collective-permute-start | bytes 61448 | tf_op jit(solution)/shard_map/ppermute | solution.py:17
  17.5 9.2 %collective-permute-start.3 = (f32[4,10,1,128]{3,2,1,0:T(1,128)S(1)}, f32[4,10,1,128]{3,2,1,0:T(1,128)S(1)}, u32[]{:S(2)}, u32[]{:S(2)}) collective-permute-start(f32[4,10,1,128]{3,2,1,0:T(1,128)S(1)} %get-tuple-element.20), channel_id=1, source_target_pairs={{1,0},{2,1},{3,2},{4,3},{5,4},{6,5},{7,6},{8,7},{9,8},{10,9},{11,1... | collective-permute-start | bytes 61448 | tf_op jit(solution)/shard_map/ppermute | solution.py:18
  26.7 0.0 copy-done.4
  26.7 0.7 fusion.97
  31.8 0.0 collective-permute-done.2
  31.8 0.0 collective-permute-done.3
  31.8 0.0 copy-done
  31.9 0.0 copy-done.2
  31.9 0.6 add_add_fusion
  32.6 0.8 select_maximum_fusion.8
  33.4 0.0 copy-start.3
  33.4 0.3 pad_maximum_fusion
  33.7 0.9 copy-done.3
  34.5 2.2 %fusion.44 = f32[3,8,64,128]{3,2,1,0:T(8,128)S(1)} fusion(f32[3,8,64,128]{3,2,1,0:T(8,128)S(1)} %copy-done, f32[3,8,64,128]{3,2,1,0:T(8,128)S(1)} %copy-done.3, f32[3,10,66,130]{3,2,1,0:T(8,128)S(1)} %select_maximum_fusion.8, f32[4,10,65,128]{3,2,1,0:T(8,128)S(1)} %get-tuple-element.18, f32[4,10,65,128]{3,2,1,0:T(8,128)S(1)} %get-tuple-element.17, ...), kind=kLoop, calls=%fused_computation.103 | loop fusion | flops 7274496 | bytes 16252928 | tf_op jit(solution)/shard_map/add | solution.py:82
  36.8 1.9 %collective-permute-start.5 = (f32[3,1,64,128]{3,2,1,0:T(8,128)S(1)}, f32[3,1,64,128]{3,2,1,0:T(8,128)S(1)}, u32[]{:S(2)}, u32[]{:S(2)}) collective-permute-start(f32[3,1,64,128]{3,2,1,0:T(8,128)S(1)} %get-tuple-element.33), channel_id=1, source_target_pairs={{0,64},{64,128},{128,192},{192,256},{256,320},{320,384},{384,448},... | collective-permute-start | bytes 294920 | tf_op jit(solution)/shard_map/ppermute | solution.py:17
  38.7 3.9 %collective-permute-start.4 = (f32[3,1,64,128]{3,2,1,0:T(8,128)S(1)}, f32[3,1,64,128]{3,2,1,0:T(8,128)S(1)}, u32[]{:S(2)}, u32[]{:S(2)}) collective-permute-start(f32[3,1,64,128]{3,2,1,0:T(8,128)S(1)} %get-tuple-element.34), channel_id=1, source_target_pairs={{64,0},{128,64},{192,128},{256,192},{320,256},{384,320},{448,384},... | collective-permute-start | bytes 294920 | tf_op jit(solution)/shard_map/ppermute | solution.py:18
  42.6 0.7 collective-permute-done.5
  43.3 3.1 %collective-permute-done.4 = f32[3,1,64,128]{3,2,1,0:T(8,128)S(1)} collective-permute-done((f32[3,1,64,128]{3,2,1,0:T(8,128)S(1)}, f32[3,1,64,128]{3,2,1,0:T(8,128)S(1)}, u32[]{:S(2)}, u32[]{:S(2)}) %collective-permute-start.4) | collective-permute-done | bytes 98336 | tf_op jit(solution)/shard_map/ppermute | solution.py:18
  46.4 1.9 %collective-permute-start.7 = (f32[3,10,1,128]{3,2,1,0:T(1,128)S(1)}, f32[3,10,1,128]{3,2,1,0:T(1,128)S(1)}, u32[]{:S(2)}, u32[]{:S(2)}) collective-permute-start(f32[3,10,1,128]{3,2,1,0:T(1,128)S(1)} %get-tuple-element.29), channel_id=1, source_target_pairs={{0,1},{1,2},{2,3},{3,4},{4,5},{5,6},{6,7},{7,8},{8,9},{9,10},{10,1... | collective-permute-start | bytes 46088 | tf_op jit(solution)/shard_map/ppermute | solution.py:17
  48.4 5.8 %collective-permute-start.6 = (f32[3,10,1,128]{3,2,1,0:T(1,128)S(1)}, f32[3,10,1,128]{3,2,1,0:T(1,128)S(1)}, u32[]{:S(2)}, u32[]{:S(2)}) collective-permute-start(f32[3,10,1,128]{3,2,1,0:T(1,128)S(1)} %get-tuple-element.30), channel_id=1, source_target_pairs={{1,0},{2,1},{3,2},{4,3},{5,4},{6,5},{7,6},{8,7},{9,8},{10,9},{11,1... | collective-permute-start | bytes 46088 | tf_op jit(solution)/shard_map/ppermute | solution.py:18
  54.1 0.0 collective-permute-done.7
  54.1 1.4 %collective-permute-done.6 = f32[3,10,1,128]{3,2,1,0:T(1,128)S(1)} collective-permute-done((f32[3,10,1,128]{3,2,1,0:T(1,128)S(1)}, f32[3,10,1,128]{3,2,1,0:T(1,128)S(1)}, u32[]{:S(2)}, u32[]{:S(2)}) %collective-permute-start.6) | collective-permute-done | bytes 15392 | tf_op jit(solution)/shard_map/ppermute | solution.py:18
  55.5 0.8 select_maximum_fusion.4
  56.3 0.2 pad_maximum_fusion.1
  56.5 2.3 %fusion.24 = f32[3,8,64,128]{3,2,1,0:T(8,128)S(1)} fusion(f32[3,8,64,128]{3,2,1,0:T(8,128)S(1)} %fusion.44, f32[3,8,64,128]{3,2,1,0:T(8,128)S(1)} %copy-done.3, f32[3,10,66,130]{3,2,1,0:T(8,128)S(1)} %select_maximum_fusion.4, f32[3,10,65,128]{3,2,1,0:T(8,128)S(1)} %get-tuple-element.28, f32[3,10,65,128]{3,2,1,0:T(8,128)S(1)} %get-tuple-element.27, ...), kind=kLoop, calls=%fused_computation.69 | loop fusion | flops 6881280 | bytes 15925248 | tf_op jit(solution)/shard_map/add | solution.py:82
  58.8 0.0 copy-start.1
  58.8 1.9 %collective-permute-start.9 = (f32[3,1,64,128]{3,2,1,0:T(8,128)S(1)}, f32[3,1,64,128]{3,2,1,0:T(8,128)S(1)}, u32[]{:S(2)}, u32[]{:S(2)}) collective-permute-start(f32[3,1,64,128]{3,2,1,0:T(8,128)S(1)} %get-tuple-element.31), channel_id=1, source_target_pairs={{0,64},{64,128},{128,192},{192,256},{256,320},{320,384},{384,448},... | collective-permute-start | bytes 294920 | tf_op jit(solution)/shard_map/ppermute | solution.py:17
  60.8 3.9 %collective-permute-start.8 = (f32[3,1,64,128]{3,2,1,0:T(8,128)S(1)}, f32[3,1,64,128]{3,2,1,0:T(8,128)S(1)}, u32[]{:S(2)}, u32[]{:S(2)}) collective-permute-start(f32[3,1,64,128]{3,2,1,0:T(8,128)S(1)} %get-tuple-element.32), channel_id=1, source_target_pairs={{64,0},{128,64},{192,128},{256,192},{320,256},{384,320},{448,384},... | collective-permute-start | bytes 294920 | tf_op jit(solution)/shard_map/ppermute | solution.py:18
  64.7 0.7 collective-permute-done.9
  65.3 3.1 %collective-permute-done.8 = f32[3,1,64,128]{3,2,1,0:T(8,128)S(1)} collective-permute-done((f32[3,1,64,128]{3,2,1,0:T(8,128)S(1)}, f32[3,1,64,128]{3,2,1,0:T(8,128)S(1)}, u32[]{:S(2)}, u32[]{:S(2)}) %collective-permute-start.8) | collective-permute-done | bytes 98336 | tf_op jit(solution)/shard_map/ppermute | solution.py:18
  68.5 1.9 %collective-permute-start.11 = (f32[3,10,1,128]{3,2,1,0:T(1,128)S(1)}, f32[3,10,1,128]{3,2,1,0:T(1,128)S(1)}, u32[]{:S(2)}, u32[]{:S(2)}) collective-permute-start(f32[3,10,1,128]{3,2,1,0:T(1,128)S(1)} %get-tuple-element.25), channel_id=1, source_target_pairs={{0,1},{1,2},{2,3},{3,4},{4,5},{5,6},{6,7},{7,8},{8,9},{9,10},{10,1... | collective-permute-start | bytes 46088 | tf_op jit(solution)/shard_map/ppermute | solution.py:17
  70.4 5.8 %collective-permute-start.10 = (f32[3,10,1,128]{3,2,1,0:T(1,128)S(1)}, f32[3,10,1,128]{3,2,1,0:T(1,128)S(1)}, u32[]{:S(2)}, u32[]{:S(2)}) collective-permute-start(f32[3,10,1,128]{3,2,1,0:T(1,128)S(1)} %get-tuple-element.26), channel_id=1, source_target_pairs={{1,0},{2,1},{3,2},{4,3},{5,4},{6,5},{7,6},{8,7},{9,8},{10,9},{11,1... | collective-permute-start | bytes 46088 | tf_op jit(solution)/shard_map/ppermute | solution.py:18
  76.2 0.0 collective-permute-done.11
  76.2 1.4 %collective-permute-done.10 = f32[3,10,1,128]{3,2,1,0:T(1,128)S(1)} collective-permute-done((f32[3,10,1,128]{3,2,1,0:T(1,128)S(1)}, f32[3,10,1,128]{3,2,1,0:T(1,128)S(1)}, u32[]{:S(2)}, u32[]{:S(2)}) %collective-permute-start.10) | collective-permute-done | bytes 15392 | tf_op jit(solution)/shard_map/ppermute | solution.py:18
  77.6 0.8 select_maximum_fusion
  78.4 0.2 pad_maximum_fusion.2
  78.6 0.0 copy-done.1
  78.6 2.2 %fusion.4 = f32[3,8,64,128]{3,2,1,0:T(8,128)S(1)} fusion(f32[3,8,64,128]{3,2,1,0:T(8,128)S(1)} %copy-done.3, f32[3,10,66,130]{3,2,1,0:T(8,128)S(1)} %select_maximum_fusion, f32[3,10,65,128]{3,2,1,0:T(8,128)S(1)} %get-tuple-element.24, f32[3,10,65,128]{3,2,1,0:T(8,128)S(1)} %get-tuple-element.23, f32[3,8,64,128]{3,2,1,0:T(8,128)S(1)} %fusion.24, ...), kind=kLoop, calls=%fused_computation.35 | loop fusion | flops 6488064 | bytes 15925248 | tf_op jit(solution)/shard_map/div | solution.py:83
  80.8 2.7 %collective-permute-start.12 = (f32[3,1,64,128]{3,2,1,0:T(8,128)S(1)}, f32[3,1,64,128]{3,2,1,0:T(8,128)S(1)}, u32[]{:S(2)}, u32[]{:S(2)}) collective-permute-start(f32[3,1,64,128]{3,2,1,0:T(8,128)S(1)} %slice.534), channel_id=1, source_target_pairs={{64,0},{128,64},{192,128},{256,192},{320,256},{384,320},{448,384},... | collective-permute-start | bytes 294920 | tf_op jit(solution)/shard_map/ppermute | solution.py:26
  83.5 5.0 %collective-permute-done.12 = f32[3,1,64,128]{3,2,1,0:T(8,128)S(1)} collective-permute-done((f32[3,1,64,128]{3,2,1,0:T(8,128)S(1)}, f32[3,1,64,128]{3,2,1,0:T(8,128)S(1)}, u32[]{:S(2)}, u32[]{:S(2)}) %collective-permute-start.12) | collective-permute-done | bytes 98336 | tf_op jit(solution)/shard_map/ppermute | solution.py:26
  88.5 0.1 pad_maximum_fusion.3
  88.6 0.1 multiply_add_fusion
  88.7 4.6 %collective-permute-start.13 = (f32[3,4,1,128]{3,2,1,0:T(1,128)S(1)}, f32[3,4,1,128]{3,2,1,0:T(1,128)S(1)}, u32[]{:S(2)}, u32[]{:S(2)}) collective-permute-start(f32[3,4,1,128]{3,2,1,0:T(1,128)S(1)} %slice.535), channel_id=1, source_target_pairs={{1,0},{2,1},{3,2},{4,3},{5,4},{6,5},{7,6},{8,7},{9,8},{10,9},{11,1... | collective-permute-start | bytes 18440 | tf_op jit(solution)/shard_map/ppermute | solution.py:26
  93.3 0.1 slice.481
  93.4 0.1 slice.480
  93.5 1.1 %collective-permute-done.13 = f32[3,4,1,128]{3,2,1,0:T(1,128)S(1)} collective-permute-done((f32[3,4,1,128]{3,2,1,0:T(1,128)S(1)}, f32[3,4,1,128]{3,2,1,0:T(1,128)S(1)}, u32[]{:S(2)}, u32[]{:S(2)}) %collective-permute-start.13) | collective-permute-done | bytes 6176 | tf_op jit(solution)/shard_map/ppermute | solution.py:26
  94.7 0.1 slice.483
  94.9 3.5 %slice.485 = f32[3,4,32,64]{3,2,1,0:T(8,128)S(1)} slice(f32[3,4,32,128]{3,2,1,0:T(8,128)S(1)} %multiply_add_fusion.2), slice={[0:3:1], [0:4:1], [0:32:1], [1:128:2]} | slice | bytes 196608 | tf_op jit(solution)/shard_map/slice | solution.py:62
  98.4 3.5 %slice.484 = f32[3,4,32,64]{3,2,1,0:T(8,128)S(1)} slice(f32[3,4,32,128]{3,2,1,0:T(8,128)S(1)} %multiply_add_fusion.2), slice={[0:3:1], [0:4:1], [0:32:1], [0:128:2]} | slice | bytes 196608 | tf_op jit(solution)/shard_map/slice | solution.py:61
  101.9 3.5 %slice.486 = f32[3,4,32,64]{3,2,1,0:T(8,128)S(1)} slice(f32[3,4,32,129]{3,2,1,0:T(8,128)S(1)} %concatenate.93), slice={[0:3:1], [0:4:1], [0:32:1], [2:129:2]} | slice | bytes 196608 | tf_op jit(solution)/shard_map/slice | solution.py:63
  105.5 0.7 multiply_add_fusion.1
  (10 shorter events, 0.2 us)
Async XLA Ops:
  0.6 31.2 %copy-start = (f32[3,8,64,128]{3,2,1,0:T(8,128)S(1)}, f32[3,8,64,128]{3,2,1,0:T(8,128)}, u32[]{:S(2)}) copy-start(f32[3,8,64,128]{3,2,1,0:T(8,128)} %param.4) | copy-start | bytes 2359300
  0.6 31.2 %copy-start.2 = (f32[8,64,128]{2,1,0:T(8,128)S(1)}, f32[8,64,128]{2,1,0:T(8,128)}, u32[]{:S(2)}) copy-start(f32[8,64,128]{2,1,0:T(8,128)} %param.6) | copy-start | bytes 786436
  0.7 26.1 %copy-start.4 = (f32[7]{0:T(128)S(1)}, f32[7]{0:T(128)}, u32[]{:S(2)}) copy-start(f32[7]{0:T(128)} %param.7) | copy-start | bytes 88
  1.8 7.4 %collective-permute-start = (f32[4,1,64,128]{3,2,1,0:T(8,128)S(1)}, f32[4,1,64,128]{3,2,1,0:T(8,128)S(1)}, u32[]{:S(2)}, u32[]{:S(2)}) collective-permute-start(f32[4,1,64,128]{3,2,1,0:T(8,128)S(1)} %get-tuple-element.21), channel_id=1, source_target_pairs={{0,64},{64,128},{128,192},{192,256},{256,320},{320,384},{384,448},... | collective-permute-start | bytes 393224 | tf_op jit(solution)/shard_map/ppermute | solution.py:17
  6.5 8.1 %collective-permute-start.1 = (f32[4,1,64,128]{3,2,1,0:T(8,128)S(1)}, f32[4,1,64,128]{3,2,1,0:T(8,128)S(1)}, u32[]{:S(2)}, u32[]{:S(2)}) collective-permute-start(f32[4,1,64,128]{3,2,1,0:T(8,128)S(1)} %get-tuple-element.22), channel_id=1, source_target_pairs={{64,0},{128,64},{192,128},{256,192},{320,256},{384,320},{448,384},... | collective-permute-start | bytes 393224 | tf_op jit(solution)/shard_map/ppermute | solution.py:18
  15.5 16.3 %collective-permute-start.2 = (f32[4,10,1,128]{3,2,1,0:T(1,128)S(1)}, f32[4,10,1,128]{3,2,1,0:T(1,128)S(1)}, u32[]{:S(2)}, u32[]{:S(2)}) collective-permute-start(f32[4,10,1,128]{3,2,1,0:T(1,128)S(1)} %get-tuple-element.19), channel_id=1, source_target_pairs={{0,1},{1,2},{2,3},{3,4},{4,5},{5,6},{6,7},{7,8},{8,9},{9,10},{10,1... | collective-permute-start | bytes 61448 | tf_op jit(solution)/shard_map/ppermute | solution.py:17
  17.5 14.4 %collective-permute-start.3 = (f32[4,10,1,128]{3,2,1,0:T(1,128)S(1)}, f32[4,10,1,128]{3,2,1,0:T(1,128)S(1)}, u32[]{:S(2)}, u32[]{:S(2)}) collective-permute-start(f32[4,10,1,128]{3,2,1,0:T(1,128)S(1)} %get-tuple-element.20), channel_id=1, source_target_pairs={{1,0},{2,1},{3,2},{4,3},{5,4},{6,5},{7,6},{8,7},{9,8},{10,9},{11,1... | collective-permute-start | bytes 61448 | tf_op jit(solution)/shard_map/ppermute | solution.py:18
  33.4 1.1 %copy-start.3 = (f32[3,8,64,128]{3,2,1,0:T(8,128)S(1)}, f32[3,8,64,128]{3,2,1,0:T(8,128)}, u32[]{:S(2)}) copy-start(f32[3,8,64,128]{3,2,1,0:T(8,128)} %param.5) | copy-start | bytes 2359300
  36.8 6.5 %collective-permute-start.5 = (f32[3,1,64,128]{3,2,1,0:T(8,128)S(1)}, f32[3,1,64,128]{3,2,1,0:T(8,128)S(1)}, u32[]{:S(2)}, u32[]{:S(2)}) collective-permute-start(f32[3,1,64,128]{3,2,1,0:T(8,128)S(1)} %get-tuple-element.33), channel_id=1, source_target_pairs={{0,64},{64,128},{128,192},{192,256},{256,320},{320,384},{384,448},... | collective-permute-start | bytes 294920 | tf_op jit(solution)/shard_map/ppermute | solution.py:17
  38.7 7.7 %collective-permute-start.4 = (f32[3,1,64,128]{3,2,1,0:T(8,128)S(1)}, f32[3,1,64,128]{3,2,1,0:T(8,128)S(1)}, u32[]{:S(2)}, u32[]{:S(2)}) collective-permute-start(f32[3,1,64,128]{3,2,1,0:T(8,128)S(1)} %get-tuple-element.34), channel_id=1, source_target_pairs={{64,0},{128,64},{192,128},{256,192},{320,256},{384,320},{448,384},... | collective-permute-start | bytes 294920 | tf_op jit(solution)/shard_map/ppermute | solution.py:18
  46.4 7.7 %collective-permute-start.7 = (f32[3,10,1,128]{3,2,1,0:T(1,128)S(1)}, f32[3,10,1,128]{3,2,1,0:T(1,128)S(1)}, u32[]{:S(2)}, u32[]{:S(2)}) collective-permute-start(f32[3,10,1,128]{3,2,1,0:T(1,128)S(1)} %get-tuple-element.29), channel_id=1, source_target_pairs={{0,1},{1,2},{2,3},{3,4},{4,5},{5,6},{6,7},{7,8},{8,9},{9,10},{10,1... | collective-permute-start | bytes 46088 | tf_op jit(solution)/shard_map/ppermute | solution.py:17
  48.4 7.2 %collective-permute-start.6 = (f32[3,10,1,128]{3,2,1,0:T(1,128)S(1)}, f32[3,10,1,128]{3,2,1,0:T(1,128)S(1)}, u32[]{:S(2)}, u32[]{:S(2)}) collective-permute-start(f32[3,10,1,128]{3,2,1,0:T(1,128)S(1)} %get-tuple-element.30), channel_id=1, source_target_pairs={{1,0},{2,1},{3,2},{4,3},{5,4},{6,5},{7,6},{8,7},{9,8},{10,9},{11,1... | collective-permute-start | bytes 46088 | tf_op jit(solution)/shard_map/ppermute | solution.py:18
  58.8 19.8 %copy-start.1 = (f32[3,8,64,128]{3,2,1,0:T(8,128)}, f32[3,8,64,128]{3,2,1,0:T(8,128)S(1)}, u32[]{:S(2)}) copy-start(f32[3,8,64,128]{3,2,1,0:T(8,128)S(1)} %fusion.24) | copy-start | bytes 2359300
  58.8 6.5 %collective-permute-start.9 = (f32[3,1,64,128]{3,2,1,0:T(8,128)S(1)}, f32[3,1,64,128]{3,2,1,0:T(8,128)S(1)}, u32[]{:S(2)}, u32[]{:S(2)}) collective-permute-start(f32[3,1,64,128]{3,2,1,0:T(8,128)S(1)} %get-tuple-element.31), channel_id=1, source_target_pairs={{0,64},{64,128},{128,192},{192,256},{256,320},{320,384},{384,448},... | collective-permute-start | bytes 294920 | tf_op jit(solution)/shard_map/ppermute | solution.py:17
  60.8 7.7 %collective-permute-start.8 = (f32[3,1,64,128]{3,2,1,0:T(8,128)S(1)}, f32[3,1,64,128]{3,2,1,0:T(8,128)S(1)}, u32[]{:S(2)}, u32[]{:S(2)}) collective-permute-start(f32[3,1,64,128]{3,2,1,0:T(8,128)S(1)} %get-tuple-element.32), channel_id=1, source_target_pairs={{64,0},{128,64},{192,128},{256,192},{320,256},{384,320},{448,384},... | collective-permute-start | bytes 294920 | tf_op jit(solution)/shard_map/ppermute | solution.py:18
  68.5 7.7 %collective-permute-start.11 = (f32[3,10,1,128]{3,2,1,0:T(1,128)S(1)}, f32[3,10,1,128]{3,2,1,0:T(1,128)S(1)}, u32[]{:S(2)}, u32[]{:S(2)}) collective-permute-start(f32[3,10,1,128]{3,2,1,0:T(1,128)S(1)} %get-tuple-element.25), channel_id=1, source_target_pairs={{0,1},{1,2},{2,3},{3,4},{4,5},{5,6},{6,7},{7,8},{8,9},{9,10},{10,1... | collective-permute-start | bytes 46088 | tf_op jit(solution)/shard_map/ppermute | solution.py:17
  70.4 7.2 %collective-permute-start.10 = (f32[3,10,1,128]{3,2,1,0:T(1,128)S(1)}, f32[3,10,1,128]{3,2,1,0:T(1,128)S(1)}, u32[]{:S(2)}, u32[]{:S(2)}) collective-permute-start(f32[3,10,1,128]{3,2,1,0:T(1,128)S(1)} %get-tuple-element.26), channel_id=1, source_target_pairs={{1,0},{2,1},{3,2},{4,3},{5,4},{6,5},{7,6},{8,7},{9,8},{10,9},{11,1... | collective-permute-start | bytes 46088 | tf_op jit(solution)/shard_map/ppermute | solution.py:18
  80.8 7.7 %collective-permute-start.12 = (f32[3,1,64,128]{3,2,1,0:T(8,128)S(1)}, f32[3,1,64,128]{3,2,1,0:T(8,128)S(1)}, u32[]{:S(2)}, u32[]{:S(2)}) collective-permute-start(f32[3,1,64,128]{3,2,1,0:T(8,128)S(1)} %slice.534), channel_id=1, source_target_pairs={{64,0},{128,64},{192,128},{256,192},{320,256},{384,320},{448,384},... | collective-permute-start | bytes 294920 | tf_op jit(solution)/shard_map/ppermute | solution.py:26
  88.7 5.9 %collective-permute-start.13 = (f32[3,4,1,128]{3,2,1,0:T(1,128)S(1)}, f32[3,4,1,128]{3,2,1,0:T(1,128)S(1)}, u32[]{:S(2)}, u32[]{:S(2)}) collective-permute-start(f32[3,4,1,128]{3,2,1,0:T(1,128)S(1)} %slice.535), channel_id=1, source_target_pairs={{1,0},{2,1},{3,2},{4,3},{5,4},{6,5},{7,6},{8,7},{9,8},{10,9},{11,1... | collective-permute-start | bytes 18440 | tf_op jit(solution)/shard_map/ppermute | solution.py:26
where the time goes:
time: 107 us; the launch traced here: 106 us
  starting transfers between devices  52.1 us (49%)
  waiting for transfers between devices  22.6 us (21%)
  other arithmetic  13.5 us (13%)
  local copies, waits for them, and re-layouts  12.5 us (12%)
  between operations  5.49 us (5%)
    ppermute x6, starting transfers between devices, padded_2(): after = lax.ppermute(initial, axis, down)  30.5 us
    ppermute x6, waiting for transfers between devices, padded_2(): after = lax.ppermute(initial, axis, down)  14.4 us
    ppermute x6, starting transfers between devices, padded_2(): before = lax.ppermute(last, axis, up)  14.3 us
    ppermute x2, starting transfers between devices, from_behind(): lax.ppermute(value, axis, [(source, source + steps) for source in range(i...  7.3 us
    ppermute x2, waiting for transfers between devices, from_behind(): lax.ppermute(value, axis, [(source, source + steps) for source in range(i...  6.09 us
    add x2, other arithmetic, per_device(): current = current + OMEGA * (right_side - image) / diag  4.51 us
    slice x2, local copies, waits for them, and re-layouts, halve(): last = lax.slice_in_dim(joined, 2, count + 1, 2, axis)  3.65 us
    slice x2, local copies, waits for them, and re-layouts, halve(): middle = lax.slice_in_dim(joined, 1, count, 2, axis)  3.64 us
  transfers between devices with their start and end apart: 14, of which 10 were waited for; matrix products, arithmetic and copies ran while one was open for 1% of the time, Pallas kernels for 0%

commit v1 on v0

v1 whole, which is shorter than its diff:
```python
import jax
import jax.numpy as jnp
from jax import lax
from jax.experimental import pallas as pl
from jax.experimental.pallas import tpu as pltpu
from jax.sharding import PartitionSpec as P

OMEGA = 0.6
COMP = 3
BELOW = 3
ABOVE = 4
TILE = 8


def pack_kernel(u, rhs, visc, to_below, to_above, to_left, to_right, sems):
    rows, cols = visc.shape[0], visc.shape[1]
    copies = []

    def copy(src, dst):
        copies.append(pltpu.make_async_copy(src, dst, sems.at[len(copies)]))
        copies[-1].start()

    def rows_of(buffer, count, first_n, first_r, count_r):
        at = 0
        for c in range(COMP):
            copy(u.at[c, pl.ds(first_n, count)], buffer.at[pl.ds(at, count)])
            at += count
        copy(visc.at[pl.ds(first_n, count)], buffer.at[pl.ds(at, count)])
        at += count
        for c in range(COMP):
            copy(rhs.at[c, pl.ds(first_r, count_r)], buffer.at[pl.ds(at, count_r)])
            at += count_r

    rows_of(to_below, ABOVE, 0, 0, ABOVE - 1)
    rows_of(to_above, BELOW, rows - BELOW, rows - BELOW + 1, BELOW - 1)
    for buffer, first in ((to_left, 0), (to_right, cols - TILE)):
        copy(u.at[:, :, pl.ds(first, TILE)], buffer.at[pl.ds(0, COMP)])
        copy(rhs.at[:, :, pl.ds(first, TILE)], buffer.at[pl.ds(COMP, COMP)])
        copy(visc.at[:, pl.ds(first, TILE)], buffer.at[2 * COMP])
    for each in copies:
        each.wait()


def pack(u, rhs, visc):
    rows, cols, lanes = visc.shape
    f32 = jnp.float32
    shapes = (
        ((4 * ABOVE + 3 * (ABOVE - 1)), cols, lanes),
        ((4 * BELOW + 3 * (BELOW - 1)), cols, lanes),
        (2 * COMP + 1, rows, TILE, lanes),
        (2 * COMP + 1, rows, TILE, lanes),
    )
    return pl.pallas_call(
        pack_kernel,
        out_shape=[jax.ShapeDtypeStruct(s, f32) for s in shapes],
        in_specs=[pl.BlockSpec(memory_space=pl.ANY)] * 3,
        out_specs=[pl.BlockSpec(memory_space=pltpu.VMEM)] * 4,
        scratch_shapes=[pltpu.SemaphoreType.DMA((20,))],
        compiler_params=pltpu.CompilerParams(vmem_limit_bytes=8 << 20),
        cost_estimate=pl.CostEstimate(flops=0, bytes_accessed=4 << 20, transcendentals=0),
        name="pack",
    )(u, rhs, visc)


def corner_kernel(left, right, to_below, to_above):
    rows = left.shape[1]
    late = lax.broadcasted_iota(jnp.int32, left.shape[2:], 0) >= TILE - BELOW

    def rows_of(buffer, count, first_n, first_r, count_r):
        at = 0
        picks = [(c, first_n + i) for c in range(COMP) for i in range(count)]
        picks += [(2 * COMP, first_n + i) for i in range(count)]
        picks += [(COMP + c, first_r + i) for c in range(COMP) for i in range(count_r)]
        for field, row in picks:
            buffer[at] = jnp.where(late, left[field, row], right[field, row])
            at += 1

    rows_of(to_below, ABOVE, 0, 0, ABOVE - 1)
    rows_of(to_above, BELOW, rows - BELOW, rows - BELOW + 1, BELOW - 1)


def corners(left, right):
    lanes = left.shape[-1]
    shapes = (
        ((4 * ABOVE + 3 * (ABOVE - 1)), TILE, lanes),
        ((4 * BELOW + 3 * (BELOW - 1)), TILE, lanes),
    )
    return pl.pallas_call(
        corner_kernel,
        out_shape=[jax.ShapeDtypeStruct(s, jnp.float32) for s in shapes],
        in_specs=[pl.BlockSpec(memory_space=pltpu.VMEM)] * 2,
        out_specs=[pl.BlockSpec(memory_space=pltpu.VMEM)] * 2,
        compiler_params=pltpu.CompilerParams(vmem_limit_bytes=8 << 20),
        cost_estimate=pl.CostEstimate(flops=0, bytes_accessed=1 << 20, transcendentals=0),
        name="corners",
    )(left, right)


def smooth_kernel(
    wts, u, rhs, visc, left, right, above, below, above_c, below_c,
    smoothed, coarse,
    u0, u1, u2, force, n, coef, inv, carry, moved, restr,
):
    rows, cols, lanes = visc.shape
    wide = cols + TILE
    sub = lax.broadcasted_iota(jnp.int32, (TILE, lanes), 0)
    late = sub >= TILE - BELOW
    own = slice(BELOW, BELOW + rows)
    main, side = slice(0, cols), slice(cols, wide)

    for c in range(COMP):
        u0[c, own, main] = u[c]
        force[c, own, main] = rhs[c]
        u0[c, own, side] = jnp.where(late, left[c], right[c])
        force[c, own, side] = jnp.where(late, left[COMP + c], right[COMP + c])
        a, b = ABOVE * c, BELOW * c
        u0[c, BELOW + rows :, main] = above[a : a + ABOVE]
        u0[c, BELOW + rows :, side] = above_c[a : a + ABOVE]
        u0[c, 0:BELOW, main] = below[b : b + BELOW]
        u0[c, 0:BELOW, side] = below_c[b : b + BELOW]
        a, b = 4 * ABOVE + (ABOVE - 1) * c, 4 * BELOW + (BELOW - 1) * c
        force[c, BELOW + rows : BELOW + rows + ABOVE - 1, main] = above[a : a + ABOVE - 1]
        force[c, BELOW + rows : BELOW + rows + ABOVE - 1, side] = above_c[a : a + ABOVE - 1]
        force[c, 1:BELOW, main] = below[b : b + BELOW - 1]
        force[c, 1:BELOW, side] = below_c[b : b + BELOW - 1]
    n[own, main] = visc[...]
    n[own, side] = jnp.where(late, left[2 * COMP], right[2 * COMP])
    n[BELOW + rows :, main] = above[3 * ABOVE : 4 * ABOVE]
    n[BELOW + rows :, side] = above_c[3 * ABOVE : 4 * ABOVE]
    n[0:BELOW, main] = below[3 * BELOW : 4 * BELOW]
    n[0:BELOW, side] = below_c[3 * BELOW : 4 * BELOW]

    def sl(x):
        return pltpu.roll(x, wide - 1, 0)

    def sl_back(x):
        return pltpu.roll(x, 1, 0)

    def sc(x):
        return pltpu.roll(x, lanes - 1, 1)

    def sc_back(x):
        return pltpu.roll(x, 1, 1)

    lane = lax.broadcasted_iota(jnp.int32, (1, lanes), 1)
    half = [0.5 * wts[k] for k in range(7)]
    w = [
        jnp.where(lane < lanes - 1, half[k], 0.0) if k in (2, 4, 5, 6) else half[k]
        for k in range(7)
    ]
    lost = half[2] + half[4] + half[5] + half[6]
    rim = jnp.where((lane == 0) | (lane == lanes - 1), lost, 0.0)

    def edges(at, move):
        low, high = n[at], n[at + 1]
        low_l, high_l = sl(low), sl(high)
        coef[0, at] = w[0] * (low + high)
        coef[1, at] = w[1] * (low + low_l)
        coef[2, at] = w[2] * (low + sc(low))
        coef[3, at] = w[3] * (low + high_l)
        coef[4, at] = w[4] * (low + sc(high))
        coef[5, at] = w[5] * (low + sc(low_l))
        coef[6, at] = w[6] * (low + sc(high_l))

    last = BELOW + rows + ABOVE - 1

    def edges_step(at, _):
        edges(at, None)
        return 0

    lax.fori_loop(0, last, edges_step, 0)

    def diag_step(at, _):
        e = [coef[k, at] for k in range(7)]
        p = {k: coef[k, at - 1] for k in (0, 3, 4, 6)}
        low = n[at]
        total = e[0] + e[1] + e[2] + e[3] + e[4] + e[5] + e[6] + p[0] + rim * low
        total = total + sc_back(e[2] + p[4]) + sl_back(e[1] + p[3] + sc_back(e[5] + p[6]))
        inv[at] = jnp.where(low > 0.0, 1.0 / total, 0.0)
        return 0

    lax.fori_loop(1, last, diag_step, 0)

    def sweep(field, first, end, put):
        def upward(c, at, v):
            high = field[c, at + 1]
            high_l = sl(high)
            high_s = sc(high)
            high_ls = sc(high_l)
            moved[c, 0], moved[c, 1], moved[c, 2] = high_l, high_s, high_ls
            return (
                coef[0, at] * (high - v),
                coef[3, at] * (high_l - v),
                coef[4, at] * (high_s - v),
                coef[6, at] * (high_ls - v),
            )

        for c in range(COMP):
            fluxes = upward(c, first - 1, field[c, first - 1])
            for k in range(4):
                carry[c, k] = fluxes[k]

        def step(at, _):
            low_n = n[at] * rim
            invd = inv[at]
            for c in range(COMP):
                v = field[c, at]
                f1 = coef[1, at] * (moved[c, 0] - v)
                f2 = coef[2, at] * (moved[c, 1] - v)
                f5 = coef[5, at] * (moved[c, 2] - v)
                f0, f3, f4, f6 = upward(c, at, v)
                inward = sc_back(f2 + carry[c, 2])
                inward = inward + sl_back(f1 + carry[c, 1] + sc_back(f5 + carry[c, 3]))
                inward = inward + carry[c, 0]
                total = ((f0 + f1) + (f2 + f3)) + ((f4 + f5) + f6)
                carry[c, 0], carry[c, 1], carry[c, 2], carry[c, 3] = f0, f3, f4, f6
                total = (total - inward) + (force[c, at] - low_n * v)
                put(c, at, v, total * invd)
            return 0

        lax.fori_loop(first, end, step, 0)

    def put1(c, at, v, change):
        u1[c, at] = v + OMEGA * change

    def put2(c, at, v, change):
        u2[c, at] = v + OMEGA * change

    def put3(c, at, v, change):
        u0[c, at] = change

    sweep(u0, 1, last, put1)
    sweep(u1, 2, last - 1, put2)
    smoothed[...] = u2[:, own, main]
    sweep(u2, 3, last - 2, put3)

    for c in range(COMP):
        for i in range(rows // 2):
            at = BELOW + 2 * i
            restr[c * (rows // 2) + i] = 0.25 * (u0[c, at] + u0[c, at + 2]) + 0.5 * u0[c, at + 1]
    parts = []
    for i in range(COMP * (rows // 2)):
        a = restr[i, pl.ds(0, cols // 2, stride=2)]
        b = restr[i, pl.ds(1, cols // 2, stride=2)]
        d = restr[i, pl.ds(2, cols // 2, stride=2)]
        parts.append(0.25 * (a + d) + 0.5 * b)
    source = lax.broadcasted_iota(jnp.int32, (lanes, lanes // 2), 0)
    target = 2 * lax.broadcasted_iota(jnp.int32, (lanes, lanes // 2), 1)
    gap = source - target
    h = jnp.where(gap == 1, 0.5, jnp.where((gap == 0) | (gap == 2), 0.25, 0.0))
    for c in range(COMP):
        block = jnp.concatenate(parts[c * (rows // 2) : (c + 1) * (rows // 2)], 0)
        out = jnp.dot(block, h, precision=lax.Precision.HIGHEST, preferred_element_type=jnp.float32)
        coarse[c] = out.reshape(rows // 2, cols // 2, lanes // 2)


def smooth(wts, u, rhs, visc, left, right, above, below, above_c, below_c):
    rows, cols, lanes = visc.shape
    deep, wide = rows + BELOW + ABOVE, cols + TILE
    f32 = jnp.float32
    vmem = pl.BlockSpec(memory_space=pltpu.VMEM)
    return pl.pallas_call(
        smooth_kernel,
        out_shape=[
            jax.ShapeDtypeStruct(u.shape, f32),
            jax.ShapeDtypeStruct((COMP, rows // 2, cols // 2, lanes // 2), f32),
        ],
        in_specs=[pl.BlockSpec(memory_space=pltpu.SMEM)] + [vmem] * 9,
        out_specs=[vmem] * 2,
        scratch_shapes=[
            pltpu.VMEM((COMP, deep, wide, lanes), f32),
            pltpu.VMEM((COMP, deep, wide, lanes), f32),
            pltpu.VMEM((COMP, deep, wide, lanes), f32),
            pltpu.VMEM((COMP, deep, wide, lanes), f32),
            pltpu.VMEM((deep, wide, lanes), f32),
            pltpu.VMEM((7, deep, wide, lanes), f32),
            pltpu.VMEM((deep, wide, lanes), f32),
            pltpu.VMEM((COMP, 4, wide, lanes), f32),
            pltpu.VMEM((COMP, 3, wide, lanes), f32),
            pltpu.VMEM((COMP * (rows // 2), wide, lanes), f32),
        ],
        compiler_params=pltpu.CompilerParams(vmem_limit_bytes=32 << 20),
        cost_estimate=pl.CostEstimate(flops=50_000_000, bytes_accessed=4 << 20, transcendentals=0),
        name="smooth",
    )(wts, u, rhs, visc, left, right, above, below, above_c, below_c)


def sent(value, axis, steps):
    count = lax.axis_size(axis)
    pairs = [(i, i + steps) for i in range(count) if 0 <= i + steps < count]
    return lax.ppermute(value, axis, pairs)


def per_device(solution, right_side, viscosity, stencil_weights):
    to_below, to_above, to_left, to_right = pack(solution, right_side, viscosity)
    above = sent(to_below, "shell", -1)
    below = sent(to_above, "shell", 1)
    right = sent(to_left, "lat", -1)
    left = sent(to_right, "lat", 1)
    to_below_c, to_above_c = corners(left, right)
    above_c = sent(to_below_c, "shell", -1)
    below_c = sent(to_above_c, "shell", 1)
    return smooth(
        stencil_weights, solution, right_side, viscosity, left, right, above, below, above_c, below_c
    )


def solution(mesh):
    in_specs = (
        P(None, "shell", "lat", None),
        P(None, "shell", "lat", None),
        P("shell", "lat", None),
        P(),
    )
    out_specs = (P(None, "shell", "lat", None), P(None, "shell", "lat", None))
    return jax.shard_map(
        per_device, mesh=mesh, in_specs=in_specs, out_specs=out_specs, check_vma=False
    )
```

time: 107 us -> 52.4 us (0.49)
  the two profiles are of different devices: /device:TPU:30 before, /device:TPU:38 now
where the time goes in v1:
time: 52.4 us; the launch traced here: 52.1 us
  starting transfers between devices  23.8 us (45%)
  Pallas kernels  15.6 us (30%)
  waiting for transfers between devices  8.7 us (17%)
  local copies, waits for them, and re-layouts  3.23 us (6%)
  between operations  0.75 us (1%)
    ppermute x6, starting transfers between devices, sent(): return lax.ppermute(value, axis, pairs)  23.8 us
    pallas_call x1, Pallas kernels, smooth(): pl.pallas_call(smooth_kernel, out_shape=[jax.ShapeDtypeStruct(u.shape, f3...  13.4 us
    ppermute x6, waiting for transfers between devices, sent(): return lax.ppermute(value, axis, pairs)  8.7 us
    unnamed x14, local copies, waits for them, and re-layouts  3.23 us
    pallas_call x1, Pallas kernels, pack(): pl.pallas_call(pack_kernel, out_shape=[jax.ShapeDtypeStruct(s, f32) for s...  2.08 us
  transfers between devices with their start and end apart: 6, of which 3 were waited for; matrix products, arithmetic and copies ran while one was open for 0% of the time, Pallas kernels for 0%

profile of v1, /device:TPU:38, one launch (start us, length us, event | category | flops | bytes accessed | tf_op | source)
XLA Modules:
  0.0 52.1 jit_solution(16640242840451352670)
XLA Ops:
  0.6 0.0 copy-start
  0.6 1.1 %copy-done = f32[3,8,64,128]{3,2,1,0:T(8,128)S(1)} copy-done((f32[3,8,64,128]{3,2,1,0:T(8,128)S(1)}, f32[3,8,64,128]{3,2,1,0:T(8,128)}, u32[]{:S(2)}) %copy-start) | copy-done | bytes 786456
  1.8 0.0 copy-start.2
  1.8 1.1 %copy-done.2 = f32[3,8,64,128]{3,2,1,0:T(8,128)S(1)} copy-done((f32[3,8,64,128]{3,2,1,0:T(8,128)S(1)}, f32[3,8,64,128]{3,2,1,0:T(8,128)}, u32[]{:S(2)}) %copy-start.2) | copy-done | bytes 786456
  2.9 0.0 copy-start.4
  2.9 0.9 %copy-done.4 = f32[8,64,128]{2,1,0:T(8,128)S(1)} copy-done((f32[8,64,128]{2,1,0:T(8,128)S(1)}, f32[8,64,128]{2,1,0:T(8,128)}, u32[]{:S(2)}) %copy-start.4) | copy-done | bytes 262168
  3.8 0.0 copy-start.1
  3.9 0.0 copy-start.3
  3.9 2.1 %pack.1 = (f32[25,64,128]{2,1,0:T(8,128)S(1)}, f32[18,64,128]{2,1,0:T(8,128)S(1)}, f32[7,8,8,128]{3,2,1,0:T(8,128)S(1)}, f32[7,8,8,128]{3,2,1,0:T(8,128)S(1)}) custom-call(f32[3,8,64,128]{3,2,1,0:T(8,128)S(1)} %copy-done, f32[3,8,64,128]{3,2,1,0:T(8,128)S(1)} %copy-done.2, f32[8,64,128]{2,1,0:T(8,128)S(1)} %copy-done.4), custom_call_target="tpu_custom_call" | custom-call | bytes 4194304 | tf_op jit(solution)/shard_map/pack/pallas_call | solution.py:53
  5.9 0.0 copy-start.5
  6.0 2.5 %collective-permute-start.2 = (f32[25,64,128]{2,1,0:T(8,128)S(1)}, f32[25,64,128]{2,1,0:T(8,128)S(1)}, u32[]{:S(2)}, u32[]{:S(2)}) collective-permute-start(f32[25,64,128]{2,1,0:T(8,128)S(1)} %get-tuple-element.10), channel_id=1, source_target_pairs={{64,0},{128,64},{192,128},{256,192},{320,256},{384,320},{448,384},... | collective-permute-start | bytes 2457608 | tf_op jit(solution)/shard_map/ppermute | solution.py:291
  8.4 3.5 %collective-permute-start.3 = (f32[18,64,128]{2,1,0:T(8,128)S(1)}, f32[18,64,128]{2,1,0:T(8,128)S(1)}, u32[]{:S(2)}, u32[]{:S(2)}) collective-permute-start(f32[18,64,128]{2,1,0:T(8,128)S(1)} %get-tuple-element.11), channel_id=1, source_target_pairs={{0,64},{64,128},{128,192},{192,256},{256,320},{320,384},{384,448},... | collective-permute-start | bytes 1769480 | tf_op jit(solution)/shard_map/ppermute | solution.py:291
  11.9 1.9 %collective-permute-start = (f32[7,8,8,128]{3,2,1,0:T(8,128)S(1)}, f32[7,8,8,128]{3,2,1,0:T(8,128)S(1)}, u32[]{:S(2)}, u32[]{:S(2)}) collective-permute-start(f32[7,8,8,128]{3,2,1,0:T(8,128)S(1)} %get-tuple-element.8), channel_id=1, source_target_pairs={{0,1},{1,2},{2,3},{3,4},{4,5},{5,6},{6,7},{7,8},{8,9},{9,10},{10,1... | collective-permute-start | bytes 688136 | tf_op jit(solution)/shard_map/ppermute | solution.py:291
  13.9 10.1 %collective-permute-start.1 = (f32[7,8,8,128]{3,2,1,0:T(8,128)S(1)}, f32[7,8,8,128]{3,2,1,0:T(8,128)S(1)}, u32[]{:S(2)}, u32[]{:S(2)}) collective-permute-start(f32[7,8,8,128]{3,2,1,0:T(8,128)S(1)} %get-tuple-element.9), channel_id=1, source_target_pairs={{1,0},{2,1},{3,2},{4,3},{5,4},{6,5},{7,6},{8,7},{9,8},{10,9},{11,1... | collective-permute-start | bytes 688136 | tf_op jit(solution)/shard_map/ppermute | solution.py:291
  24.0 1.8 %collective-permute-done.left = f32[7,8,8,128]{3,2,1,0:T(8,128)S(1)} collective-permute-done((f32[7,8,8,128]{3,2,1,0:T(8,128)S(1)}, f32[7,8,8,128]{3,2,1,0:T(8,128)S(1)}, u32[]{:S(2)}, u32[]{:S(2)}) %collective-permute-start) | collective-permute-done | bytes 229408 | tf_op jit(solution)/shard_map/ppermute | solution.py:291
  25.7 1.8 %collective-permute-done.1.right = f32[7,8,8,128]{3,2,1,0:T(8,128)S(1)} collective-permute-done((f32[7,8,8,128]{3,2,1,0:T(8,128)S(1)}, f32[7,8,8,128]{3,2,1,0:T(8,128)S(1)}, u32[]{:S(2)}, u32[]{:S(2)}) %collective-permute-start.1) | collective-permute-done | bytes 229408 | tf_op jit(solution)/shard_map/ppermute | solution.py:291
  27.5 0.0 copy-start.6
  27.5 3.6 %collective-permute-start.4 = (f32[25,8,128]{2,1,0:T(8,128)S(1)}, f32[25,8,128]{2,1,0:T(8,128)S(1)}, u32[]{:S(2)}, u32[]{:S(2)}) collective-permute-start(f32[25,8,128]{2,1,0:T(8,128)S(1)} %get-tuple-element.12), channel_id=1, source_target_pairs={{64,0},{128,64},{192,128},{256,192},{320,256},{384,320},{448,384},... | collective-permute-start | bytes 307208 | tf_op jit(solution)/shard_map/ppermute | solution.py:291
  31.1 2.3 %collective-permute-start.5 = (f32[18,8,128]{2,1,0:T(8,128)S(1)}, f32[18,8,128]{2,1,0:T(8,128)S(1)}, u32[]{:S(2)}, u32[]{:S(2)}) collective-permute-start(f32[18,8,128]{2,1,0:T(8,128)S(1)} %get-tuple-element.13), channel_id=1, source_target_pairs={{0,64},{64,128},{128,192},{192,256},{256,320},{320,384},{384,448},... | collective-permute-start | bytes 221192 | tf_op jit(solution)/shard_map/ppermute | solution.py:291
  33.4 5.2 %collective-permute-done.5.below_c = f32[18,8,128]{2,1,0:T(8,128)S(1)} collective-permute-done((f32[18,8,128]{2,1,0:T(8,128)S(1)}, f32[18,8,128]{2,1,0:T(8,128)S(1)}, u32[]{:S(2)}, u32[]{:S(2)}) %collective-permute-start.5) | collective-permute-done | bytes 73760 | tf_op jit(solution)/shard_map/ppermute | solution.py:291
  38.6 0.0 collective-permute-done.4.above_c
  38.6 0.0 collective-permute-done.3.below
  38.6 0.0 collective-permute-done.2.above
  38.6 0.0 copy-done.1
  38.6 0.0 copy-done.3
  38.6 0.0 copy-done.5
  38.6 0.0 copy-done.6
  38.6 13.4 %smooth.1 = (f32[3,8,64,128]{3,2,1,0:T(8,128)}, f32[3,4,32,64]{3,2,1,0:T(8,128)}) custom-call(f32[7]{0:T(128)S(1)} %copy-done.6, f32[3,8,64,128]{3,2,1,0:T(8,128)S(1)} %copy-done.1, f32[3,8,64,128]{3,2,1,0:T(8,128)S(1)} %copy-done.3, f32[8,64,128]{2,1,0:T(8,128)S(1)} %copy-done.5, f32[7,8,8,128]{3,2,1,0:T(8,128)S(1)} %collective-permute-done.left, ...), custom_call_target="tpu_custom_call" | custom-call | flops 50000000 | bytes 4194304 | tf_op jit(solution)/shard_map/smooth/pallas_call | solution.py:262
  (1 shorter events, 0.0 us)
Async XLA Ops:
  0.6 1.1 %copy-start = (f32[3,8,64,128]{3,2,1,0:T(8,128)S(1)}, f32[3,8,64,128]{3,2,1,0:T(8,128)}, u32[]{:S(2)}) copy-start(f32[3,8,64,128]{3,2,1,0:T(8,128)} %u.3) | copy-start | bytes 2359300
  1.8 1.1 %copy-start.2 = (f32[3,8,64,128]{3,2,1,0:T(8,128)S(1)}, f32[3,8,64,128]{3,2,1,0:T(8,128)}, u32[]{:S(2)}) copy-start(f32[3,8,64,128]{3,2,1,0:T(8,128)} %rhs.3) | copy-start | bytes 2359300
  2.9 0.9 %copy-start.4 = (f32[8,64,128]{2,1,0:T(8,128)S(1)}, f32[8,64,128]{2,1,0:T(8,128)}, u32[]{:S(2)}) copy-start(f32[8,64,128]{2,1,0:T(8,128)} %visc.3) | copy-start | bytes 786436
  3.8 34.7 %copy-start.1 = (f32[3,8,64,128]{3,2,1,0:T(8,128)S(1)}, f32[3,8,64,128]{3,2,1,0:T(8,128)}, u32[]{:S(2)}) copy-start(f32[3,8,64,128]{3,2,1,0:T(8,128)} %u.3) | copy-start | bytes 2359300
  3.9 34.7 %copy-start.3 = (f32[3,8,64,128]{3,2,1,0:T(8,128)S(1)}, f32[3,8,64,128]{3,2,1,0:T(8,128)}, u32[]{:S(2)}) copy-start(f32[3,8,64,128]{3,2,1,0:T(8,128)} %rhs.3) | copy-start | bytes 2359300
  5.9 32.7 %copy-start.5 = (f32[8,64,128]{2,1,0:T(8,128)S(1)}, f32[8,64,128]{2,1,0:T(8,128)}, u32[]{:S(2)}) copy-start(f32[8,64,128]{2,1,0:T(8,128)} %visc.3) | copy-start | bytes 786436
  6.0 32.6 %collective-permute-start.2 = (f32[25,64,128]{2,1,0:T(8,128)S(1)}, f32[25,64,128]{2,1,0:T(8,128)S(1)}, u32[]{:S(2)}, u32[]{:S(2)}) collective-permute-start(f32[25,64,128]{2,1,0:T(8,128)S(1)} %get-tuple-element.10), channel_id=1, source_target_pairs={{64,0},{128,64},{192,128},{256,192},{320,256},{384,320},{448,384},... | collective-permute-start | bytes 2457608 | tf_op jit(solution)/shard_map/ppermute | solution.py:291
  8.4 30.1 %collective-permute-start.3 = (f32[18,64,128]{2,1,0:T(8,128)S(1)}, f32[18,64,128]{2,1,0:T(8,128)S(1)}, u32[]{:S(2)}, u32[]{:S(2)}) collective-permute-start(f32[18,64,128]{2,1,0:T(8,128)S(1)} %get-tuple-element.11), channel_id=1, source_target_pairs={{0,64},{64,128},{128,192},{192,256},{256,320},{320,384},{384,448},... | collective-permute-start | bytes 1769480 | tf_op jit(solution)/shard_map/ppermute | solution.py:291
  11.9 13.8 %collective-permute-start = (f32[7,8,8,128]{3,2,1,0:T(8,128)S(1)}, f32[7,8,8,128]{3,2,1,0:T(8,128)S(1)}, u32[]{:S(2)}, u32[]{:S(2)}) collective-permute-start(f32[7,8,8,128]{3,2,1,0:T(8,128)S(1)} %get-tuple-element.8), channel_id=1, source_target_pairs={{0,1},{1,2},{2,3},{3,4},{4,5},{5,6},{6,7},{7,8},{8,9},{9,10},{10,1... | collective-permute-start | bytes 688136 | tf_op jit(solution)/shard_map/ppermute | solution.py:291
  13.9 13.6 %collective-permute-start.1 = (f32[7,8,8,128]{3,2,1,0:T(8,128)S(1)}, f32[7,8,8,128]{3,2,1,0:T(8,128)S(1)}, u32[]{:S(2)}, u32[]{:S(2)}) collective-permute-start(f32[7,8,8,128]{3,2,1,0:T(8,128)S(1)} %get-tuple-element.9), channel_id=1, source_target_pairs={{1,0},{2,1},{3,2},{4,3},{5,4},{6,5},{7,6},{8,7},{9,8},{10,9},{11,1... | collective-permute-start | bytes 688136 | tf_op jit(solution)/shard_map/ppermute | solution.py:291
  27.5 11.1 %copy-start.6 = (f32[7]{0:T(128)S(1)}, f32[7]{0:T(128)}, u32[]{:S(2)}) copy-start(f32[7]{0:T(128)} %wts.1) | copy-start | bytes 88
  27.5 11.0 %collective-permute-start.4 = (f32[25,8,128]{2,1,0:T(8,128)S(1)}, f32[25,8,128]{2,1,0:T(8,128)S(1)}, u32[]{:S(2)}, u32[]{:S(2)}) collective-permute-start(f32[25,8,128]{2,1,0:T(8,128)S(1)} %get-tuple-element.12), channel_id=1, source_target_pairs={{64,0},{128,64},{192,128},{256,192},{320,256},{384,320},{448,384},... | collective-permute-start | bytes 307208 | tf_op jit(solution)/shard_map/ppermute | solution.py:291
  31.1 7.5 %collective-permute-start.5 = (f32[18,8,128]{2,1,0:T(8,128)S(1)}, f32[18,8,128]{2,1,0:T(8,128)S(1)}, u32[]{:S(2)}, u32[]{:S(2)}) collective-permute-start(f32[18,8,128]{2,1,0:T(8,128)S(1)} %get-tuple-element.13), channel_id=1, source_target_pairs={{0,64},{64,128},{128,192},{192,256},{256,320},{320,384},{384,448},... | collective-permute-start | bytes 221192 | tf_op jit(solution)/shard_map/ppermute | solution.py:291

commit v2 on v1

v2 whole, which is shorter than its diff:
```python
import jax
import jax.numpy as jnp
from jax import lax
from jax.experimental import pallas as pl
from jax.experimental.pallas import tpu as pltpu
from jax.sharding import PartitionSpec as P

OMEGA = 0.6
COMP = 3
BELOW = 3
ABOVE = 4
TILE = 8


def pack_kernel(u, rhs, visc, to_below, to_above, to_left, to_right, sems):
    rows, cols = visc.shape[0], visc.shape[1]
    copies = []

    def copy(src, dst):
        copies.append(pltpu.make_async_copy(src, dst, sems.at[len(copies)]))
        copies[-1].start()

    def rows_of(buffer, count, first_n, first_r, count_r):
        at = 0
        for c in range(COMP):
            copy(u.at[c, pl.ds(first_n, count)], buffer.at[pl.ds(at, count)])
            at += count
        copy(visc.at[pl.ds(first_n, count)], buffer.at[pl.ds(at, count)])
        at += count
        for c in range(COMP):
            copy(rhs.at[c, pl.ds(first_r, count_r)], buffer.at[pl.ds(at, count_r)])
            at += count_r

    rows_of(to_below, ABOVE, 0, 0, ABOVE - 1)
    rows_of(to_above, BELOW, rows - BELOW, rows - BELOW + 1, BELOW - 1)
    for buffer, first in ((to_left, 0), (to_right, cols - TILE)):
        copy(u.at[:, :, pl.ds(first, TILE)], buffer.at[pl.ds(0, COMP)])
        copy(rhs.at[:, :, pl.ds(first, TILE)], buffer.at[pl.ds(COMP, COMP)])
        copy(visc.at[:, pl.ds(first, TILE)], buffer.at[2 * COMP])
    for each in copies:
        each.wait()


def pack(u, rhs, visc):
    rows, cols, lanes = visc.shape
    f32 = jnp.float32
    shapes = (
        ((4 * ABOVE + 3 * (ABOVE - 1)), cols, lanes),
        ((4 * BELOW + 3 * (BELOW - 1)), cols, lanes),
        (2 * COMP + 1, rows, TILE, lanes),
        (2 * COMP + 1, rows, TILE, lanes),
    )
    return pl.pallas_call(
        pack_kernel,
        out_shape=[jax.ShapeDtypeStruct(s, f32) for s in shapes],
        in_specs=[pl.BlockSpec(memory_space=pltpu.HBM)] * 3,
        out_specs=[pl.BlockSpec(memory_space=pltpu.VMEM)] * 4,
        scratch_shapes=[pltpu.SemaphoreType.DMA((20,))],
        compiler_params=pltpu.CompilerParams(vmem_limit_bytes=8 << 20),
        cost_estimate=pl.CostEstimate(flops=0, bytes_accessed=4 << 20, transcendentals=0),
        name="pack",
    )(*(pltpu.with_memory_space_constraint(x, pltpu.HBM) for x in (u, rhs, visc)))


def corner_kernel(left, right, to_below, to_above):
    rows = left.shape[1]
    late = lax.broadcasted_iota(jnp.int32, left.shape[2:], 0) >= TILE - BELOW

    def rows_of(buffer, count, first_n, first_r, count_r):
        at = 0
        picks = [(c, first_n + i) for c in range(COMP) for i in range(count)]
        picks += [(2 * COMP, first_n + i) for i in range(count)]
        picks += [(COMP + c, first_r + i) for c in range(COMP) for i in range(count_r)]
        for field, row in picks:
            buffer[at] = jnp.where(late, left[field, row], right[field, row])
            at += 1

    rows_of(to_below, ABOVE, 0, 0, ABOVE - 1)
    rows_of(to_above, BELOW, rows - BELOW, rows - BELOW + 1, BELOW - 1)


def corners(left, right):
    lanes = left.shape[-1]
    shapes = (
        ((4 * ABOVE + 3 * (ABOVE - 1)), TILE, lanes),
        ((4 * BELOW + 3 * (BELOW - 1)), TILE, lanes),
    )
    return pl.pallas_call(
        corner_kernel,
        out_shape=[jax.ShapeDtypeStruct(s, jnp.float32) for s in shapes],
        in_specs=[pl.BlockSpec(memory_space=pltpu.VMEM)] * 2,
        out_specs=[pl.BlockSpec(memory_space=pltpu.VMEM)] * 2,
        compiler_params=pltpu.CompilerParams(vmem_limit_bytes=8 << 20),
        cost_estimate=pl.CostEstimate(flops=0, bytes_accessed=1 << 20, transcendentals=0),
        name="corners",
    )(left, right)


def smooth_kernel(
    wts, u, rhs, visc, left, right, above, below, above_c, below_c,
    smoothed, coarse,
    a, b, force, n, coef, inv, restr,
):
    rows, cols, lanes = visc.shape
    wide = cols + TILE
    tiles = wide // TILE
    late = lax.broadcasted_iota(jnp.int32, (TILE, lanes), 0) >= TILE - BELOW
    lane = lax.broadcasted_iota(jnp.int32, (TILE, lanes), 1)

    def part(ref, at, t, shift=0):
        return ref[(*at, pl.ds(TILE * (t + 1) + shift, TILE))]

    def put(ref, at, t, value):
        ref[(*at, pl.ds(TILE * (t + 1), TILE))] = value

    def put_round(ref, at, t, value):
        put(ref, at, t, value)
        if t == 0:
            put(ref, at, tiles, value)
        if t == tiles - 1:
            put(ref, at, -1, value)

    def ahead(x):
        return pltpu.roll(x, lanes - 1, 1)

    def behind(x):
        return pltpu.roll(x, 1, 1)

    def lay(ref, at, main, side):
        for t in range(tiles - 1):
            put_round(ref, at, t, main(t))
        put_round(ref, at, tiles - 1, side)

    def lay_force(c, at, main, side):
        for t in range(tiles - 1):
            force[c, at, pl.ds(TILE * t, TILE)] = main(t)
        force[c, at, pl.ds(cols, TILE)] = side

    def of(ref, *at):
        return lambda t: ref[(*at, pl.ds(TILE * t, TILE))]

    def own_step(r, _):
        at = r + BELOW
        for c in range(COMP):
            lay(a, (c, at), of(u, c, r), jnp.where(late, left[c, r], right[c, r]))
            lay_force(c, at, of(rhs, c, r), jnp.where(late, left[COMP + c, r], right[COMP + c, r]))
        lay(n, (at,), of(visc, r), jnp.where(late, left[2 * COMP, r], right[2 * COMP, r]))
        return 0

    def halo(main, side, first, count, first_r, count_r):
        def step(i, _):
            for c in range(COMP):
                lay(a, (c, first + i), of(main, c * count + i), side[c * count + i])
            lay(n, (first + i,), of(main, COMP * count + i), side[COMP * count + i])
            return 0

        def step_r(i, _):
            for c in range(COMP):
                j = (COMP + 1) * count + c * count_r + i
                lay_force(c, first_r + i, of(main, j), side[j])
            return 0

        lax.fori_loop(0, count, step, 0)
        lax.fori_loop(0, count_r, step_r, 0)

    lax.fori_loop(0, rows, own_step, 0)
    halo(above, above_c, BELOW + rows, ABOVE, BELOW + rows, ABOVE - 1)
    halo(below, below_c, 0, BELOW, 1, BELOW - 1)

    plain = ((1, 0, 0), (0, 1, 1), (1, 1, 3), (-1, 0, 0), (0, -1, 1), (-1, -1, 3))
    from_next = ((0, 0, 2), (1, 0, 4), (0, 1, 5), (1, 1, 6))
    from_prev = ((0, 0, 2), (-1, 0, 4), (0, -1, 5), (-1, -1, 6))
    groups = (plain, from_next, from_prev)

    half = [0.5 * wts[k] for k in range(7)]
    lost = half[2] + half[4] + half[5] + half[6]
    rim = jnp.where((lane == 0) | (lane == lanes - 1), lost, 0.0)
    weight = [[half[k] for _, _, k in plain]]
    weight += [[jnp.where(lane > 0, half[k], 0.0) for _, _, k in from_next]]
    weight += [[jnp.where(lane < lanes - 1, half[k], 0.0) for _, _, k in from_prev]]

    def total(terms):
        while len(terms) > 1:
            terms = [sum(terms[i : i + 2]) for i in range(0, len(terms), 2)]
        return terms[0]

    def coef_step(at, _):
        for t in range(tiles):
            here = part(n, (at,), t)
            sums, j = [], 0
            for group, own, ws in zip(groups, (here, behind(here), ahead(here)), weight):
                cs = []
                for (up, side, _), w in zip(group, ws):
                    cs.append(w * (own + part(n, (at + up,), t, side)))
                    coef[j, at, pl.ds(TILE * t, TILE)] = cs[-1]
                    j += 1
                sums.append(total(cs))
            diag = (sums[0] + rim * here) + (ahead(sums[1]) + behind(sums[2]))
            inv[at, pl.ds(TILE * t, TILE)] = jnp.where(here > 0.0, 1.0 / diag, 0.0)
        return 0

    last = BELOW + rows + ABOVE - 1
    lax.fori_loop(1, last, coef_step, 0, unroll=2)

    def sweep(field, first, end, store):
        def step(at, _):
            for t in range(tiles):
                here = pl.ds(TILE * t, TILE)
                cs = [coef[j, at, here] for j in range(14)]
                invd = inv[at, here]
                for c in range(COMP):
                    sums, j = [], 0
                    for group in groups:
                        terms = []
                        for up, side, _ in group:
                            terms.append(cs[j] * part(field, (c, at + up), t, side))
                            j += 1
                        sums.append(total(terms))
                    target = (sums[0] + force[c, at, here]) + (ahead(sums[1]) + behind(sums[2]))
                    store(c, at, t, part(field, (c, at), t), target * invd)
            return 0

        lax.fori_loop(first, end, step, 0, unroll=3)

    def store1(c, at, t, v, target):
        put_round(b, (c, at), t, (1.0 - OMEGA) * v + OMEGA * target)

    def store2(c, at, t, v, target):
        put_round(a, (c, at), t, (1.0 - OMEGA) * v + OMEGA * target)

    def store3(c, at, t, v, target):
        b[c, at, pl.ds(TILE * (t + 1), TILE)] = target - v

    sweep(a, 1, last, store1)
    sweep(b, 2, last - 1, store2)
    smoothed[...] = a[:, BELOW : BELOW + rows, TILE : TILE + cols]
    sweep(a, 3, last - 2, store3)

    for c in range(COMP):
        for i in range(rows // 2):
            at = BELOW + 2 * i
            restr[c * (rows // 2) + i] = 0.25 * (b[c, at, TILE:] + b[c, at + 2, TILE:]) + 0.5 * b[c, at + 1, TILE:]
    parts = []
    for i in range(COMP * (rows // 2)):
        p = restr[i, pl.ds(0, cols // 2, stride=2)]
        q = restr[i, pl.ds(1, cols // 2, stride=2)]
        d = restr[i, pl.ds(2, cols // 2, stride=2)]
        parts.append(0.25 * (p + d) + 0.5 * q)
    source = lax.broadcasted_iota(jnp.int32, (lanes, lanes // 2), 0)
    target = 2 * lax.broadcasted_iota(jnp.int32, (lanes, lanes // 2), 1)
    gap = source - target
    h = jnp.where(gap == 1, 0.5, jnp.where((gap == 0) | (gap == 2), 0.25, 0.0))
    for c in range(COMP):
        block = jnp.concatenate(parts[c * (rows // 2) : (c + 1) * (rows // 2)], 0)
        out = jnp.dot(block, h, precision=lax.Precision.HIGHEST, preferred_element_type=jnp.float32)
        coarse[c] = out.reshape(rows // 2, cols // 2, lanes // 2)


def smooth(wts, u, rhs, visc, left, right, above, below, above_c, below_c):
    rows, cols, lanes = visc.shape
    deep, wide = rows + BELOW + ABOVE, cols + TILE
    f32 = jnp.float32
    vmem = pl.BlockSpec(memory_space=pltpu.VMEM)
    padded = wide + 2 * TILE
    return pl.pallas_call(
        smooth_kernel,
        out_shape=[
            jax.ShapeDtypeStruct(u.shape, f32),
            jax.ShapeDtypeStruct((COMP, rows // 2, cols // 2, lanes // 2), f32),
        ],
        in_specs=[pl.BlockSpec(memory_space=pltpu.SMEM)] + [vmem] * 9,
        out_specs=[vmem] * 2,
        scratch_shapes=[pltpu.VMEM((COMP, deep, padded, lanes), f32)] * 2
        + [pltpu.VMEM((COMP, deep, wide, lanes), f32)]
        + [pltpu.VMEM((deep, padded, lanes), f32)]
        + [
            pltpu.VMEM((14, deep, wide, lanes), f32),
            pltpu.VMEM((deep, wide, lanes), f32),
            pltpu.VMEM((COMP * (rows // 2), wide + TILE, lanes), f32),
        ],
        compiler_params=pltpu.CompilerParams(vmem_limit_bytes=24 << 20),
        cost_estimate=pl.CostEstimate(flops=50_000_000, bytes_accessed=4 << 20, transcendentals=0),
        name="smooth",
    )(wts, u, rhs, visc, left, right, above, below, above_c, below_c)


def sent(value, axis, steps):
    count = lax.axis_size(axis)
    pairs = [(i, i + steps) for i in range(count) if 0 <= i + steps < count]
    return lax.ppermute(value, axis, pairs)


def per_device(solution, right_side, viscosity, stencil_weights):
    to_below, to_above, to_left, to_right = pack(solution, right_side, viscosity)
    above = sent(to_below, "shell", -1)
    right = sent(to_left, "lat", -1)
    left = sent(to_right, "lat", 1)
    below = sent(to_above, "shell", 1)
    to_below_c, to_above_c = corners(left, right)
    above_c = sent(to_below_c, "shell", -1)
    below_c = sent(to_above_c, "shell", 1)
    return smooth(
        stencil_weights, solution, right_side, viscosity, left, right, above, below, above_c, below_c
    )


def solution(mesh):
    in_specs = (
        P(None, "shell", "lat", None),
        P(None, "shell", "lat", None),
        P("shell", "lat", None),
        P(),
    )
    out_specs = (P(None, "shell", "lat", None), P(None, "shell", "lat", None))
    return jax.shard_map(
        per_device, mesh=mesh, in_specs=in_specs, out_specs=out_specs, check_vma=False
    )
```

time: 52.4 us -> 44.1 us (0.84)
  Pallas kernels: 15.6 us -> 10.5 us
  local copies, waits for them, and re-layouts: 3.23 us -> 0.02 us
    pallas_call x1, Pallas kernels: 13.4 us -> 8.67 us  [smooth(): pl.pallas_call(smooth_kernel, out_shape=[jax.ShapeDtypeStruct(u.shape, f3...]
    unnamed x14 -> x8, local copies, waits for them, and re-layouts: 3.23 us -> 0.02 us
where the time goes in v2:
time: 44.1 us; the launch traced here: 43.8 us
  starting transfers between devices  23.8 us (54%)
  Pallas kernels  10.5 us (24%)
  waiting for transfers between devices  8.7 us (20%)
  between operations  0.76 us (2%)
    ppermute x6, starting transfers between devices, sent(): return lax.ppermute(value, axis, pairs)  23.8 us
    ppermute x6, waiting for transfers between devices, sent(): return lax.ppermute(value, axis, pairs)  8.7 us
    pallas_call x1, Pallas kernels, smooth(): pl.pallas_call(smooth_kernel, out_shape=[jax.ShapeDtypeStruct(u.shape, f3...  8.67 us
    pallas_call x1, Pallas kernels, pack(): pl.pallas_call(pack_kernel, out_shape=[jax.ShapeDtypeStruct(s, f32) for s...  1.81 us
  transfers between devices with their start and end apart: 6, of which 3 were waited for; matrix products, arithmetic and copies ran while one was open for 0% of the time, Pallas kernels for 0%

profile of v2, /device:TPU:38, one launch (start us, length us, event | category | flops | bytes accessed | tf_op | source)
XLA Modules:
  0.0 43.8 jit_solution(6344177255176222273)
XLA Ops:
  0.6 0.0 copy-start.1
  0.6 0.0 copy-start
  0.6 1.8 %pack.1 = (f32[25,64,128]{2,1,0:T(8,128)S(1)}, f32[18,64,128]{2,1,0:T(8,128)S(1)}, f32[7,8,8,128]{3,2,1,0:T(8,128)S(1)}, f32[7,8,8,128]{3,2,1,0:T(8,128)S(1)}) custom-call(f32[3,8,64,128]{3,2,1,0:T(8,128)} %u.3, f32[3,8,64,128]{3,2,1,0:T(8,128)} %rhs.3, f32[8,64,128]{2,1,0:T(8,128)} %visc.3), custom_call_target="tpu_custom_call" | custom-call | bytes 4194304 | tf_op jit(solution)/shard_map/pack/pallas_call | solution.py:53
  2.5 0.0 copy-start.2
  2.5 2.5 %collective-permute-start.2 = (f32[25,64,128]{2,1,0:T(8,128)S(1)}, f32[25,64,128]{2,1,0:T(8,128)S(1)}, u32[]{:S(2)}, u32[]{:S(2)}) collective-permute-start(f32[25,64,128]{2,1,0:T(8,128)S(1)} %get-tuple-element.10), channel_id=1, source_target_pairs={{64,0},{128,64},{192,128},{256,192},{320,256},{384,320},{448,384},... | collective-permute-start | bytes 2457608 | tf_op jit(solution)/shard_map/ppermute | solution.py:290
  5.0 3.5 %collective-permute-start.3 = (f32[18,64,128]{2,1,0:T(8,128)S(1)}, f32[18,64,128]{2,1,0:T(8,128)S(1)}, u32[]{:S(2)}, u32[]{:S(2)}) collective-permute-start(f32[18,64,128]{2,1,0:T(8,128)S(1)} %get-tuple-element.11), channel_id=1, source_target_pairs={{0,64},{64,128},{128,192},{192,256},{256,320},{320,384},{384,448},... | collective-permute-start | bytes 1769480 | tf_op jit(solution)/shard_map/ppermute | solution.py:290
  8.5 1.9 %collective-permute-start = (f32[7,8,8,128]{3,2,1,0:T(8,128)S(1)}, f32[7,8,8,128]{3,2,1,0:T(8,128)S(1)}, u32[]{:S(2)}, u32[]{:S(2)}) collective-permute-start(f32[7,8,8,128]{3,2,1,0:T(8,128)S(1)} %get-tuple-element.8), channel_id=1, source_target_pairs={{0,1},{1,2},{2,3},{3,4},{4,5},{5,6},{6,7},{7,8},{8,9},{9,10},{10,1... | collective-permute-start | bytes 688136 | tf_op jit(solution)/shard_map/ppermute | solution.py:290
  10.4 10.1 %collective-permute-start.1 = (f32[7,8,8,128]{3,2,1,0:T(8,128)S(1)}, f32[7,8,8,128]{3,2,1,0:T(8,128)S(1)}, u32[]{:S(2)}, u32[]{:S(2)}) collective-permute-start(f32[7,8,8,128]{3,2,1,0:T(8,128)S(1)} %get-tuple-element.9), channel_id=1, source_target_pairs={{1,0},{2,1},{3,2},{4,3},{5,4},{6,5},{7,6},{8,7},{9,8},{10,9},{11,1... | collective-permute-start | bytes 688136 | tf_op jit(solution)/shard_map/ppermute | solution.py:290
  20.5 1.8 %collective-permute-done.left = f32[7,8,8,128]{3,2,1,0:T(8,128)S(1)} collective-permute-done((f32[7,8,8,128]{3,2,1,0:T(8,128)S(1)}, f32[7,8,8,128]{3,2,1,0:T(8,128)S(1)}, u32[]{:S(2)}, u32[]{:S(2)}) %collective-permute-start) | collective-permute-done | bytes 229408 | tf_op jit(solution)/shard_map/ppermute | solution.py:290
  22.3 1.8 %collective-permute-done.1.right = f32[7,8,8,128]{3,2,1,0:T(8,128)S(1)} collective-permute-done((f32[7,8,8,128]{3,2,1,0:T(8,128)S(1)}, f32[7,8,8,128]{3,2,1,0:T(8,128)S(1)}, u32[]{:S(2)}, u32[]{:S(2)}) %collective-permute-start.1) | collective-permute-done | bytes 229408 | tf_op jit(solution)/shard_map/ppermute | solution.py:290
  24.0 0.0 copy-start.3
  24.1 3.6 %collective-permute-start.4 = (f32[25,8,128]{2,1,0:T(8,128)S(1)}, f32[25,8,128]{2,1,0:T(8,128)S(1)}, u32[]{:S(2)}, u32[]{:S(2)}) collective-permute-start(f32[25,8,128]{2,1,0:T(8,128)S(1)} %get-tuple-element.12), channel_id=1, source_target_pairs={{64,0},{128,64},{192,128},{256,192},{320,256},{384,320},{448,384},... | collective-permute-start | bytes 307208 | tf_op jit(solution)/shard_map/ppermute | solution.py:290
  27.6 2.3 %collective-permute-start.5 = (f32[18,8,128]{2,1,0:T(8,128)S(1)}, f32[18,8,128]{2,1,0:T(8,128)S(1)}, u32[]{:S(2)}, u32[]{:S(2)}) collective-permute-start(f32[18,8,128]{2,1,0:T(8,128)S(1)} %get-tuple-element.13), channel_id=1, source_target_pairs={{0,64},{64,128},{128,192},{192,256},{256,320},{320,384},{384,448},... | collective-permute-start | bytes 221192 | tf_op jit(solution)/shard_map/ppermute | solution.py:290
  29.9 5.2 %collective-permute-done.5.below_c = f32[18,8,128]{2,1,0:T(8,128)S(1)} collective-permute-done((f32[18,8,128]{2,1,0:T(8,128)S(1)}, f32[18,8,128]{2,1,0:T(8,128)S(1)}, u32[]{:S(2)}, u32[]{:S(2)}) %collective-permute-start.5) | collective-permute-done | bytes 73760 | tf_op jit(solution)/shard_map/ppermute | solution.py:290
  35.1 0.0 collective-permute-done.4.above_c
  35.1 0.0 collective-permute-done.3.below
  35.1 0.0 collective-permute-done.2.above
  35.1 0.0 copy-done.1
  35.1 0.0 copy-done
  35.1 0.0 copy-done.2
  35.1 0.0 copy-done.3
  35.1 8.7 %smooth.1 = (f32[3,8,64,128]{3,2,1,0:T(8,128)}, f32[3,4,32,64]{3,2,1,0:T(8,128)}) custom-call(f32[7]{0:T(128)S(1)} %copy-done.3, f32[3,8,64,128]{3,2,1,0:T(8,128)S(1)} %copy-done, f32[3,8,64,128]{3,2,1,0:T(8,128)S(1)} %copy-done.1, f32[8,64,128]{2,1,0:T(8,128)S(1)} %copy-done.2, f32[7,8,8,128]{3,2,1,0:T(8,128)S(1)} %collective-permute-done.left, ...), custom_call_target="tpu_custom_call" | custom-call | flops 50000000 | bytes 4194304 | tf_op jit(solution)/shard_map/smooth/pallas_call | solution.py:265
  (1 shorter events, 0.0 us)
Async XLA Ops:
  0.6 34.5 %copy-start.1 = (f32[3,8,64,128]{3,2,1,0:T(8,128)S(1)}, f32[3,8,64,128]{3,2,1,0:T(8,128)}, u32[]{:S(2)}) copy-start(f32[3,8,64,128]{3,2,1,0:T(8,128)} %rhs.3) | copy-start | bytes 2359300
  0.6 34.5 %copy-start = (f32[3,8,64,128]{3,2,1,0:T(8,128)S(1)}, f32[3,8,64,128]{3,2,1,0:T(8,128)}, u32[]{:S(2)}) copy-start(f32[3,8,64,128]{3,2,1,0:T(8,128)} %u.3) | copy-start | bytes 2359300
  2.5 32.7 %copy-start.2 = (f32[8,64,128]{2,1,0:T(8,128)S(1)}, f32[8,64,128]{2,1,0:T(8,128)}, u32[]{:S(2)}) copy-start(f32[8,64,128]{2,1,0:T(8,128)} %visc.3) | copy-start | bytes 786436
  2.5 32.6 %collective-permute-start.2 = (f32[25,64,128]{2,1,0:T(8,128)S(1)}, f32[25,64,128]{2,1,0:T(8,128)S(1)}, u32[]{:S(2)}, u32[]{:S(2)}) collective-permute-start(f32[25,64,128]{2,1,0:T(8,128)S(1)} %get-tuple-element.10), channel_id=1, source_target_pairs={{64,0},{128,64},{192,128},{256,192},{320,256},{384,320},{448,384},... | collective-permute-start | bytes 2457608 | tf_op jit(solution)/shard_map/ppermute | solution.py:290
  5.0 30.1 %collective-permute-start.3 = (f32[18,64,128]{2,1,0:T(8,128)S(1)}, f32[18,64,128]{2,1,0:T(8,128)S(1)}, u32[]{:S(2)}, u32[]{:S(2)}) collective-permute-start(f32[18,64,128]{2,1,0:T(8,128)S(1)} %get-tuple-element.11), channel_id=1, source_target_pairs={{0,64},{64,128},{128,192},{192,256},{256,320},{320,384},{384,448},... | collective-permute-start | bytes 1769480 | tf_op jit(solution)/shard_map/ppermute | solution.py:290
  8.5 13.8 %collective-permute-start = (f32[7,8,8,128]{3,2,1,0:T(8,128)S(1)}, f32[7,8,8,128]{3,2,1,0:T(8,128)S(1)}, u32[]{:S(2)}, u32[]{:S(2)}) collective-permute-start(f32[7,8,8,128]{3,2,1,0:T(8,128)S(1)} %get-tuple-element.8), channel_id=1, source_target_pairs={{0,1},{1,2},{2,3},{3,4},{4,5},{5,6},{6,7},{7,8},{8,9},{9,10},{10,1... | collective-permute-start | bytes 688136 | tf_op jit(solution)/shard_map/ppermute | solution.py:290
  10.4 13.6 %collective-permute-start.1 = (f32[7,8,8,128]{3,2,1,0:T(8,128)S(1)}, f32[7,8,8,128]{3,2,1,0:T(8,128)S(1)}, u32[]{:S(2)}, u32[]{:S(2)}) collective-permute-start(f32[7,8,8,128]{3,2,1,0:T(8,128)S(1)} %get-tuple-element.9), channel_id=1, source_target_pairs={{1,0},{2,1},{3,2},{4,3},{5,4},{6,5},{7,6},{8,7},{9,8},{10,9},{11,1... | collective-permute-start | bytes 688136 | tf_op jit(solution)/shard_map/ppermute | solution.py:290
  24.0 11.1 %copy-start.3 = (f32[7]{0:T(128)S(1)}, f32[7]{0:T(128)}, u32[]{:S(2)}) copy-start(f32[7]{0:T(128)} %wts.1) | copy-start | bytes 88
  24.1 11.0 %collective-permute-start.4 = (f32[25,8,128]{2,1,0:T(8,128)S(1)}, f32[25,8,128]{2,1,0:T(8,128)S(1)}, u32[]{:S(2)}, u32[]{:S(2)}) collective-permute-start(f32[25,8,128]{2,1,0:T(8,128)S(1)} %get-tuple-element.12), channel_id=1, source_target_pairs={{64,0},{128,64},{192,128},{256,192},{320,256},{384,320},{448,384},... | collective-permute-start | bytes 307208 | tf_op jit(solution)/shard_map/ppermute | solution.py:290
  27.6 7.5 %collective-permute-start.5 = (f32[18,8,128]{2,1,0:T(8,128)S(1)}, f32[18,8,128]{2,1,0:T(8,128)S(1)}, u32[]{:S(2)}, u32[]{:S(2)}) collective-permute-start(f32[18,8,128]{2,1,0:T(8,128)S(1)} %get-tuple-element.13), channel_id=1, source_target_pairs={{0,64},{64,128},{128,192},{192,256},{256,320},{320,384},{384,448},... | collective-permute-start | bytes 221192 | tf_op jit(solution)/shard_map/ppermute | solution.py:290

commit v3 on v2

v3 whole, which is shorter than its diff:
```python
import jax
import jax.numpy as jnp
from jax import lax
from jax.experimental import pallas as pl
from jax.experimental.pallas import tpu as pltpu
from jax.sharding import PartitionSpec as P

OMEGA = 0.6
COMP = 3
BELOW = 3
ABOVE = 4
TILE = 8


def turned(x):
    return pltpu.roll(x, TILE // 2, 0)


def row_of(ref, field, pair, odd):
    return turned(ref[field, pair]) if odd else ref[field, pair]


def pack_kernel(u, rhs, visc, to_left, to_right, to_below, to_above, first_cols, last_cols, sems):
    rows, cols, lanes = visc.shape
    pairs = []
    for buffer, first in ((first_cols, 0), (last_cols, cols - TILE)):
        pairs.append((u.at[:, :, pl.ds(first, TILE)], buffer.at[pl.ds(0, COMP)]))
        pairs.append((rhs.at[:, :, pl.ds(first, TILE)], buffer.at[pl.ds(COMP, COMP)]))
        pairs.append((visc.at[:, pl.ds(first, TILE)], buffer.at[2 * COMP]))
    for buffer, count, first in ((to_below, ABOVE, 0), (to_above, BELOW, rows - BELOW)):
        short, first_r = count - 1, first if first == 0 else first + 1
        for c in range(COMP):
            pairs.append((u.at[c, pl.ds(first, count)], buffer.at[pl.ds(c * count, count)]))
        pairs.append((visc.at[pl.ds(first, count)], buffer.at[pl.ds(COMP * count, count)]))
        for c in range(COMP):
            at = (COMP + 1) * count + c * short
            pairs.append((rhs.at[c, pl.ds(first_r, short)], buffer.at[pl.ds(at, short)]))
    copies = [pltpu.make_async_copy(src, dst, sems.at[i]) for i, (src, dst) in enumerate(pairs)]
    for each in copies:
        each.start()
    for each in copies[:6]:
        each.wait()
    low = lax.broadcasted_iota(jnp.int32, (TILE, lanes), 0) < TILE // 2
    for field in range(2 * COMP + 1):
        for i in range(rows // 2):
            a, b = first_cols[field, 2 * i], first_cols[field, 2 * i + 1]
            to_left[field, i] = jnp.where(low, a, turned(b))
            a, b = last_cols[field, 2 * i], last_cols[field, 2 * i + 1]
            to_right[field, i] = jnp.where(low, turned(b), a)
    for each in copies[6:]:
        each.wait()


def shell_rows(count):
    return (COMP + 1) * count + COMP * (count - 1)


def pack(u, rhs, visc):
    rows, cols, lanes = visc.shape
    shapes = ((2 * COMP + 1, rows // 2, TILE, lanes),) * 2
    shapes += ((shell_rows(ABOVE), cols, lanes), (shell_rows(BELOW), cols, lanes))
    return pl.pallas_call(
        pack_kernel,
        out_shape=[jax.ShapeDtypeStruct(s, jnp.float32) for s in shapes],
        in_specs=[pl.BlockSpec(memory_space=pltpu.HBM)] * 3,
        out_specs=[pl.BlockSpec(memory_space=pltpu.VMEM)] * 4,
        scratch_shapes=[pltpu.VMEM((2 * COMP + 1, rows, TILE, lanes), jnp.float32)] * 2
        + [pltpu.SemaphoreType.DMA((20,))],
        compiler_params=pltpu.CompilerParams(vmem_limit_bytes=8 << 20),
        cost_estimate=pl.CostEstimate(flops=0, bytes_accessed=4 << 20, transcendentals=0),
        name="pack",
    )(*(pltpu.with_memory_space_constraint(x, pltpu.HBM) for x in (u, rhs, visc)))


def held(value, until):
    anywhere = pl.BlockSpec(memory_space=pl.ANY)
    return pl.pallas_call(
        lambda *_: None,
        out_shape=jax.ShapeDtypeStruct(value.shape, value.dtype),
        in_specs=[anywhere] * 2,
        out_specs=anywhere,
        input_output_aliases={0: 0},
        cost_estimate=pl.CostEstimate(flops=0, bytes_accessed=1024, transcendentals=0),
        name="held",
    )(value, until)


def corner_kernel(left, right, to_below, to_above):
    rows = 2 * left.shape[1]
    late = lax.broadcasted_iota(jnp.int32, left.shape[2:], 0) >= TILE - BELOW

    def rows_of(buffer, count, first_n, first_r, count_r):
        at = 0
        picks = [(c, first_n + i) for c in range(COMP) for i in range(count)]
        picks += [(2 * COMP, first_n + i) for i in range(count)]
        picks += [(COMP + c, first_r + i) for c in range(COMP) for i in range(count_r)]
        for field, row in picks:
            buffer[at] = jnp.where(
                late, row_of(left, field, row // 2, row % 2), row_of(right, field, row // 2, row % 2)
            )
            at += 1

    rows_of(to_below, ABOVE, 0, 0, ABOVE - 1)
    rows_of(to_above, BELOW, rows - BELOW, rows - BELOW + 1, BELOW - 1)


def corners(left, right):
    lanes = left.shape[-1]
    shapes = (
        ((4 * ABOVE + 3 * (ABOVE - 1)), TILE, lanes),
        ((4 * BELOW + 3 * (BELOW - 1)), TILE, lanes),
    )
    return pl.pallas_call(
        corner_kernel,
        out_shape=[jax.ShapeDtypeStruct(s, jnp.float32) for s in shapes],
        in_specs=[pl.BlockSpec(memory_space=pltpu.VMEM)] * 2,
        out_specs=[pl.BlockSpec(memory_space=pltpu.VMEM)] * 2,
        compiler_params=pltpu.CompilerParams(vmem_limit_bytes=8 << 20),
        cost_estimate=pl.CostEstimate(flops=0, bytes_accessed=1 << 20, transcendentals=0),
        name="corners",
    )(left, right)


def stencil_parts(wts, a, b, force, n, coef, inv):
    wide, lanes = coef.shape[-2:]
    tiles = wide // TILE
    lane = lax.broadcasted_iota(jnp.int32, (TILE, lanes), 1)

    def over(step, spans):
        for first, end in spans:
            unroll = 3 if (end - first) % 3 == 0 else 2 if (end - first) % 2 == 0 else end - first
            lax.fori_loop(first, end, step, 0, unroll=unroll)

    def part(ref, at, t, shift=0):
        return ref[(*at, pl.ds(TILE * (t + 1) + shift, TILE))]

    def put(ref, at, t, value):
        ref[(*at, pl.ds(TILE * (t + 1), TILE))] = value

    def put_round(ref, at, t, value):
        put(ref, at, t, value)
        if t == 0:
            put(ref, at, tiles, value)
        if t == tiles - 1:
            put(ref, at, -1, value)

    def ahead(x):
        return pltpu.roll(x, lanes - 1, 1)

    def behind(x):
        return pltpu.roll(x, 1, 1)

    def lay(ref, at, main, side):
        for t in range(tiles - 1):
            put_round(ref, at, t, main(t))
        put_round(ref, at, tiles - 1, side)

    def lay_force(c, at, main, side):
        for t in range(tiles - 1):
            force[c, at, pl.ds(TILE * t, TILE)] = main(t)
        force[c, at, pl.ds(TILE * (tiles - 1), TILE)] = side

    def of(ref, *at):
        return lambda t: ref[(*at, pl.ds(TILE * t, TILE))]

    plain = ((1, 0, 0), (0, 1, 1), (1, 1, 3), (-1, 0, 0), (0, -1, 1), (-1, -1, 3))
    from_next = ((0, 0, 2), (1, 0, 4), (0, 1, 5), (1, 1, 6))
    from_prev = ((0, 0, 2), (-1, 0, 4), (0, -1, 5), (-1, -1, 6))
    groups = (plain, from_next, from_prev)

    half = [0.5 * wts[k] for k in range(7)]
    lost = half[2] + half[4] + half[5] + half[6]
    rim = jnp.where((lane == 0) | (lane == lanes - 1), lost, 0.0)
    weight = [[half[k] for _, _, k in plain]]
    weight += [[jnp.where(lane > 0, half[k], 0.0) for _, _, k in from_next]]
    weight += [[jnp.where(lane < lanes - 1, half[k], 0.0) for _, _, k in from_prev]]

    def total(terms):
        while len(terms) > 1:
            terms = [sum(terms[i : i + 2]) for i in range(0, len(terms), 2)]
        return terms[0]

    def coef_step(at, _):
        for t in range(tiles):
            here = part(n, (at,), t)
            sums, j = [], 0
            for group, own, ws in zip(groups, (here, behind(here), ahead(here)), weight):
                cs = []
                for (up, side, _), w in zip(group, ws):
                    cs.append(w * (own + part(n, (at + up,), t, side)))
                    coef[j, at, pl.ds(TILE * t, TILE)] = cs[-1]
                    j += 1
                sums.append(total(cs))
            diag = (sums[0] + rim * here) + (ahead(sums[1]) + behind(sums[2]))
            inv[at, pl.ds(TILE * t, TILE)] = jnp.where(here > 0.0, 1.0 / diag, 0.0)
        return 0

    def coefs(*spans):
        over(coef_step, spans)

    def sweep(field, store, *spans):
        def step(at, _):
            for t in range(tiles):
                here = pl.ds(TILE * t, TILE)
                cs = [coef[j, at, here] for j in range(14)]
                invd = inv[at, here]
                for c in range(COMP):
                    sums, j = [], 0
                    for group in groups:
                        terms = []
                        for up, side, _ in group:
                            terms.append(cs[j] * part(field, (c, at + up), t, side))
                            j += 1
                        sums.append(total(terms))
                    target = (sums[0] + force[c, at, here]) + (ahead(sums[1]) + behind(sums[2]))
                    store(c, at, t, part(field, (c, at), t), target * invd)
            return 0

        over(step, spans)

    def store1(c, at, t, v, target):
        put_round(b, (c, at), t, (1.0 - OMEGA) * v + OMEGA * target)

    def store2(c, at, t, v, target):
        put_round(a, (c, at), t, (1.0 - OMEGA) * v + OMEGA * target)

    def store3(c, at, t, v, target):
        b[c, at, pl.ds(TILE * (t + 1), TILE)] = target - v

    return (
        lay,
        lay_force,
        of,
        coefs,
        lambda *spans: sweep(a, store1, *spans),
        lambda *spans: sweep(b, store2, *spans),
        lambda *spans: sweep(a, store3, *spans),
    )


def inner_kernel(wts, u, rhs, visc, left, right, _, a, b, force, n, coef, inv):
    rows, cols, lanes = visc.shape
    late = lax.broadcasted_iota(jnp.int32, (TILE, lanes), 0) >= TILE - BELOW
    lay, lay_force, of, coefs, sweep1, sweep2, residual = stencil_parts(wts, a, b, force, n, coef, inv)

    def own_step(i, _):
        for odd in range(2):
            r = 2 * i + odd
            at = r + BELOW

            def side(field):
                return jnp.where(late, row_of(left, field, i, odd), row_of(right, field, i, odd))

            for c in range(COMP):
                lay(a, (c, at), of(u, c, r), side(c))
                lay_force(c, at, of(rhs, c, r), side(COMP + c))
            lay(n, (at,), of(visc, r), side(2 * COMP))
        return 0

    first, end = BELOW, BELOW + rows
    lax.fori_loop(0, rows // 2, own_step, 0)
    coefs((first + 1, end - 1))
    sweep1((first + 1, end - 1))
    sweep2((first + 2, end - 2))
    residual((first + 3, end - 3))


def outer_kernel(
    wts, above, below, above_c, below_c, *refs
):
    a, b, force, n, coef, inv = refs[6:12]
    smoothed, coarse, restr, sems = refs[12:]
    rows, cols = smoothed.shape[1:3]
    lanes = smoothed.shape[3]
    lay, lay_force, of, coefs, sweep1, sweep2, residual = stencil_parts(wts, a, b, force, n, coef, inv)

    def halo(main, side, first, count, first_r, count_r):
        def step(i, _):
            for c in range(COMP):
                lay(a, (c, first + i), of(main, c * count + i), side[c * count + i])
            lay(n, (first + i,), of(main, COMP * count + i), side[COMP * count + i])
            return 0

        def step_r(i, _):
            for c in range(COMP):
                j = (COMP + 1) * count + c * count_r + i
                lay_force(c, first_r + i, of(main, j), side[j])
            return 0

        lax.fori_loop(0, count, step, 0)
        lax.fori_loop(0, count_r, step_r, 0)

    halo(above, above_c, BELOW + rows, ABOVE, BELOW + rows, ABOVE - 1)
    halo(below, below_c, 0, BELOW, 1, BELOW - 1)

    first, end = BELOW, BELOW + rows
    coefs((first - 2, first + 1), (end - 1, end + 3))
    sweep1((first - 2, first + 1), (end - 1, end + 3))
    sweep2((first - 1, first + 2), (end - 2, end + 2))
    copies = [
        pltpu.make_async_copy(a.at[c, pl.ds(first, rows), pl.ds(TILE, cols)], smoothed.at[c], sems.at[c])
        for c in range(COMP)
    ]
    for each in copies:
        each.start()
    residual((first, first + 3), (end - 3, end + 1))

    for c in range(COMP):
        for i in range(rows // 2):
            at = BELOW + 2 * i
            restr[c * (rows // 2) + i] = 0.25 * (b[c, at, TILE:] + b[c, at + 2, TILE:]) + 0.5 * b[c, at + 1, TILE:]
    parts = []
    for i in range(COMP * (rows // 2)):
        p = restr[i, pl.ds(0, cols // 2, stride=2)]
        q = restr[i, pl.ds(1, cols // 2, stride=2)]
        d = restr[i, pl.ds(2, cols // 2, stride=2)]
        parts.append(0.25 * (p + d) + 0.5 * q)
    source = lax.broadcasted_iota(jnp.int32, (lanes, lanes // 2), 0)
    target = 2 * lax.broadcasted_iota(jnp.int32, (lanes, lanes // 2), 1)
    gap = source - target
    h = jnp.where(gap == 1, 0.5, jnp.where((gap == 0) | (gap == 2), 0.25, 0.0))
    for c in range(COMP):
        block = jnp.concatenate(parts[c * (rows // 2) : (c + 1) * (rows // 2)], 0)
        out = jnp.dot(block, h, precision=lax.Precision.HIGHEST, preferred_element_type=jnp.float32)
        coarse[c] = out.reshape(rows // 2, cols // 2, lanes // 2)
    for each in copies:
        each.wait()


def state_shapes(rows, cols, lanes):
    deep, wide = rows + BELOW + ABOVE, cols + TILE
    padded = wide + 2 * TILE
    shapes = (
        (COMP, deep, padded, lanes),
        (COMP, deep, padded, lanes),
        (COMP, deep, wide, lanes),
        (deep, padded, lanes),
        (14, deep, wide, lanes),
        (deep, wide, lanes),
    )
    return [jax.ShapeDtypeStruct(s, jnp.float32) for s in shapes]


def inner(wts, u, rhs, visc, left, right, after):
    vmem = pl.BlockSpec(memory_space=pltpu.VMEM)
    return pl.pallas_call(
        inner_kernel,
        out_shape=state_shapes(*visc.shape),
        in_specs=[pl.BlockSpec(memory_space=pltpu.SMEM)] + [vmem] * 5 + [pl.BlockSpec(memory_space=pl.ANY)],
        out_specs=[vmem] * 6,
        compiler_params=pltpu.CompilerParams(vmem_limit_bytes=16 << 20),
        cost_estimate=pl.CostEstimate(flops=20_000_000, bytes_accessed=16 << 20, transcendentals=0),
        name="inner",
    )(wts, u, rhs, visc, left, right, after)


def outer(wts, above, below, above_c, below_c, state, rows, cols, lanes):
    vmem = pl.BlockSpec(memory_space=pltpu.VMEM)
    f32 = jnp.float32
    shapes = state_shapes(rows, cols, lanes)
    out = pl.pallas_call(
        outer_kernel,
        out_shape=shapes
        + [
            jax.ShapeDtypeStruct((COMP, rows, cols, lanes), f32),
            jax.ShapeDtypeStruct((COMP, rows // 2, cols // 2, lanes // 2), f32),
        ],
        in_specs=[pl.BlockSpec(memory_space=pltpu.SMEM)] + [vmem] * 10,
        out_specs=[vmem] * 6 + [pl.BlockSpec(memory_space=pltpu.HBM), vmem],
        input_output_aliases={5 + i: i for i in range(6)},
        scratch_shapes=[
            pltpu.VMEM((COMP * (rows // 2), cols + 2 * TILE, lanes), f32),
            pltpu.SemaphoreType.DMA((COMP,)),
        ],
        compiler_params=pltpu.CompilerParams(vmem_limit_bytes=16 << 20),
        cost_estimate=pl.CostEstimate(flops=40_000_000, bytes_accessed=16 << 20, transcendentals=0),
        name="outer",
    )(wts, above, below, above_c, below_c, *state)
    return out[6], out[7]


def sent(value, axis, steps):
    count = lax.axis_size(axis)
    pairs = [(i, i + steps) for i in range(count) if 0 <= i + steps < count]
    return lax.ppermute(value, axis, pairs)


def per_device(solution, right_side, viscosity, stencil_weights):
    to_left, to_right, to_below, to_above = pack(solution, right_side, viscosity)
    above = sent(to_below, "shell", -1)
    below = sent(to_above, "shell", 1)
    left = sent(to_right, "lat", 1)
    right = sent(to_left, "lat", -1)
    to_below_c, to_above_c = corners(left, right)
    above_c = sent(to_below_c, "shell", -1)
    below_c = sent(to_above_c, "shell", 1)
    state = inner(stencil_weights, solution, right_side, viscosity, left, right, to_below_c)
    return outer(stencil_weights, above, below, above_c, below_c, state, *viscosity.shape)


def solution(mesh):
    in_specs = (
        P(None, "shell", "lat", None),
        P(None, "shell", "lat", None),
        P("shell", "lat", None),
        P(),
    )
    out_specs = (P(None, "shell", "lat", None), P(None, "shell", "lat", None))
    return jax.shard_map(
        per_device, mesh=mesh, in_specs=in_specs, out_specs=out_specs, check_vma=False
    )
```

time: 44.1 us -> 40.3 us (0.914)
  the two profiles are of different devices: /device:TPU:38 before, /device:TPU:30 now
where the time goes in v3:
time: 40.3 us; the launch traced here: 40 us
  starting transfers between devices  26.1 us (65%)
  Pallas kernels  10.8 us (27%)
  waiting for transfers between devices  2.36 us (6%)
  between operations  0.79 us (2%)
    ppermute x6, starting transfers between devices, sent(): return lax.ppermute(value, axis, pairs)  26.1 us
    pallas_call x1, Pallas kernels, outer(): pl.pallas_call(outer_kernel, out_shape=shapes + [jax.ShapeDtypeStruct((CO...  5.83 us
    pallas_call x1, Pallas kernels, inner(): pl.pallas_call(inner_kernel, out_shape=state_shapes(*visc.shape), in_spec...  3.12 us
    ppermute x6, waiting for transfers between devices, sent(): return lax.ppermute(value, axis, pairs)  2.36 us
    pallas_call x1, Pallas kernels, pack(): pl.pallas_call(pack_kernel, out_shape=[jax.ShapeDtypeStruct(s, jnp.float3...  1.8 us
  transfers between devices with their start and end apart: 6, of which 2 were waited for; matrix products, arithmetic and copies ran while one was open for 0% of the time, Pallas kernels for 8%

profile of v3, /device:TPU:30, one launch (start us, length us, event | category | flops | bytes accessed | tf_op | source)
XLA Modules:
  0.0 40.0 jit_solution(6124095030238206578)
XLA Ops:
  0.6 0.0 copy-start.2
  0.6 0.0 copy-start.1
  0.7 0.0 copy-start
  0.7 0.0 copy-start.3
  0.7 1.8 %pack.1 = (f32[7,4,8,128]{3,2,1,0:T(8,128)S(1)}, f32[7,4,8,128]{3,2,1,0:T(8,128)S(1)}, f32[25,64,128]{2,1,0:T(8,128)S(1)}, f32[18,64,128]{2,1,0:T(8,128)S(1)}) custom-call(f32[3,8,64,128]{3,2,1,0:T(8,128)} %u.3, f32[3,8,64,128]{3,2,1,0:T(8,128)} %rhs.3, f32[8,64,128]{2,1,0:T(8,128)} %visc.3), custom_call_target="tpu_custom_call" | custom-call | bytes 4194304 | tf_op jit(solution)/shard_map/pack/pallas_call | solution.py:62
  2.5 2.4 %collective-permute-start = (f32[25,64,128]{2,1,0:T(8,128)S(1)}, f32[25,64,128]{2,1,0:T(8,128)S(1)}, u32[]{:S(2)}, u32[]{:S(2)}) collective-permute-start(f32[25,64,128]{2,1,0:T(8,128)S(1)} %get-tuple-element.16), channel_id=1, source_target_pairs={{64,0},{128,64},{192,128},{256,192},{320,256},{384,320},{448,384},... | collective-permute-start | bytes 2457608 | tf_op jit(solution)/shard_map/ppermute | solution.py:385
  4.8 4.7 %collective-permute-start.1 = (f32[18,64,128]{2,1,0:T(8,128)S(1)}, f32[18,64,128]{2,1,0:T(8,128)S(1)}, u32[]{:S(2)}, u32[]{:S(2)}) collective-permute-start(f32[18,64,128]{2,1,0:T(8,128)S(1)} %get-tuple-element.17), channel_id=1, source_target_pairs={{0,64},{64,128},{128,192},{192,256},{256,320},{320,384},{384,448},... | collective-permute-start | bytes 1769480 | tf_op jit(solution)/shard_map/ppermute | solution.py:385
  9.5 1.9 %collective-permute-start.2 = (f32[7,4,8,128]{3,2,1,0:T(8,128)S(1)}, f32[7,4,8,128]{3,2,1,0:T(8,128)S(1)}, u32[]{:S(2)}, u32[]{:S(2)}) collective-permute-start(f32[7,4,8,128]{3,2,1,0:T(8,128)S(1)} %get-tuple-element.18), channel_id=1, source_target_pairs={{0,1},{1,2},{2,3},{3,4},{4,5},{5,6},{6,7},{7,8},{8,9},{9,10},{10,1... | collective-permute-start | bytes 344072 | tf_op jit(solution)/shard_map/ppermute | solution.py:385
  11.5 10.1 %collective-permute-start.3 = (f32[7,4,8,128]{3,2,1,0:T(8,128)S(1)}, f32[7,4,8,128]{3,2,1,0:T(8,128)S(1)}, u32[]{:S(2)}, u32[]{:S(2)}) collective-permute-start(f32[7,4,8,128]{3,2,1,0:T(8,128)S(1)} %get-tuple-element.19), channel_id=1, source_target_pairs={{1,0},{2,1},{3,2},{4,3},{5,4},{6,5},{7,6},{8,7},{9,8},{10,9},{11,1... | collective-permute-start | bytes 344072 | tf_op jit(solution)/shard_map/ppermute | solution.py:385
  21.6 0.5 %collective-permute-done.2.left = f32[7,4,8,128]{3,2,1,0:T(8,128)S(1)} collective-permute-done((f32[7,4,8,128]{3,2,1,0:T(8,128)S(1)}, f32[7,4,8,128]{3,2,1,0:T(8,128)S(1)}, u32[]{:S(2)}, u32[]{:S(2)}) %collective-permute-start.2) | collective-permute-done | bytes 114720 | tf_op jit(solution)/shard_map/ppermute | solution.py:385
  22.1 1.8 %collective-permute-done.3.right = f32[7,4,8,128]{3,2,1,0:T(8,128)S(1)} collective-permute-done((f32[7,4,8,128]{3,2,1,0:T(8,128)S(1)}, f32[7,4,8,128]{3,2,1,0:T(8,128)S(1)}, u32[]{:S(2)}, u32[]{:S(2)}) %collective-permute-start.3) | collective-permute-done | bytes 114720 | tf_op jit(solution)/shard_map/ppermute | solution.py:385
  23.9 1.9 %collective-permute-start.4 = (f32[25,8,128]{2,1,0:T(8,128)S(1)}, f32[25,8,128]{2,1,0:T(8,128)S(1)}, u32[]{:S(2)}, u32[]{:S(2)}) collective-permute-start(f32[25,8,128]{2,1,0:T(8,128)S(1)} %get-tuple-element.20._), channel_id=1, source_target_pairs={{64,0},{128,64},{192,128},{256,192},{320,256},{384,320},{448,384},... | collective-permute-start | bytes 307208 | tf_op jit(solution)/shard_map/ppermute | solution.py:385
  25.9 5.1 %collective-permute-start.5 = (f32[18,8,128]{2,1,0:T(8,128)S(1)}, f32[18,8,128]{2,1,0:T(8,128)S(1)}, u32[]{:S(2)}, u32[]{:S(2)}) collective-permute-start(f32[18,8,128]{2,1,0:T(8,128)S(1)} %get-tuple-element.21), channel_id=1, source_target_pairs={{0,64},{64,128},{128,192},{192,256},{256,320},{320,384},{384,448},... | collective-permute-start | bytes 221192 | tf_op jit(solution)/shard_map/ppermute | solution.py:385
  31.0 0.0 copy-done.2
  31.0 0.0 copy-done.1
  31.0 0.0 copy-done
  31.0 0.0 copy-done.3
  31.0 3.1 %inner.1 = (f32[3,15,88,128]{3,2,1,0:T(8,128)S(1)}, f32[3,15,88,128]{3,2,1,0:T(8,128)S(1)}, f32[3,15,72,128]{3,2,1,0:T(8,128)S(1)}, f32[15,88,128]{2,1,0:T(8,128...) custom-call(f32[7]{0:T(128)S(1)} %copy-done.3, f32[3,8,64,128]{3,2,1,0:T(8,128)S(1)} %copy-done, ...), custom_call_target="tpu_custom_call" | custom-call | flops 20000000 | bytes 16777216 | tf_op jit(solution)/shard_map/inner/pallas_call | solution.py:346
  34.2 0.0 collective-permute-done.5.below_c
  34.2 0.0 collective-permute-done.4.above_c
  34.2 0.0 collective-permute-done.1.below
  34.2 0.0 collective-permute-done.above
  34.2 5.8 %outer.1 = (f32[3,15,88,128]{3,2,1,0:T(8,128)S(1)}, f32[3,15,88,128]{3,2,1,0:T(8,128)S(1)}, f32[3,15,72,128]{3,2,1,0:T(8,128)S(1)}, f32[15,88,128]{2,1,0:T(8,128...) custom-call(f32[7]{0:T(128)S(1)} %copy-done.3, ...), custom_call_target="tpu_custom_call", output_to_operand_aliasing={{0}: (5, {}), {1}: (6, {}), {2}: (7, {}), {3}: (8, {}), {4}... | custom-call | flops 40000000 | bytes 16777216 | tf_op jit(solution)/shard_map/outer/pallas_call | solution.py:361
  (1 shorter events, 0.0 us)
Async XLA Ops:
  0.6 30.4 %copy-start.2 = (f32[8,64,128]{2,1,0:T(8,128)S(1)}, f32[8,64,128]{2,1,0:T(8,128)}, u32[]{:S(2)}) copy-start(f32[8,64,128]{2,1,0:T(8,128)} %visc.3) | copy-start | bytes 786436
  0.6 30.4 %copy-start.1 = (f32[3,8,64,128]{3,2,1,0:T(8,128)S(1)}, f32[3,8,64,128]{3,2,1,0:T(8,128)}, u32[]{:S(2)}) copy-start(f32[3,8,64,128]{3,2,1,0:T(8,128)} %rhs.3) | copy-start | bytes 2359300
  0.7 30.4 %copy-start = (f32[3,8,64,128]{3,2,1,0:T(8,128)S(1)}, f32[3,8,64,128]{3,2,1,0:T(8,128)}, u32[]{:S(2)}) copy-start(f32[3,8,64,128]{3,2,1,0:T(8,128)} %u.3) | copy-start | bytes 2359300
  0.7 30.4 %copy-start.3 = (f32[7]{0:T(128)S(1)}, f32[7]{0:T(128)}, u32[]{:S(2)}) copy-start(f32[7]{0:T(128)} %wts.3) | copy-start | bytes 88
  2.5 31.7 %collective-permute-start = (f32[25,64,128]{2,1,0:T(8,128)S(1)}, f32[25,64,128]{2,1,0:T(8,128)S(1)}, u32[]{:S(2)}, u32[]{:S(2)}) collective-permute-start(f32[25,64,128]{2,1,0:T(8,128)S(1)} %get-tuple-element.16), channel_id=1, source_target_pairs={{64,0},{128,64},{192,128},{256,192},{320,256},{384,320},{448,384},... | collective-permute-start | bytes 2457608 | tf_op jit(solution)/shard_map/ppermute | solution.py:385
  4.8 29.4 %collective-permute-start.1 = (f32[18,64,128]{2,1,0:T(8,128)S(1)}, f32[18,64,128]{2,1,0:T(8,128)S(1)}, u32[]{:S(2)}, u32[]{:S(2)}) collective-permute-start(f32[18,64,128]{2,1,0:T(8,128)S(1)} %get-tuple-element.17), channel_id=1, source_target_pairs={{0,64},{64,128},{128,192},{192,256},{256,320},{320,384},{384,448},... | collective-permute-start | bytes 1769480 | tf_op jit(solution)/shard_map/ppermute | solution.py:385
  9.5 12.6 %collective-permute-start.2 = (f32[7,4,8,128]{3,2,1,0:T(8,128)S(1)}, f32[7,4,8,128]{3,2,1,0:T(8,128)S(1)}, u32[]{:S(2)}, u32[]{:S(2)}) collective-permute-start(f32[7,4,8,128]{3,2,1,0:T(8,128)S(1)} %get-tuple-element.18), channel_id=1, source_target_pairs={{0,1},{1,2},{2,3},{3,4},{4,5},{5,6},{6,7},{7,8},{8,9},{9,10},{10,1... | collective-permute-start | bytes 344072 | tf_op jit(solution)/shard_map/ppermute | solution.py:385
  11.5 12.4 %collective-permute-start.3 = (f32[7,4,8,128]{3,2,1,0:T(8,128)S(1)}, f32[7,4,8,128]{3,2,1,0:T(8,128)S(1)}, u32[]{:S(2)}, u32[]{:S(2)}) collective-permute-start(f32[7,4,8,128]{3,2,1,0:T(8,128)S(1)} %get-tuple-element.19), channel_id=1, source_target_pairs={{1,0},{2,1},{3,2},{4,3},{5,4},{6,5},{7,6},{8,7},{9,8},{10,9},{11,1... | collective-permute-start | bytes 344072 | tf_op jit(solution)/shard_map/ppermute | solution.py:385
  23.9 10.2 %collective-permute-start.4 = (f32[25,8,128]{2,1,0:T(8,128)S(1)}, f32[25,8,128]{2,1,0:T(8,128)S(1)}, u32[]{:S(2)}, u32[]{:S(2)}) collective-permute-start(f32[25,8,128]{2,1,0:T(8,128)S(1)} %get-tuple-element.20._), channel_id=1, source_target_pairs={{64,0},{128,64},{192,128},{256,192},{320,256},{384,320},{448,384},... | collective-permute-start | bytes 307208 | tf_op jit(solution)/shard_map/ppermute | solution.py:385
  25.9 8.3 %collective-permute-start.5 = (f32[18,8,128]{2,1,0:T(8,128)S(1)}, f32[18,8,128]{2,1,0:T(8,128)S(1)}, u32[]{:S(2)}, u32[]{:S(2)}) collective-permute-start(f32[18,8,128]{2,1,0:T(8,128)S(1)} %get-tuple-element.21), channel_id=1, source_target_pairs={{0,64},{64,128},{128,192},{192,256},{256,320},{320,384},{384,448},... | collective-permute-start | bytes 221192 | tf_op jit(solution)/shard_map/ppermute | solution.py:385

commit v4 on v3

v4 whole, which is shorter than its diff:
```python
import functools

import jax
import jax.numpy as jnp
from jax import lax
from jax.experimental import pallas as pl
from jax.experimental.pallas import tpu as pltpu
from jax.sharding import PartitionSpec as P

OMEGA = 0.6
COMP = 3
BELOW = 3
ABOVE = 4
TILE = 8


GROUPS = (
    ((1, 0, 0), (0, 1, 1), (1, 1, 3), (-1, 0, 0), (0, -1, 1), (-1, -1, 3)),
    ((0, 0, 2), (1, 0, 4), (0, 1, 5), (1, 1, 6)),
    ((0, 0, 2), (-1, 0, 4), (0, -1, 5), (-1, -1, 6)),
)


def turned(x):
    return pltpu.roll(x, TILE // 2, 0)


def row_of(ref, field, pair, odd):
    return turned(ref[field, pair]) if odd else ref[field, pair]


NEAR = 14


def pack_kernel(
    wts, u, rhs, visc, to_left, to_right, to_below, to_above, own_visc, weight, first_cols, last_cols, held, sems
):
    rows, cols, lanes = visc.shape
    pairs = []
    for buffer, first in ((first_cols, 0), (last_cols, cols - TILE)):
        pairs.append((u.at[:, :, pl.ds(first, TILE)], buffer.at[pl.ds(0, COMP)]))
        pairs.append((rhs.at[:, :, pl.ds(first, TILE)], buffer.at[pl.ds(COMP, COMP)]))
        pairs.append((visc.at[:, pl.ds(first, TILE)], buffer.at[2 * COMP]))
    for buffer, count, first in ((to_below, ABOVE, 0), (to_above, BELOW, rows - BELOW)):
        short, first_r = count - 1, first if first == 0 else first + 1
        for c in range(COMP):
            pairs.append((u.at[c, pl.ds(first, count)], buffer.at[pl.ds(c * count, count)]))
        pairs.append((visc.at[pl.ds(first, count)], buffer.at[pl.ds(COMP * count, count)]))
        for c in range(COMP):
            at = (COMP + 1) * count + c * short
            pairs.append((rhs.at[c, pl.ds(first_r, short)], buffer.at[pl.ds(at, short)]))
    pairs.append((wts, held))
    pairs.append((visc, own_visc))
    copies = [pltpu.make_async_copy(src, dst, sems.at[i]) for i, (src, dst) in enumerate(pairs)]
    for each in copies:
        each.start()
    for each in copies[:6]:
        each.wait()
    low = lax.broadcasted_iota(jnp.int32, (TILE, lanes), 0) < TILE // 2
    for field in range(2 * COMP + 1):
        for i in range(rows // 2):
            a, b = first_cols[field, 2 * i], first_cols[field, 2 * i + 1]
            to_left[field, i] = jnp.where(low, a, turned(b))
            a, b = last_cols[field, 2 * i], last_cols[field, 2 * i + 1]
            to_right[field, i] = jnp.where(low, turned(b), a)
    for each in copies[6:]:
        each.wait()
    lane = lax.broadcasted_iota(jnp.int32, (TILE, lanes), 1)
    half = [0.5 * held[k] for k in range(7)]
    j = 0
    for group, inside in zip(GROUPS, (lane >= 0, lane > 0, lane < lanes - 1)):
        for _, _, k in group:
            weight[j] = jnp.where(inside, half[k], 0.0)
            j += 1
    lost = half[2] + half[4] + half[5] + half[6]
    weight[j] = jnp.where((lane == 0) | (lane == lanes - 1), lost, 0.0)


def shell_rows(count):
    return (COMP + 1) * count + COMP * (count - 1)


def pack(wts, u, rhs, visc):
    rows, cols, lanes = visc.shape
    shapes = ((2 * COMP + 1, rows // 2, TILE, lanes),) * 2
    shapes += ((shell_rows(ABOVE), cols, lanes), (shell_rows(BELOW), cols, lanes))
    shapes += (visc.shape, (NEAR + 1, TILE, lanes))
    return pl.pallas_call(
        pack_kernel,
        out_shape=[jax.ShapeDtypeStruct(s, jnp.float32) for s in shapes],
        in_specs=[pl.BlockSpec(memory_space=pltpu.HBM)] * 4,
        out_specs=[pl.BlockSpec(memory_space=pltpu.VMEM)] * 6,
        scratch_shapes=[pltpu.VMEM((2 * COMP + 1, rows, TILE, lanes), jnp.float32)] * 2
        + [pltpu.SMEM((7,), jnp.float32), pltpu.SemaphoreType.DMA((22,))],
        compiler_params=pltpu.CompilerParams(vmem_limit_bytes=8 << 20),
        cost_estimate=pl.CostEstimate(flops=0, bytes_accessed=4 << 20, transcendentals=0),
        name="pack",
    )(*(pltpu.with_memory_space_constraint(x, pltpu.HBM) for x in (wts, u, rhs, visc)))


def corner_kernel(left, right, _, to_below, to_above):
    rows = 2 * left.shape[1]
    late = lax.broadcasted_iota(jnp.int32, left.shape[2:], 0) >= TILE - BELOW

    def rows_of(buffer, count, first_n, first_r, count_r):
        at = 0
        picks = [(c, first_n + i) for c in range(COMP) for i in range(count)]
        picks += [(2 * COMP, first_n + i) for i in range(count)]
        picks += [(COMP + c, first_r + i) for c in range(COMP) for i in range(count_r)]
        for field, row in picks:
            buffer[at] = jnp.where(
                late, row_of(left, field, row // 2, row % 2), row_of(right, field, row // 2, row % 2)
            )
            at += 1

    rows_of(to_below, ABOVE, 0, 0, ABOVE - 1)
    rows_of(to_above, BELOW, rows - BELOW, rows - BELOW + 1, BELOW - 1)


def corners(left, right, after):
    lanes = left.shape[-1]
    shapes = (
        ((4 * ABOVE + 3 * (ABOVE - 1)), TILE, lanes),
        ((4 * BELOW + 3 * (BELOW - 1)), TILE, lanes),
    )
    return pl.pallas_call(
        corner_kernel,
        out_shape=[jax.ShapeDtypeStruct(s, jnp.float32) for s in shapes],
        in_specs=[pl.BlockSpec(memory_space=pltpu.VMEM)] * 2 + [pl.BlockSpec(memory_space=pl.ANY)],
        out_specs=[pl.BlockSpec(memory_space=pltpu.VMEM)] * 2,
        compiler_params=pltpu.CompilerParams(vmem_limit_bytes=8 << 20),
        cost_estimate=pl.CostEstimate(flops=0, bytes_accessed=1 << 20, transcendentals=0),
        name="corners",
    )(left, right, after)


def stencil_parts(weight, a, b, force, n, coef, inv):
    wide, lanes = coef.shape[-2:]
    tiles = wide // TILE

    def over(step, spans):
        for first, end in spans:
            unroll = 3 if (end - first) % 3 == 0 else 2 if (end - first) % 2 == 0 else end - first

            def body(at, _):
                step(at)
                return 0

            lax.fori_loop(first, end, body, 0, unroll=unroll)

    def part(ref, at, t, shift=0):
        return ref[(*at, pl.ds(TILE * (t + 1) + shift, TILE))]

    def put(ref, at, t, value):
        ref[(*at, pl.ds(TILE * (t + 1), TILE))] = value

    def put_round(ref, at, t, value):
        put(ref, at, t, value)
        if t == 0:
            put(ref, at, tiles, value)
        if t == tiles - 1:
            put(ref, at, -1, value)

    def ahead(x):
        return pltpu.roll(x, lanes - 1, 1)

    def behind(x):
        return pltpu.roll(x, 1, 1)

    def lay(ref, at, main):
        for t in range(tiles - 1):
            put_round(ref, at, t, main(t))

    def lay_side(ref, at, side):
        put_round(ref, at, tiles - 1, side)

    def lay_force(c, at, main):
        for t in range(tiles - 1):
            force[c, at, pl.ds(TILE * t, TILE)] = main(t)

    def lay_force_side(c, at, side):
        force[c, at, pl.ds(TILE * (tiles - 1), TILE)] = side

    def of(ref, *at):
        return lambda t: ref[(*at, pl.ds(TILE * t, TILE))]

    def total(terms):
        while len(terms) > 1:
            terms = [sum(terms[i : i + 2]) for i in range(0, len(terms), 2)]
        return terms[0]

    def coef_row(at, chosen):
        for t in chosen:
            here = part(n, (at,), t)
            sums, j = [], 0
            for group, own in zip(GROUPS, (here, behind(here), ahead(here))):
                cs = []
                for up, side, _ in group:
                    cs.append(weight[j] * (own + part(n, (at + up,), t, side)))
                    coef[j, at, pl.ds(TILE * t, TILE)] = cs[-1]
                    j += 1
                sums.append(total(cs))
            diag = (sums[0] + weight[NEAR] * here) + (ahead(sums[1]) + behind(sums[2]))
            inv[at, pl.ds(TILE * t, TILE)] = jnp.where(here > 0.0, 1.0 / diag, 0.0)

    def coefs(spans, chosen=range(tiles)):
        over(lambda at: coef_row(at, chosen), spans)

    def sweep(field, store, spans, chosen=range(tiles)):
        def step(at):
            for t in chosen:
                here = pl.ds(TILE * t, TILE)
                cs = [coef[j, at, here] for j in range(NEAR)]
                invd = inv[at, here]
                for c in range(COMP):
                    sums, j = [], 0
                    for group in GROUPS:
                        terms = []
                        for up, side, _ in group:
                            terms.append(cs[j] * part(field, (c, at + up), t, side))
                            j += 1
                        sums.append(total(terms))
                    target = (sums[0] + force[c, at, here]) + (ahead(sums[1]) + behind(sums[2]))
                    store(c, at, t, part(field, (c, at), t), target * invd)

        over(step, spans)

    def store1(c, at, t, v, target):
        put_round(b, (c, at), t, (1.0 - OMEGA) * v + OMEGA * target)

    def store2(c, at, t, v, target):
        put_round(a, (c, at), t, (1.0 - OMEGA) * v + OMEGA * target)

    def store3(c, at, t, v, target):
        b[c, at, pl.ds(TILE * (t + 1), TILE)] = target - v

    return (
        (lay, lay_side, lay_force, lay_force_side, of),
        coefs,
        functools.partial(sweep, a, store1),
        functools.partial(sweep, b, store2),
        functools.partial(sweep, a, store3),
    )


def middle_kernel(weight, u, rhs, visc, a, b, force, n, coef, inv):
    rows, cols, _ = visc.shape
    laying, coefs, sweep1, sweep2, residual = stencil_parts(weight, a, b, force, n, coef, inv)
    lay, _, lay_force, _, of = laying

    def own_step(r, _):
        at = r + BELOW
        for c in range(COMP):
            lay(a, (c, at), of(u, c, r))
            lay_force(c, at, of(rhs, c, r))
        lay(n, (at,), of(visc, r))
        return 0

    first, end, last = BELOW, BELOW + rows, cols // TILE
    lax.fori_loop(0, rows, own_step, 0)
    coefs([(first + 1, end - 1)], range(1, last - 1))
    sweep1([(first + 1, end - 1)], range(1, last - 1))
    sweep2([(first + 2, end - 2)], range(2, last - 2))
    residual([(first + 3, end - 3)], range(3, last - 3))


def inner_kernel(weight, left, right, _, *refs):
    a, b, force, n, coef, inv = refs[6:]
    rows, lanes = 2 * left.shape[1], left.shape[3]
    late = lax.broadcasted_iota(jnp.int32, (TILE, lanes), 0) >= TILE - BELOW
    laying, coefs, sweep1, sweep2, residual = stencil_parts(weight, a, b, force, n, coef, inv)
    _, lay_side, _, lay_force_side, _ = laying

    def own_step(i, _):
        for odd in range(2):
            at = 2 * i + odd + BELOW

            def side(field):
                return jnp.where(late, row_of(left, field, i, odd), row_of(right, field, i, odd))

            for c in range(COMP):
                lay_side(a, (c, at), side(c))
                lay_force_side(c, at, side(COMP + c))
            lay_side(n, (at,), side(2 * COMP))
        return 0

    first, end, last = BELOW, BELOW + rows, inv.shape[1] // TILE - 1

    def rest(edge):
        return [t for t in range(last + 1) if not edge <= t < last - edge]

    lax.fori_loop(0, rows // 2, own_step, 0)
    coefs([(first + 1, end - 1)], rest(1))
    sweep1([(first + 1, end - 1)], rest(1))
    sweep2([(first + 2, end - 2)], rest(2))
    residual([(first + 3, end - 3)], rest(3))


def outer_kernel(
    weight, above, below, above_c, below_c, *refs
):
    a, b, force, n, coef, inv = refs[6:12]
    smoothed, coarse, restr, sems = refs[12:]
    rows, cols = smoothed.shape[1:3]
    lanes = smoothed.shape[3]
    laying, coefs, sweep1, sweep2, residual = stencil_parts(weight, a, b, force, n, coef, inv)
    lay, lay_side, lay_force, lay_force_side, of = laying

    def halo(main, side, first, count, first_r, count_r):
        def step(i, _):
            for c in range(COMP):
                lay(a, (c, first + i), of(main, c * count + i))
                lay_side(a, (c, first + i), side[c * count + i])
            lay(n, (first + i,), of(main, COMP * count + i))
            lay_side(n, (first + i,), side[COMP * count + i])
            return 0

        def step_r(i, _):
            for c in range(COMP):
                j = (COMP + 1) * count + c * count_r + i
                lay_force(c, first_r + i, of(main, j))
                lay_force_side(c, first_r + i, side[j])
            return 0

        lax.fori_loop(0, count, step, 0)
        lax.fori_loop(0, count_r, step_r, 0)

    halo(above, above_c, BELOW + rows, ABOVE, BELOW + rows, ABOVE - 1)
    halo(below, below_c, 0, BELOW, 1, BELOW - 1)

    first, end = BELOW, BELOW + rows
    coefs(((first - 2, first + 1), (end - 1, end + 3)))
    sweep1(((first - 2, first + 1), (end - 1, end + 3)))
    sweep2(((first - 1, first + 2), (end - 2, end + 2)))
    copies = [
        pltpu.make_async_copy(a.at[c, pl.ds(first, rows), pl.ds(TILE, cols)], smoothed.at[c], sems.at[c])
        for c in range(COMP)
    ]
    for each in copies:
        each.start()
    residual(((first, first + 3), (end - 3, end + 1)))

    for c in range(COMP):
        for i in range(rows // 2):
            at = BELOW + 2 * i
            restr[c * (rows // 2) + i] = 0.25 * (b[c, at, TILE:] + b[c, at + 2, TILE:]) + 0.5 * b[c, at + 1, TILE:]
    parts = []
    for i in range(COMP * (rows // 2)):
        p = restr[i, pl.ds(0, cols // 2, stride=2)]
        q = restr[i, pl.ds(1, cols // 2, stride=2)]
        d = restr[i, pl.ds(2, cols // 2, stride=2)]
        parts.append(0.25 * (p + d) + 0.5 * q)
    source = lax.broadcasted_iota(jnp.int32, (lanes, lanes // 2), 0)
    target = 2 * lax.broadcasted_iota(jnp.int32, (lanes, lanes // 2), 1)
    gap = source - target
    h = jnp.where(gap == 1, 0.5, jnp.where((gap == 0) | (gap == 2), 0.25, 0.0))
    for c in range(COMP):
        block = jnp.concatenate(parts[c * (rows // 2) : (c + 1) * (rows // 2)], 0)
        out = jnp.dot(block, h, precision=lax.Precision.HIGHEST, preferred_element_type=jnp.float32)
        coarse[c] = out.reshape(rows // 2, cols // 2, lanes // 2)
    for each in copies:
        each.wait()


def state_shapes(rows, cols, lanes):
    deep, wide = rows + BELOW + ABOVE, cols + TILE
    padded = wide + 2 * TILE
    shapes = (
        (COMP, deep, padded, lanes),
        (COMP, deep, padded, lanes),
        (COMP, deep, wide, lanes),
        (deep, padded, lanes),
        (14, deep, wide, lanes),
        (deep, wide, lanes),
    )
    return [jax.ShapeDtypeStruct(s, jnp.float32) for s in shapes]


def middle(weight, u, rhs, visc):
    vmem = pl.BlockSpec(memory_space=pltpu.VMEM)
    return pl.pallas_call(
        middle_kernel,
        out_shape=state_shapes(*visc.shape),
        in_specs=[vmem] * 4,
        out_specs=[vmem] * 6,
        compiler_params=pltpu.CompilerParams(vmem_limit_bytes=16 << 20),
        cost_estimate=pl.CostEstimate(flops=10_000_000, bytes_accessed=8 << 20, transcendentals=0),
        name="middle",
    )(weight, u, rhs, visc)


def inner(weight, left, right, after, state):
    vmem = pl.BlockSpec(memory_space=pltpu.VMEM)
    return pl.pallas_call(
        inner_kernel,
        out_shape=[jax.ShapeDtypeStruct(x.shape, x.dtype) for x in state],
        in_specs=[vmem] * 3 + [pl.BlockSpec(memory_space=pl.ANY)] + [vmem] * 6,
        out_specs=[vmem] * 6,
        input_output_aliases={4 + i: i for i in range(6)},
        compiler_params=pltpu.CompilerParams(vmem_limit_bytes=16 << 20),
        cost_estimate=pl.CostEstimate(flops=10_000_000, bytes_accessed=8 << 20, transcendentals=0),
        name="inner",
    )(weight, left, right, after, *state)


def outer(weight, above, below, above_c, below_c, state, rows, cols, lanes):
    vmem = pl.BlockSpec(memory_space=pltpu.VMEM)
    f32 = jnp.float32
    shapes = state_shapes(rows, cols, lanes)
    out = pl.pallas_call(
        outer_kernel,
        out_shape=shapes
        + [
            jax.ShapeDtypeStruct((COMP, rows, cols, lanes), f32),
            jax.ShapeDtypeStruct((COMP, rows // 2, cols // 2, lanes // 2), f32),
        ],
        in_specs=[vmem] * 11,
        out_specs=[vmem] * 6 + [pl.BlockSpec(memory_space=pltpu.HBM), vmem],
        input_output_aliases={5 + i: i for i in range(6)},
        scratch_shapes=[
            pltpu.VMEM((COMP * (rows // 2), cols + 2 * TILE, lanes), f32),
            pltpu.SemaphoreType.DMA((COMP,)),
        ],
        compiler_params=pltpu.CompilerParams(vmem_limit_bytes=16 << 20),
        cost_estimate=pl.CostEstimate(flops=40_000_000, bytes_accessed=16 << 20, transcendentals=0),
        name="outer",
    )(weight, above, below, above_c, below_c, *state)
    return out[6], out[7]


def sent(value, axis, steps):
    count = lax.axis_size(axis)
    pairs = [(i, i + steps) for i in range(count) if 0 <= i + steps < count]
    return lax.ppermute(value, axis, pairs)


def per_device(solution, right_side, viscosity, stencil_weights):
    to_left, to_right, to_below, to_above, own_visc, weight = pack(stencil_weights, solution, right_side, viscosity)
    above = sent(to_below, "shell", -1)
    below = sent(to_above, "shell", 1)
    left = sent(to_right, "lat", 1)
    right = sent(to_left, "lat", -1)
    state = middle(weight, solution, right_side, own_visc)
    to_below_c, to_above_c = corners(left, right, state[-1])
    above_c = sent(to_below_c, "shell", -1)
    below_c = sent(to_above_c, "shell", 1)
    state = inner(weight, left, right, to_below_c, state)
    return outer(weight, above, below, above_c, below_c, state, *viscosity.shape)


def solution(mesh):
    in_specs = (
        P(None, "shell", "lat", None),
        P(None, "shell", "lat", None),
        P("shell", "lat", None),
        P(),
    )
    out_specs = (P(None, "shell", "lat", None), P(None, "shell", "lat", None))
    return jax.shard_map(
        per_device, mesh=mesh, in_specs=in_specs, out_specs=out_specs, check_vma=False
    )
```

time: 40.3 us -> 39.5 us (0.980)
  the two profiles are of different devices: /device:TPU:30 before, /device:TPU:38 now
where the time goes in v4:
time: 39.5 us; the launch traced here: 39.3 us
  starting transfers between devices  23.7 us (60%)
  Pallas kernels  10.4 us (26%)
  waiting for transfers between devices  4.46 us (11%)
  between operations  0.74 us (2%)
    ppermute x6, starting transfers between devices, sent(): return lax.ppermute(value, axis, pairs)  23.7 us
    pallas_call x1, Pallas kernels, outer(): pl.pallas_call(outer_kernel, out_shape=shapes + [jax.ShapeDtypeStruct((CO...  5.38 us
    ppermute x6, waiting for transfers between devices, sent(): return lax.ppermute(value, axis, pairs)  4.46 us
    pallas_call x1, Pallas kernels, pack(): pl.pallas_call(pack_kernel, out_shape=[jax.ShapeDtypeStruct(s, jnp.float3...  1.94 us
    pallas_call x1, Pallas kernels, middle(): pl.pallas_call(middle_kernel, out_shape=state_shapes(*visc.shape), in_spe...  1.66 us
    pallas_call x1, Pallas kernels, inner(): pl.pallas_call(inner_kernel, out_shape=[jax.ShapeDtypeStruct(x.shape, x.d...  1.37 us
  transfers between devices with their start and end apart: 6, of which 2 were waited for; matrix products, arithmetic and copies ran while one was open for 0% of the time, Pallas kernels for 8%

profile of v4, /device:TPU:38, one launch (start us, length us, event | category | flops | bytes accessed | tf_op | source)
XLA Modules:
  0.0 39.3 jit_solution(17841886464250665934)
XLA Ops:
  0.6 0.0 copy-start.1
  0.6 0.0 copy-start
  0.7 1.9 %pack.1 = (f32[7,4,8,128]{3,2,1,0:T(8,128)S(1)}, f32[7,4,8,128]{3,2,1,0:T(8,128)S(1)}, f32[25,64,128]{2,1,0:T(8,128)S(1)}, f32[18,64,128]{2,1,0:T(8,128)S(1)}, f...) custom-call(f32[7]{0:T(128)} %wts.1, f32[3,8,64,128]{3,2,1,0:T(8,128)} %u.3, f32[3,8,64,128]{3,2,1,0:T(8,128)} %rhs.3, ...), custom_call_target="tpu_custom_call" | custom-call | bytes 4194304 | tf_op jit(solution)/shard_map/pack/pallas_call | solution.py:88
  2.6 2.4 %collective-permute-start = (f32[25,64,128]{2,1,0:T(8,128)S(1)}, f32[25,64,128]{2,1,0:T(8,128)S(1)}, u32[]{:S(2)}, u32[]{:S(2)}) collective-permute-start(f32[25,64,128]{2,1,0:T(8,128)S(1)} %get-tuple-element.25), channel_id=1, source_target_pairs={{64,0},{128,64},{192,128},{256,192},{320,256},{384,320},{448,384},... | collective-permute-start | bytes 2457608 | tf_op jit(solution)/shard_map/ppermute | solution.py:434
  5.0 3.5 %collective-permute-start.1 = (f32[18,64,128]{2,1,0:T(8,128)S(1)}, f32[18,64,128]{2,1,0:T(8,128)S(1)}, u32[]{:S(2)}, u32[]{:S(2)}) collective-permute-start(f32[18,64,128]{2,1,0:T(8,128)S(1)} %get-tuple-element.26), channel_id=1, source_target_pairs={{0,64},{64,128},{128,192},{192,256},{256,320},{320,384},{384,448},... | collective-permute-start | bytes 1769480 | tf_op jit(solution)/shard_map/ppermute | solution.py:434
  8.5 1.9 %collective-permute-start.2 = (f32[7,4,8,128]{3,2,1,0:T(8,128)S(1)}, f32[7,4,8,128]{3,2,1,0:T(8,128)S(1)}, u32[]{:S(2)}, u32[]{:S(2)}) collective-permute-start(f32[7,4,8,128]{3,2,1,0:T(8,128)S(1)} %get-tuple-element.27), channel_id=1, source_target_pairs={{0,1},{1,2},{2,3},{3,4},{4,5},{5,6},{6,7},{7,8},{8,9},{9,10},{10,1... | collective-permute-start | bytes 344072 | tf_op jit(solution)/shard_map/ppermute | solution.py:434
  10.4 10.1 %collective-permute-start.3 = (f32[7,4,8,128]{3,2,1,0:T(8,128)S(1)}, f32[7,4,8,128]{3,2,1,0:T(8,128)S(1)}, u32[]{:S(2)}, u32[]{:S(2)}) collective-permute-start(f32[7,4,8,128]{3,2,1,0:T(8,128)S(1)} %get-tuple-element.28), channel_id=1, source_target_pairs={{1,0},{2,1},{3,2},{4,3},{5,4},{6,5},{7,6},{8,7},{9,8},{10,9},{11,1... | collective-permute-start | bytes 344072 | tf_op jit(solution)/shard_map/ppermute | solution.py:434
  20.5 0.0 copy-done.1
  20.5 0.0 copy-done
  20.5 1.7 %middle.1 = (f32[3,15,88,128]{3,2,1,0:T(8,128)S(1)}, f32[3,15,88,128]{3,2,1,0:T(8,128)S(1)}, f32[3,15,72,128]{3,2,1,0:T(8,128)S(1)}, f32[15,88,128]{2,1,0:T(8,12...) custom-call(f32[15,8,128]{2,1,0:T(8,128)S(1)} %get-tuple-element.24.weight, ...), custom_call_target="tpu_custom_call" | custom-call | flops 10000000 | bytes 8388608 | tf_op jit(solution)/shard_map/middle/pallas_call | solution.py:381
  22.2 0.0 collective-permute-done.2.left
  22.2 0.7 %collective-permute-done.3.right = f32[7,4,8,128]{3,2,1,0:T(8,128)S(1)} collective-permute-done((f32[7,4,8,128]{3,2,1,0:T(8,128)S(1)}, f32[7,4,8,128]{3,2,1,0:T(8,128)S(1)}, u32[]{:S(2)}, u32[]{:S(2)}) %collective-permute-start.3) | collective-permute-done | bytes 114720 | tf_op jit(solution)/shard_map/ppermute | solution.py:434
  22.9 3.6 %collective-permute-start.4 = (f32[25,8,128]{2,1,0:T(8,128)S(1)}, f32[25,8,128]{2,1,0:T(8,128)S(1)}, u32[]{:S(2)}, u32[]{:S(2)}) collective-permute-start(f32[25,8,128]{2,1,0:T(8,128)S(1)} %get-tuple-element.31._), channel_id=1, source_target_pairs={{64,0},{128,64},{192,128},{256,192},{320,256},{384,320},{448,384},... | collective-permute-start | bytes 307208 | tf_op jit(solution)/shard_map/ppermute | solution.py:434
  26.4 2.3 %collective-permute-start.5 = (f32[18,8,128]{2,1,0:T(8,128)S(1)}, f32[18,8,128]{2,1,0:T(8,128)S(1)}, u32[]{:S(2)}, u32[]{:S(2)}) collective-permute-start(f32[18,8,128]{2,1,0:T(8,128)S(1)} %get-tuple-element.32), channel_id=1, source_target_pairs={{0,64},{64,128},{128,192},{192,256},{256,320},{320,384},{384,448},... | collective-permute-start | bytes 221192 | tf_op jit(solution)/shard_map/ppermute | solution.py:434
  28.7 1.4 %inner.1 = (f32[3,15,88,128]{3,2,1,0:T(8,128)S(1)}, f32[3,15,88,128]{3,2,1,0:T(8,128)S(1)}, f32[3,15,72,128]{3,2,1,0:T(8,128)S(1)}, f32[15,88,128]{2,1,0:T(8,128...) custom-call(f32[15,8,128]{2,1,0:T(8,128)S(1)} %get-tuple-element.24., ...), custom_call_target="tpu_custom_call", output_to_operand_aliasing={{0}: (4, {}), {1}: (5, {}), {2}: (6, {}), {3}: (7, {}), {4}... | custom-call | flops 10000000 | bytes 8388608 | tf_op jit(solution)/shard_map/inner/pallas_call | solution.py:394
  30.1 3.8 %collective-permute-done.5.below_c = f32[18,8,128]{2,1,0:T(8,128)S(1)} collective-permute-done((f32[18,8,128]{2,1,0:T(8,128)S(1)}, f32[18,8,128]{2,1,0:T(8,128)S(1)}, u32[]{:S(2)}, u32[]{:S(2)}) %collective-permute-start.5) | collective-permute-done | bytes 73760 | tf_op jit(solution)/shard_map/ppermute | solution.py:434
  33.9 0.0 collective-permute-done.4.above_c
  33.9 0.0 collective-permute-done.1.below
  33.9 0.0 collective-permute-done.above
  33.9 5.4 %outer.1 = (f32[3,15,88,128]{3,2,1,0:T(8,128)S(1)}, f32[3,15,88,128]{3,2,1,0:T(8,128)S(1)}, f32[3,15,72,128]{3,2,1,0:T(8,128)S(1)}, f32[15,88,128]{2,1,0:T(8,128...) custom-call(f32[15,8,128]{2,1,0:T(8,128)S(1)} %get-tuple-element.24., ...), custom_call_target="tpu_custom_call", output_to_operand_aliasing={{0}: (5, {}), {1}: (6, {}), {2}: (7, {}), {3}: (8, {}), {4}... | custom-call | flops 40000000 | bytes 16777216 | tf_op jit(solution)/shard_map/outer/pallas_call | solution.py:410
  (1 shorter events, 0.0 us)
Async XLA Ops:
  0.6 19.9 %copy-start.1 = (f32[3,8,64,128]{3,2,1,0:T(8,128)S(1)}, f32[3,8,64,128]{3,2,1,0:T(8,128)}, u32[]{:S(2)}) copy-start(f32[3,8,64,128]{3,2,1,0:T(8,128)} %rhs.3) | copy-start | bytes 2359300
  0.6 19.9 %copy-start = (f32[3,8,64,128]{3,2,1,0:T(8,128)S(1)}, f32[3,8,64,128]{3,2,1,0:T(8,128)}, u32[]{:S(2)}) copy-start(f32[3,8,64,128]{3,2,1,0:T(8,128)} %u.3) | copy-start | bytes 2359300
  2.6 31.3 %collective-permute-start = (f32[25,64,128]{2,1,0:T(8,128)S(1)}, f32[25,64,128]{2,1,0:T(8,128)S(1)}, u32[]{:S(2)}, u32[]{:S(2)}) collective-permute-start(f32[25,64,128]{2,1,0:T(8,128)S(1)} %get-tuple-element.25), channel_id=1, source_target_pairs={{64,0},{128,64},{192,128},{256,192},{320,256},{384,320},{448,384},... | collective-permute-start | bytes 2457608 | tf_op jit(solution)/shard_map/ppermute | solution.py:434
  5.0 28.9 %collective-permute-start.1 = (f32[18,64,128]{2,1,0:T(8,128)S(1)}, f32[18,64,128]{2,1,0:T(8,128)S(1)}, u32[]{:S(2)}, u32[]{:S(2)}) collective-permute-start(f32[18,64,128]{2,1,0:T(8,128)S(1)} %get-tuple-element.26), channel_id=1, source_target_pairs={{0,64},{64,128},{128,192},{192,256},{256,320},{320,384},{384,448},... | collective-permute-start | bytes 1769480 | tf_op jit(solution)/shard_map/ppermute | solution.py:434
  8.5 13.7 %collective-permute-start.2 = (f32[7,4,8,128]{3,2,1,0:T(8,128)S(1)}, f32[7,4,8,128]{3,2,1,0:T(8,128)S(1)}, u32[]{:S(2)}, u32[]{:S(2)}) collective-permute-start(f32[7,4,8,128]{3,2,1,0:T(8,128)S(1)} %get-tuple-element.27), channel_id=1, source_target_pairs={{0,1},{1,2},{2,3},{3,4},{4,5},{5,6},{6,7},{7,8},{8,9},{9,10},{10,1... | collective-permute-start | bytes 344072 | tf_op jit(solution)/shard_map/ppermute | solution.py:434
  10.4 12.4 %collective-permute-start.3 = (f32[7,4,8,128]{3,2,1,0:T(8,128)S(1)}, f32[7,4,8,128]{3,2,1,0:T(8,128)S(1)}, u32[]{:S(2)}, u32[]{:S(2)}) collective-permute-start(f32[7,4,8,128]{3,2,1,0:T(8,128)S(1)} %get-tuple-element.28), channel_id=1, source_target_pairs={{1,0},{2,1},{3,2},{4,3},{5,4},{6,5},{7,6},{8,7},{9,8},{10,9},{11,1... | collective-permute-start | bytes 344072 | tf_op jit(solution)/shard_map/ppermute | solution.py:434
  22.9 11.0 %collective-permute-start.4 = (f32[25,8,128]{2,1,0:T(8,128)S(1)}, f32[25,8,128]{2,1,0:T(8,128)S(1)}, u32[]{:S(2)}, u32[]{:S(2)}) collective-permute-start(f32[25,8,128]{2,1,0:T(8,128)S(1)} %get-tuple-element.31._), channel_id=1, source_target_pairs={{64,0},{128,64},{192,128},{256,192},{320,256},{384,320},{448,384},... | collective-permute-start | bytes 307208 | tf_op jit(solution)/shard_map/ppermute | solution.py:434
  26.4 7.5 %collective-permute-start.5 = (f32[18,8,128]{2,1,0:T(8,128)S(1)}, f32[18,8,128]{2,1,0:T(8,128)S(1)}, u32[]{:S(2)}, u32[]{:S(2)}) collective-permute-start(f32[18,8,128]{2,1,0:T(8,128)S(1)} %get-tuple-element.32), channel_id=1, source_target_pairs={{0,64},{64,128},{128,192},{192,256},{256,320},{320,384},{384,448},... | collective-permute-start | bytes 221192 | tf_op jit(solution)/shard_map/ppermute | solution.py:434

commit v5 on v4

--- a/solution.py
+++ b/solution.py
@@ -286,59 +286,75 @@
 
     first, end, last = BELOW, BELOW + rows, inv.shape[1] // TILE - 1
 
-    def rest(edge):
-        return [t for t in range(last + 1) if not edge <= t < last - edge]
-
     lax.fori_loop(0, rows // 2, own_step, 0)
-    coefs([(first + 1, end - 1)], rest(1))
-    sweep1([(first + 1, end - 1)], rest(1))
-    sweep2([(first + 2, end - 2)], rest(2))
-    residual([(first + 3, end - 3)], rest(3))
-
-
-def outer_kernel(
-    weight, above, below, above_c, below_c, *refs
-):
+    coefs([(first + 1, end - 1)], rest(last, 1))
+    sweep1([(first + 1, end - 1)], rest(last, 1))
+    sweep2([(first + 2, end - 2)], rest(last, 2))
+    residual([(first + 3, end - 3)], rest(last, 3))
+
+
+def rest(last, edge):
+    return [t for t in range(last + 1) if not edge <= t < last - edge]
+
+
+def halo_rows(rows):
+    return ((ABOVE, BELOW + rows, BELOW + rows), (BELOW, 0, 1))
+
+
+def outer_middle_kernel(weight, above, below, *refs):
+    a, b, force, n, coef, inv = refs[6:]
+    rows, cols = a.shape[1] - BELOW - ABOVE, above.shape[1]
+    laying, coefs, sweep1, sweep2, residual = stencil_parts(weight, a, b, force, n, coef, inv)
+    lay, _, lay_force, _, of = laying
+    for main, (count, at, at_r) in zip((above, below), halo_rows(rows)):
+
+        def step(i, _):
+            for c in range(COMP):
+                lay(a, (c, at + i), of(main, c * count + i))
+            lay(n, (at + i,), of(main, COMP * count + i))
+            return 0
+
+        def step_r(i, _):
+            for c in range(COMP):
+                lay_force(c, at_r + i, of(main, (COMP + 1) * count + c * (count - 1) + i))
+            return 0
+
+        lax.fori_loop(0, count, step, 0)
+        lax.fori_loop(0, count - 1, step_r, 0)
+
+    first, end, last = BELOW, BELOW + rows, cols // TILE
+    coefs([(first - 2, first + 1), (end - 1, end + 3)], range(1, last - 1))
+    sweep1([(first - 2, first + 1), (end - 1, end + 3)], range(1, last - 1))
+    sweep2([(first - 1, first + 2), (end - 2, end + 2)], range(2, last - 2))
+    residual([(first, first + 3), (end - 3, end + 1)], range(3, last - 3))
+
+
+def outer_kernel(weight, above_c, below_c, *refs):
     a, b, force, n, coef, inv = refs[6:12]
     smoothed, coarse, restr, sems = refs[12:]
-    rows, cols = smoothed.shape[1:3]
-    lanes = smoothed.shape[3]
+    rows, cols, lanes = smoothed.shape[1:]
     laying, coefs, sweep1, sweep2, residual = stencil_parts(weight, a, b, force, n, coef, inv)
-    lay, lay_side, lay_force, lay_force_side, of = laying
-
-    def halo(main, side, first, count, first_r, count_r):
-        def step(i, _):
+    _, lay_side, _, lay_force_side, _ = laying
+    for side, (count, at, at_r) in zip((above_c, below_c), halo_rows(rows)):
+        for i in range(count):
             for c in range(COMP):
-                lay(a, (c, first + i), of(main, c * count + i))
-                lay_side(a, (c, first + i), side[c * count + i])
-            lay(n, (first + i,), of(main, COMP * count + i))
-            lay_side(n, (first + i,), side[COMP * count + i])
-            return 0
-
-        def step_r(i, _):
+                lay_side(a, (c, at + i), side[c * count + i])
+            lay_side(n, (at + i,), side[COMP * count + i])
+        for i in range(count - 1):
             for c in range(COMP):
-                j = (COMP + 1) * count + c * count_r + i
-                lay_force(c, first_r + i, of(main, j))
-                lay_force_side(c, first_r + i, side[j])
-            return 0
-
-        lax.fori_loop(0, count, step, 0)
-        lax.fori_loop(0, count_r, step_r, 0)
-
-    halo(above, above_c, BELOW + rows, ABOVE, BELOW + rows, ABOVE - 1)
-    halo(below, below_c, 0, BELOW, 1, BELOW - 1)
-
-    first, end = BELOW, BELOW + rows
-    coefs(((first - 2, first + 1), (end - 1, end + 3)))
-    sweep1(((first - 2, first + 1), (end - 1, end + 3)))
-    sweep2(((first - 1, first + 2), (end - 2, end + 2)))
+                lay_force_side(c, at_r + i, side[(COMP + 1) * count + c * (count - 1) + i])
+
+    first, end, last = BELOW, BELOW + rows, cols // TILE
+    coefs([(first - 2, first + 1), (end - 1, end + 3)], rest(last, 1))
+    sweep1([(first - 2, first + 1), (end - 1, end + 3)], rest(last, 1))
+    sweep2([(first - 1, first + 2), (end - 2, end + 2)], rest(last, 2))
     copies = [
         pltpu.make_async_copy(a.at[c, pl.ds(first, rows), pl.ds(TILE, cols)], smoothed.at[c], sems.at[c])
         for c in range(COMP)
     ]
     for each in copies:
         each.start()
-    residual(((first, first + 3), (end - 3, end + 1)))
+    residual([(first, first + 3), (end - 3, end + 1)], rest(last, 3))
 
     for c in range(COMP):
         for i in range(rows // 2):
@@ -403,7 +419,21 @@
     )(weight, left, right, after, *state)
 
 
-def outer(weight, above, below, above_c, below_c, state, rows, cols, lanes):
+def outer_middle(weight, above, below, state):
+    vmem = pl.BlockSpec(memory_space=pltpu.VMEM)
+    return pl.pallas_call(
+        outer_middle_kernel,
+        out_shape=[jax.ShapeDtypeStruct(x.shape, x.dtype) for x in state],
+        in_specs=[vmem] * 9,
+        out_specs=[vmem] * 6,
+        input_output_aliases={3 + i: i for i in range(6)},
+        compiler_params=pltpu.CompilerParams(vmem_limit_bytes=16 << 20),
+        cost_estimate=pl.CostEstimate(flops=10_000_000, bytes_accessed=8 << 20, transcendentals=0),
+        name="outer_middle",
+    )(weight, above, below, *state)
+
+
+def outer(weight, above_c, below_c, state, rows, cols, lanes):
     vmem = pl.BlockSpec(memory_space=pltpu.VMEM)
     f32 = jnp.float32
     shapes = state_shapes(rows, cols, lanes)
@@ -414,17 +444,17 @@
             jax.ShapeDtypeStruct((COMP, rows, cols, lanes), f32),
             jax.ShapeDtypeStruct((COMP, rows // 2, cols // 2, lanes // 2), f32),
         ],
-        in_specs=[vmem] * 11,
+        in_specs=[vmem] * 9,
         out_specs=[vmem] * 6 + [pl.BlockSpec(memory_space=pltpu.HBM), vmem],
-        input_output_aliases={5 + i: i for i in range(6)},
+        input_output_aliases={3 + i: i for i in range(6)},
         scratch_shapes=[
             pltpu.VMEM((COMP * (rows // 2), cols + 2 * TILE, lanes), f32),
             pltpu.SemaphoreType.DMA((COMP,)),
         ],
         compiler_params=pltpu.CompilerParams(vmem_limit_bytes=16 << 20),
-        cost_estimate=pl.CostEstimate(flops=40_000_000, bytes_accessed=16 << 20, transcendentals=0),
+        cost_estimate=pl.CostEstimate(flops=20_000_000, bytes_accessed=16 << 20, transcendentals=0),
         name="outer",
-    )(weight, above, below, above_c, below_c, *state)
+    )(weight, above_c, below_c, *state)
     return out[6], out[7]
 
 
@@ -445,7 +475,8 @@
     above_c = sent(to_below_c, "shell", -1)
     below_c = sent(to_above_c, "shell", 1)
     state = inner(weight, left, right, to_below_c, state)
-    return outer(weight, above, below, above_c, below_c, state, *viscosity.shape)
+    state = outer_middle(weight, above, below, state)
+    return outer(weight, above_c, below_c, state, *viscosity.shape)
 
 
 def solution(mesh):

time: 39.5 us -> 38.9 us (0.985)
  the two profiles are of different devices: /device:TPU:38 before, /device:TPU:30 now
where the time goes in v5:
time: 38.9 us; the launch traced here: 38.7 us
  starting transfers between devices  26.1 us (67%)
  Pallas kernels  11.1 us (29%)
  between operations  0.78 us (2%)
  waiting for transfers between devices  0.67 us (2%)
    ppermute x6, starting transfers between devices, sent(): return lax.ppermute(value, axis, pairs)  26.1 us
    pallas_call x1, Pallas kernels, outer(): pl.pallas_call(outer_kernel, out_shape=shapes + [jax.ShapeDtypeStruct((CO...  3.66 us
    pallas_call x1, Pallas kernels, outer_middle(): pl.pallas_call(outer_middle_kernel, out_shape=[jax.ShapeDtypeStruct(x.sha...  2.44 us
    pallas_call x1, Pallas kernels, pack(): pl.pallas_call(pack_kernel, out_shape=[jax.ShapeDtypeStruct(s, jnp.float3...  1.94 us
    pallas_call x1, Pallas kernels, middle(): pl.pallas_call(middle_kernel, out_shape=state_shapes(*visc.shape), in_spe...  1.66 us
    pallas_call x1, Pallas kernels, inner(): pl.pallas_call(inner_kernel, out_shape=[jax.ShapeDtypeStruct(x.shape, x.d...  1.37 us
  transfers between devices with their start and end apart: 6, of which 1 were waited for; matrix products, arithmetic and copies ran while one was open for 0% of the time, Pallas kernels for 14%

profile of v5, /device:TPU:30, one launch (start us, length us, event | category | flops | bytes accessed | tf_op | source)
XLA Modules:
  0.0 38.7 jit_solution(14713073781990917092)
XLA Ops:
  0.6 0.0 copy-start.1
  0.6 0.0 copy-start
  0.7 1.9 %pack.1 = (f32[7,4,8,128]{3,2,1,0:T(8,128)S(1)}, f32[7,4,8,128]{3,2,1,0:T(8,128)S(1)}, f32[25,64,128]{2,1,0:T(8,128)S(1)}, f32[18,64,128]{2,1,0:T(8,128)S(1)}, f...) custom-call(f32[7]{0:T(128)} %wts.1, f32[3,8,64,128]{3,2,1,0:T(8,128)} %u.3, f32[3,8,64,128]{3,2,1,0:T(8,128)} %rhs.3, ...), custom_call_target="tpu_custom_call" | custom-call | bytes 4194304 | tf_op jit(solution)/shard_map/pack/pallas_call | solution.py:88
  2.6 2.4 %collective-permute-start.4 = (f32[25,64,128]{2,1,0:T(8,128)S(1)}, f32[25,64,128]{2,1,0:T(8,128)S(1)}, u32[]{:S(2)}, u32[]{:S(2)}) collective-permute-start(f32[25,64,128]{2,1,0:T(8,128)S(1)} %get-tuple-element.37), channel_id=1, source_target_pairs={{64,0},{128,64},{192,128},{256,192},{320,256},{384,320},{448,384},... | collective-permute-start | bytes 2457608 | tf_op jit(solution)/shard_map/ppermute | solution.py:464
  5.0 4.7 %collective-permute-start.5 = (f32[18,64,128]{2,1,0:T(8,128)S(1)}, f32[18,64,128]{2,1,0:T(8,128)S(1)}, u32[]{:S(2)}, u32[]{:S(2)}) collective-permute-start(f32[18,64,128]{2,1,0:T(8,128)S(1)} %get-tuple-element.38), channel_id=1, source_target_pairs={{0,64},{64,128},{128,192},{192,256},{256,320},{320,384},{384,448},... | collective-permute-start | bytes 1769480 | tf_op jit(solution)/shard_map/ppermute | solution.py:464
  9.7 1.9 %collective-permute-start = (f32[7,4,8,128]{3,2,1,0:T(8,128)S(1)}, f32[7,4,8,128]{3,2,1,0:T(8,128)S(1)}, u32[]{:S(2)}, u32[]{:S(2)}) collective-permute-start(f32[7,4,8,128]{3,2,1,0:T(8,128)S(1)} %get-tuple-element.31), channel_id=1, source_target_pairs={{0,1},{1,2},{2,3},{3,4},{4,5},{5,6},{6,7},{7,8},{8,9},{9,10},{10,1... | collective-permute-start | bytes 344072 | tf_op jit(solution)/shard_map/ppermute | solution.py:464
  11.6 10.1 %collective-permute-start.1 = (f32[7,4,8,128]{3,2,1,0:T(8,128)S(1)}, f32[7,4,8,128]{3,2,1,0:T(8,128)S(1)}, u32[]{:S(2)}, u32[]{:S(2)}) collective-permute-start(f32[7,4,8,128]{3,2,1,0:T(8,128)S(1)} %get-tuple-element.32), channel_id=1, source_target_pairs={{1,0},{2,1},{3,2},{4,3},{5,4},{6,5},{7,6},{8,7},{9,8},{10,9},{11,1... | collective-permute-start | bytes 344072 | tf_op jit(solution)/shard_map/ppermute | solution.py:464
  21.7 0.0 copy-done.1
  21.7 0.0 copy-done
  21.7 1.7 %middle.1 = (f32[3,15,88,128]{3,2,1,0:T(8,128)S(1)}, f32[3,15,88,128]{3,2,1,0:T(8,128)S(1)}, f32[3,15,72,128]{3,2,1,0:T(8,128)S(1)}, f32[15,88,128]{2,1,0:T(8,12...) custom-call(f32[15,8,128]{2,1,0:T(8,128)S(1)} %get-tuple-element.30.weight, ...), custom_call_target="tpu_custom_call" | custom-call | flops 10000000 | bytes 8388608 | tf_op jit(solution)/shard_map/middle/pallas_call | solution.py:397
  23.4 0.0 collective-permute-done.left
  23.4 0.7 %collective-permute-done.1.right = f32[7,4,8,128]{3,2,1,0:T(8,128)S(1)} collective-permute-done((f32[7,4,8,128]{3,2,1,0:T(8,128)S(1)}, f32[7,4,8,128]{3,2,1,0:T(8,128)S(1)}, u32[]{:S(2)}, u32[]{:S(2)}) %collective-permute-start.1) | collective-permute-done | bytes 114720 | tf_op jit(solution)/shard_map/ppermute | solution.py:464
  24.1 1.9 %collective-permute-start.2 = (f32[25,8,128]{2,1,0:T(8,128)S(1)}, f32[25,8,128]{2,1,0:T(8,128)S(1)}, u32[]{:S(2)}, u32[]{:S(2)}) collective-permute-start(f32[25,8,128]{2,1,0:T(8,128)S(1)} %get-tuple-element.35._), channel_id=1, source_target_pairs={{64,0},{128,64},{192,128},{256,192},{320,256},{384,320},{448,384},... | collective-permute-start | bytes 307208 | tf_op jit(solution)/shard_map/ppermute | solution.py:464
  26.0 5.1 %collective-permute-start.3 = (f32[18,8,128]{2,1,0:T(8,128)S(1)}, f32[18,8,128]{2,1,0:T(8,128)S(1)}, u32[]{:S(2)}, u32[]{:S(2)}) collective-permute-start(f32[18,8,128]{2,1,0:T(8,128)S(1)} %get-tuple-element.36), channel_id=1, source_target_pairs={{0,64},{64,128},{128,192},{192,256},{256,320},{320,384},{384,448},... | collective-permute-start | bytes 221192 | tf_op jit(solution)/shard_map/ppermute | solution.py:464
  31.1 1.4 %inner.1 = (f32[3,15,88,128]{3,2,1,0:T(8,128)S(1)}, f32[3,15,88,128]{3,2,1,0:T(8,128)S(1)}, f32[3,15,72,128]{3,2,1,0:T(8,128)S(1)}, f32[15,88,128]{2,1,0:T(8,128...) custom-call(f32[15,8,128]{2,1,0:T(8,128)S(1)} %get-tuple-element.30., ...), custom_call_target="tpu_custom_call", output_to_operand_aliasing={{0}: (4, {}), {1}: (5, {}), {2}: (6, {}), {3}: (7, {}), {4}... | custom-call | flops 10000000 | bytes 8388608 | tf_op jit(solution)/shard_map/inner/pallas_call | solution.py:410
  32.5 0.0 collective-permute-done.5.below
  32.5 0.0 collective-permute-done.4.above
  32.5 2.4 %outer_middle.1 = (f32[3,15,88,128]{3,2,1,0:T(8,128)S(1)}, f32[3,15,88,128]{3,2,1,0:T(8,128)S(1)}, f32[3,15,72,128]{3,2,1,0:T(8,128)S(1)}, f32[15,88,128]{2,1,0:...) custom-call(f32[15,8,128]{2,1,0:T(8,128)S(1)} %get-tuple-element.30., ...), custom_call_target="tpu_custom_call", output_to_operand_aliasing={{0}: (3, {}), {1}: (4, {}), {2}: (5, {}), {3}: (6, {}), {4}... | custom-call | flops 10000000 | bytes 8388608 | tf_op jit(solution)/shard_map/outer_middle/pallas_call | solution.py:424
  35.0 0.0 collective-permute-done.3.below_c
  35.0 0.0 collective-permute-done.2.above_c
  35.0 3.7 %outer.1 = (f32[3,15,88,128]{3,2,1,0:T(8,128)S(1)}, f32[3,15,88,128]{3,2,1,0:T(8,128)S(1)}, f32[3,15,72,128]{3,2,1,0:T(8,128)S(1)}, f32[15,88,128]{2,1,0:T(8,128...) custom-call(f32[15,8,128]{2,1,0:T(8,128)S(1)} %get-tuple-element.30., ...), custom_call_target="tpu_custom_call", output_to_operand_aliasing={{0}: (3, {}), {1}: (4, {}), {2}: (5, {}), {3}: (6, {}), {4}... | custom-call | flops 20000000 | bytes 16777216 | tf_op jit(solution)/shard_map/outer/pallas_call | solution.py:440
  (1 shorter events, 0.0 us)
Async XLA Ops:
  0.6 21.1 %copy-start.1 = (f32[3,8,64,128]{3,2,1,0:T(8,128)S(1)}, f32[3,8,64,128]{3,2,1,0:T(8,128)}, u32[]{:S(2)}) copy-start(f32[3,8,64,128]{3,2,1,0:T(8,128)} %rhs.3) | copy-start | bytes 2359300
  0.6 21.1 %copy-start = (f32[3,8,64,128]{3,2,1,0:T(8,128)S(1)}, f32[3,8,64,128]{3,2,1,0:T(8,128)}, u32[]{:S(2)}) copy-start(f32[3,8,64,128]{3,2,1,0:T(8,128)} %u.3) | copy-start | bytes 2359300
  2.6 29.9 %collective-permute-start.4 = (f32[25,64,128]{2,1,0:T(8,128)S(1)}, f32[25,64,128]{2,1,0:T(8,128)S(1)}, u32[]{:S(2)}, u32[]{:S(2)}) collective-permute-start(f32[25,64,128]{2,1,0:T(8,128)S(1)} %get-tuple-element.37), channel_id=1, source_target_pairs={{64,0},{128,64},{192,128},{256,192},{320,256},{384,320},{448,384},... | collective-permute-start | bytes 2457608 | tf_op jit(solution)/shard_map/ppermute | solution.py:464
  5.0 27.5 %collective-permute-start.5 = (f32[18,64,128]{2,1,0:T(8,128)S(1)}, f32[18,64,128]{2,1,0:T(8,128)S(1)}, u32[]{:S(2)}, u32[]{:S(2)}) collective-permute-start(f32[18,64,128]{2,1,0:T(8,128)S(1)} %get-tuple-element.38), channel_id=1, source_target_pairs={{0,64},{64,128},{128,192},{192,256},{256,320},{320,384},{384,448},... | collective-permute-start | bytes 1769480 | tf_op jit(solution)/shard_map/ppermute | solution.py:464
  9.7 13.7 %collective-permute-start = (f32[7,4,8,128]{3,2,1,0:T(8,128)S(1)}, f32[7,4,8,128]{3,2,1,0:T(8,128)S(1)}, u32[]{:S(2)}, u32[]{:S(2)}) collective-permute-start(f32[7,4,8,128]{3,2,1,0:T(8,128)S(1)} %get-tuple-element.31), channel_id=1, source_target_pairs={{0,1},{1,2},{2,3},{3,4},{4,5},{5,6},{6,7},{7,8},{8,9},{9,10},{10,1... | collective-permute-start | bytes 344072 | tf_op jit(solution)/shard_map/ppermute | solution.py:464
  11.6 12.4 %collective-permute-start.1 = (f32[7,4,8,128]{3,2,1,0:T(8,128)S(1)}, f32[7,4,8,128]{3,2,1,0:T(8,128)S(1)}, u32[]{:S(2)}, u32[]{:S(2)}) collective-permute-start(f32[7,4,8,128]{3,2,1,0:T(8,128)S(1)} %get-tuple-element.32), channel_id=1, source_target_pairs={{1,0},{2,1},{3,2},{4,3},{5,4},{6,5},{7,6},{8,7},{9,8},{10,9},{11,1... | collective-permute-start | bytes 344072 | tf_op jit(solution)/shard_map/ppermute | solution.py:464
  24.1 10.9 %collective-permute-start.2 = (f32[25,8,128]{2,1,0:T(8,128)S(1)}, f32[25,8,128]{2,1,0:T(8,128)S(1)}, u32[]{:S(2)}, u32[]{:S(2)}) collective-permute-start(f32[25,8,128]{2,1,0:T(8,128)S(1)} %get-tuple-element.35._), channel_id=1, source_target_pairs={{64,0},{128,64},{192,128},{256,192},{320,256},{384,320},{448,384},... | collective-permute-start | bytes 307208 | tf_op jit(solution)/shard_map/ppermute | solution.py:464
  26.0 9.0 %collective-permute-start.3 = (f32[18,8,128]{2,1,0:T(8,128)S(1)}, f32[18,8,128]{2,1,0:T(8,128)S(1)}, u32[]{:S(2)}, u32[]{:S(2)}) collective-permute-start(f32[18,8,128]{2,1,0:T(8,128)S(1)} %get-tuple-element.36), channel_id=1, source_target_pairs={{0,64},{64,128},{128,192},{192,256},{256,320},{320,384},{384,448},... | collective-permute-start | bytes 221192 | tf_op jit(solution)/shard_map/ppermute | solution.py:464

commit v6 on v5

--- a/solution.py
+++ b/solution.py
@@ -10,6 +10,7 @@
 OMEGA = 0.6
 COMP = 3
 BELOW = 3
+LONGEST = 21
 ABOVE = 4
 TILE = 8
 
@@ -138,9 +139,9 @@
     wide, lanes = coef.shape[-2:]
     tiles = wide // TILE
 
-    def over(step, spans):
+    def over(step, spans, width):
         for first, end in spans:
-            unroll = 3 if (end - first) % 3 == 0 else 2 if (end - first) % 2 == 0 else end - first
+            unroll = max(u for u in (1, 2, 3, 4, 6) if (end - first) % u == 0 and (u <= 2 or u * width <= LONGEST))
 
             def body(at, _):
                 step(at)
@@ -201,10 +202,10 @@
                     j += 1
                 sums.append(total(cs))
             diag = (sums[0] + weight[NEAR] * here) + (ahead(sums[1]) + behind(sums[2]))
-            inv[at, pl.ds(TILE * t, TILE)] = jnp.where(here > 0.0, 1.0 / diag, 0.0)
+            inv[at, pl.ds(TILE * t, TILE)] = jnp.where(here > 0.0, OMEGA / diag, 0.0)
 
     def coefs(spans, chosen=range(tiles)):
-        over(lambda at: coef_row(at, chosen), spans)
+        over(lambda at: coef_row(at, chosen), spans, len(chosen))
 
     def sweep(field, store, spans, chosen=range(tiles)):
         def step(at):
@@ -223,16 +224,16 @@
                     target = (sums[0] + force[c, at, here]) + (ahead(sums[1]) + behind(sums[2]))
                     store(c, at, t, part(field, (c, at), t), target * invd)
 
-        over(step, spans)
+        over(step, spans, len(chosen))
 
     def store1(c, at, t, v, target):
-        put_round(b, (c, at), t, (1.0 - OMEGA) * v + OMEGA * target)
+        put_round(b, (c, at), t, (1.0 - OMEGA) * v + target)
 
     def store2(c, at, t, v, target):
-        put_round(a, (c, at), t, (1.0 - OMEGA) * v + OMEGA * target)
+        put_round(a, (c, at), t, (1.0 - OMEGA) * v + target)
 
     def store3(c, at, t, v, target):
-        b[c, at, pl.ds(TILE * (t + 1), TILE)] = target - v
+        b[c, at, pl.ds(TILE * (t + 1), TILE)] = (1.0 / OMEGA) * target - v
 
     return (
         (lay, lay_side, lay_force, lay_force_side, of),

time: 38.9 us -> 38.2 us (0.982)
  Pallas kernels: 11.1 us -> 10.3 us
  transfers between devices with their start and end apart: 6 -> 6, of which waited for: 1 -> 1; matrix products, arithmetic and copies ran while one was open for 0% -> 0% of each run, Pallas kernels for 14% -> 13%
where the time goes in v6:
time: 38.2 us; the launch traced here: 37.9 us
  starting transfers between devices  26.1 us (68%)
  Pallas kernels  10.3 us (27%)
  between operations  0.77 us (2%)
  waiting for transfers between devices  0.71 us (2%)
    ppermute x6, starting transfers between devices, sent(): return lax.ppermute(value, axis, pairs)  26.1 us
    pallas_call x1, Pallas kernels, outer(): pl.pallas_call(outer_kernel, out_shape=shapes + [jax.ShapeDtypeStruct((CO...  3.29 us
    pallas_call x1, Pallas kernels, outer_middle(): pl.pallas_call(outer_middle_kernel, out_shape=[jax.ShapeDtypeStruct(x.sha...  2.26 us
    pallas_call x1, Pallas kernels, pack(): pl.pallas_call(pack_kernel, out_shape=[jax.ShapeDtypeStruct(s, jnp.float3...  1.94 us
    pallas_call x1, Pallas kernels, middle(): pl.pallas_call(middle_kernel, out_shape=state_shapes(*visc.shape), in_spe...  1.62 us
    pallas_call x1, Pallas kernels, inner(): pl.pallas_call(inner_kernel, out_shape=[jax.ShapeDtypeStruct(x.shape, x.d...  1.18 us
  transfers between devices with their start and end apart: 6, of which 1 were waited for; matrix products, arithmetic and copies ran while one was open for 0% of the time, Pallas kernels for 13%

profile of v6, /device:TPU:30, one launch (start us, length us, event | category | flops | bytes accessed | tf_op | source)
XLA Modules:
  0.0 37.9 jit_solution(4093411415132706663)
XLA Ops:
  0.6 0.0 copy-start.1
  0.6 0.0 copy-start
  0.7 1.9 %pack.1 = (f32[7,4,8,128]{3,2,1,0:T(8,128)S(1)}, f32[7,4,8,128]{3,2,1,0:T(8,128)S(1)}, f32[25,64,128]{2,1,0:T(8,128)S(1)}, f32[18,64,128]{2,1,0:T(8,128)S(1)}, f...) custom-call(f32[7]{0:T(128)} %wts.1, f32[3,8,64,128]{3,2,1,0:T(8,128)} %u.3, f32[3,8,64,128]{3,2,1,0:T(8,128)} %rhs.3, ...), custom_call_target="tpu_custom_call" | custom-call | bytes 4194304 | tf_op jit(solution)/shard_map/pack/pallas_call | solution.py:89
  2.6 2.4 %collective-permute-start.4 = (f32[25,64,128]{2,1,0:T(8,128)S(1)}, f32[25,64,128]{2,1,0:T(8,128)S(1)}, u32[]{:S(2)}, u32[]{:S(2)}) collective-permute-start(f32[25,64,128]{2,1,0:T(8,128)S(1)} %get-tuple-element.37), channel_id=1, source_target_pairs={{64,0},{128,64},{192,128},{256,192},{320,256},{384,320},{448,384},... | collective-permute-start | bytes 2457608 | tf_op jit(solution)/shard_map/ppermute | solution.py:465
  5.0 4.7 %collective-permute-start.5 = (f32[18,64,128]{2,1,0:T(8,128)S(1)}, f32[18,64,128]{2,1,0:T(8,128)S(1)}, u32[]{:S(2)}, u32[]{:S(2)}) collective-permute-start(f32[18,64,128]{2,1,0:T(8,128)S(1)} %get-tuple-element.38), channel_id=1, source_target_pairs={{0,64},{64,128},{128,192},{192,256},{256,320},{320,384},{384,448},... | collective-permute-start | bytes 1769480 | tf_op jit(solution)/shard_map/ppermute | solution.py:465
  9.7 1.9 %collective-permute-start = (f32[7,4,8,128]{3,2,1,0:T(8,128)S(1)}, f32[7,4,8,128]{3,2,1,0:T(8,128)S(1)}, u32[]{:S(2)}, u32[]{:S(2)}) collective-permute-start(f32[7,4,8,128]{3,2,1,0:T(8,128)S(1)} %get-tuple-element.31), channel_id=1, source_target_pairs={{0,1},{1,2},{2,3},{3,4},{4,5},{5,6},{6,7},{7,8},{8,9},{9,10},{10,1... | collective-permute-start | bytes 344072 | tf_op jit(solution)/shard_map/ppermute | solution.py:465
  11.6 10.1 %collective-permute-start.1 = (f32[7,4,8,128]{3,2,1,0:T(8,128)S(1)}, f32[7,4,8,128]{3,2,1,0:T(8,128)S(1)}, u32[]{:S(2)}, u32[]{:S(2)}) collective-permute-start(f32[7,4,8,128]{3,2,1,0:T(8,128)S(1)} %get-tuple-element.32), channel_id=1, source_target_pairs={{1,0},{2,1},{3,2},{4,3},{5,4},{6,5},{7,6},{8,7},{9,8},{10,9},{11,1... | collective-permute-start | bytes 344072 | tf_op jit(solution)/shard_map/ppermute | solution.py:465
  21.7 0.0 copy-done.1
  21.7 0.0 copy-done
  21.7 1.6 %middle.1 = (f32[3,15,88,128]{3,2,1,0:T(8,128)S(1)}, f32[3,15,88,128]{3,2,1,0:T(8,128)S(1)}, f32[3,15,72,128]{3,2,1,0:T(8,128)S(1)}, f32[15,88,128]{2,1,0:T(8,12...) custom-call(f32[15,8,128]{2,1,0:T(8,128)S(1)} %get-tuple-element.30.weight, ...), custom_call_target="tpu_custom_call" | custom-call | flops 10000000 | bytes 8388608 | tf_op jit(solution)/shard_map/middle/pallas_call | solution.py:398
  23.3 0.0 collective-permute-done.left
  23.3 0.7 %collective-permute-done.1.right = f32[7,4,8,128]{3,2,1,0:T(8,128)S(1)} collective-permute-done((f32[7,4,8,128]{3,2,1,0:T(8,128)S(1)}, f32[7,4,8,128]{3,2,1,0:T(8,128)S(1)}, u32[]{:S(2)}, u32[]{:S(2)}) %collective-permute-start.1) | collective-permute-done | bytes 114720 | tf_op jit(solution)/shard_map/ppermute | solution.py:465
  24.1 1.9 %collective-permute-start.2 = (f32[25,8,128]{2,1,0:T(8,128)S(1)}, f32[25,8,128]{2,1,0:T(8,128)S(1)}, u32[]{:S(2)}, u32[]{:S(2)}) collective-permute-start(f32[25,8,128]{2,1,0:T(8,128)S(1)} %get-tuple-element.35._), channel_id=1, source_target_pairs={{64,0},{128,64},{192,128},{256,192},{320,256},{384,320},{448,384},... | collective-permute-start | bytes 307208 | tf_op jit(solution)/shard_map/ppermute | solution.py:465
  26.0 5.1 %collective-permute-start.3 = (f32[18,8,128]{2,1,0:T(8,128)S(1)}, f32[18,8,128]{2,1,0:T(8,128)S(1)}, u32[]{:S(2)}, u32[]{:S(2)}) collective-permute-start(f32[18,8,128]{2,1,0:T(8,128)S(1)} %get-tuple-element.36), channel_id=1, source_target_pairs={{0,64},{64,128},{128,192},{192,256},{256,320},{320,384},{384,448},... | collective-permute-start | bytes 221192 | tf_op jit(solution)/shard_map/ppermute | solution.py:465
  31.1 1.2 %inner.1 = (f32[3,15,88,128]{3,2,1,0:T(8,128)S(1)}, f32[3,15,88,128]{3,2,1,0:T(8,128)S(1)}, f32[3,15,72,128]{3,2,1,0:T(8,128)S(1)}, f32[15,88,128]{2,1,0:T(8,128...) custom-call(f32[15,8,128]{2,1,0:T(8,128)S(1)} %get-tuple-element.30., ...), custom_call_target="tpu_custom_call", output_to_operand_aliasing={{0}: (4, {}), {1}: (5, {}), {2}: (6, {}), {3}: (7, {}), {4}... | custom-call | flops 10000000 | bytes 8388608 | tf_op jit(solution)/shard_map/inner/pallas_call | solution.py:411
  32.3 0.0 collective-permute-done.5.below
  32.3 0.0 collective-permute-done.4.above
  32.3 2.3 %outer_middle.1 = (f32[3,15,88,128]{3,2,1,0:T(8,128)S(1)}, f32[3,15,88,128]{3,2,1,0:T(8,128)S(1)}, f32[3,15,72,128]{3,2,1,0:T(8,128)S(1)}, f32[15,88,128]{2,1,0:...) custom-call(f32[15,8,128]{2,1,0:T(8,128)S(1)} %get-tuple-element.30., ...), custom_call_target="tpu_custom_call", output_to_operand_aliasing={{0}: (3, {}), {1}: (4, {}), {2}: (5, {}), {3}: (6, {}), {4}... | custom-call | flops 10000000 | bytes 8388608 | tf_op jit(solution)/shard_map/outer_middle/pallas_call | solution.py:425
  34.6 0.0 collective-permute-done.3.below_c
  34.6 0.0 collective-permute-done.2.above_c
  34.6 3.3 %outer.1 = (f32[3,15,88,128]{3,2,1,0:T(8,128)S(1)}, f32[3,15,88,128]{3,2,1,0:T(8,128)S(1)}, f32[3,15,72,128]{3,2,1,0:T(8,128)S(1)}, f32[15,88,128]{2,1,0:T(8,128...) custom-call(f32[15,8,128]{2,1,0:T(8,128)S(1)} %get-tuple-element.30., ...), custom_call_target="tpu_custom_call", output_to_operand_aliasing={{0}: (3, {}), {1}: (4, {}), {2}: (5, {}), {3}: (6, {}), {4}... | custom-call | flops 20000000 | bytes 16777216 | tf_op jit(solution)/shard_map/outer/pallas_call | solution.py:441
  (1 shorter events, 0.0 us)
Async XLA Ops:
  0.6 21.1 %copy-start.1 = (f32[3,8,64,128]{3,2,1,0:T(8,128)S(1)}, f32[3,8,64,128]{3,2,1,0:T(8,128)}, u32[]{:S(2)}) copy-start(f32[3,8,64,128]{3,2,1,0:T(8,128)} %rhs.3) | copy-start | bytes 2359300
  0.6 21.1 %copy-start = (f32[3,8,64,128]{3,2,1,0:T(8,128)S(1)}, f32[3,8,64,128]{3,2,1,0:T(8,128)}, u32[]{:S(2)}) copy-start(f32[3,8,64,128]{3,2,1,0:T(8,128)} %u.3) | copy-start | bytes 2359300
  2.6 29.7 %collective-permute-start.4 = (f32[25,64,128]{2,1,0:T(8,128)S(1)}, f32[25,64,128]{2,1,0:T(8,128)S(1)}, u32[]{:S(2)}, u32[]{:S(2)}) collective-permute-start(f32[25,64,128]{2,1,0:T(8,128)S(1)} %get-tuple-element.37), channel_id=1, source_target_pairs={{64,0},{128,64},{192,128},{256,192},{320,256},{384,320},{448,384},... | collective-permute-start | bytes 2457608 | tf_op jit(solution)/shard_map/ppermute | solution.py:465
  5.0 27.4 %collective-permute-start.5 = (f32[18,64,128]{2,1,0:T(8,128)S(1)}, f32[18,64,128]{2,1,0:T(8,128)S(1)}, u32[]{:S(2)}, u32[]{:S(2)}) collective-permute-start(f32[18,64,128]{2,1,0:T(8,128)S(1)} %get-tuple-element.38), channel_id=1, source_target_pairs={{0,64},{64,128},{128,192},{192,256},{256,320},{320,384},{384,448},... | collective-permute-start | bytes 1769480 | tf_op jit(solution)/shard_map/ppermute | solution.py:465
  9.7 13.7 %collective-permute-start = (f32[7,4,8,128]{3,2,1,0:T(8,128)S(1)}, f32[7,4,8,128]{3,2,1,0:T(8,128)S(1)}, u32[]{:S(2)}, u32[]{:S(2)}) collective-permute-start(f32[7,4,8,128]{3,2,1,0:T(8,128)S(1)} %get-tuple-element.31), channel_id=1, source_target_pairs={{0,1},{1,2},{2,3},{3,4},{4,5},{5,6},{6,7},{7,8},{8,9},{9,10},{10,1... | collective-permute-start | bytes 344072 | tf_op jit(solution)/shard_map/ppermute | solution.py:465
  11.6 12.4 %collective-permute-start.1 = (f32[7,4,8,128]{3,2,1,0:T(8,128)S(1)}, f32[7,4,8,128]{3,2,1,0:T(8,128)S(1)}, u32[]{:S(2)}, u32[]{:S(2)}) collective-permute-start(f32[7,4,8,128]{3,2,1,0:T(8,128)S(1)} %get-tuple-element.32), channel_id=1, source_target_pairs={{1,0},{2,1},{3,2},{4,3},{5,4},{6,5},{7,6},{8,7},{9,8},{10,9},{11,1... | collective-permute-start | bytes 344072 | tf_op jit(solution)/shard_map/ppermute | solution.py:465
  24.1 10.5 %collective-permute-start.2 = (f32[25,8,128]{2,1,0:T(8,128)S(1)}, f32[25,8,128]{2,1,0:T(8,128)S(1)}, u32[]{:S(2)}, u32[]{:S(2)}) collective-permute-start(f32[25,8,128]{2,1,0:T(8,128)S(1)} %get-tuple-element.35._), channel_id=1, source_target_pairs={{64,0},{128,64},{192,128},{256,192},{320,256},{384,320},{448,384},... | collective-permute-start | bytes 307208 | tf_op jit(solution)/shard_map/ppermute | solution.py:465
  26.0 8.6 %collective-permute-start.3 = (f32[18,8,128]{2,1,0:T(8,128)S(1)}, f32[18,8,128]{2,1,0:T(8,128)S(1)}, u32[]{:S(2)}, u32[]{:S(2)}) collective-permute-start(f32[18,8,128]{2,1,0:T(8,128)S(1)} %get-tuple-element.36), channel_id=1, source_target_pairs={{0,64},{64,128},{128,192},{192,256},{256,320},{320,384},{384,448},... | collective-permute-start | bytes 221192 | tf_op jit(solution)/shard_map/ppermute | solution.py:465

commit v7 on v6

--- a/solution.py
+++ b/solution.py
@@ -37,7 +37,7 @@
     wts, u, rhs, visc, to_left, to_right, to_below, to_above, own_visc, weight, first_cols, last_cols, held, sems
 ):
     rows, cols, lanes = visc.shape
-    pairs = []
+    pairs = [(wts, held)]
     for buffer, first in ((first_cols, 0), (last_cols, cols - TILE)):
         pairs.append((u.at[:, :, pl.ds(first, TILE)], buffer.at[pl.ds(0, COMP)]))
         pairs.append((rhs.at[:, :, pl.ds(first, TILE)], buffer.at[pl.ds(COMP, COMP)]))
@@ -50,22 +50,11 @@
         for c in range(COMP):
             at = (COMP + 1) * count + c * short
             pairs.append((rhs.at[c, pl.ds(first_r, short)], buffer.at[pl.ds(at, short)]))
-    pairs.append((wts, held))
     pairs.append((visc, own_visc))
     copies = [pltpu.make_async_copy(src, dst, sems.at[i]) for i, (src, dst) in enumerate(pairs)]
     for each in copies:
         each.start()
-    for each in copies[:6]:
-        each.wait()
-    low = lax.broadcasted_iota(jnp.int32, (TILE, lanes), 0) < TILE // 2
-    for field in range(2 * COMP + 1):
-        for i in range(rows // 2):
-            a, b = first_cols[field, 2 * i], first_cols[field, 2 * i + 1]
-            to_left[field, i] = jnp.where(low, a, turned(b))
-            a, b = last_cols[field, 2 * i], last_cols[field, 2 * i + 1]
-            to_right[field, i] = jnp.where(low, turned(b), a)
-    for each in copies[6:]:
-        each.wait()
+    copies[0].wait()
     lane = lax.broadcasted_iota(jnp.int32, (TILE, lanes), 1)
     half = [0.5 * held[k] for k in range(7)]
     j = 0
@@ -75,6 +64,17 @@
             j += 1
     lost = half[2] + half[4] + half[5] + half[6]
     weight[j] = jnp.where((lane == 0) | (lane == lanes - 1), lost, 0.0)
+    for each in copies[1:7]:
+        each.wait()
+    low = lax.broadcasted_iota(jnp.int32, (TILE, lanes), 0) < TILE // 2
+    for field in range(2 * COMP + 1):
+        for i in range(rows // 2):
+            a, b = first_cols[field, 2 * i], first_cols[field, 2 * i + 1]
+            to_left[field, i] = jnp.where(low, a, turned(b))
+            a, b = last_cols[field, 2 * i], last_cols[field, 2 * i + 1]
+            to_right[field, i] = jnp.where(low, turned(b), a)
+    for each in copies[7:]:
+        each.wait()
 
 
 def shell_rows(count):

time: 38.2 us -> 38.2 us (level)
  no operation moved by 1% of the time
where the time goes in v7:
time: 38.2 us; the launch traced here: 37.9 us
  starting transfers between devices  26.1 us (68%)
  Pallas kernels  10.3 us (27%)
  between operations  0.77 us (2%)
  waiting for transfers between devices  0.71 us (2%)
    ppermute x6, starting transfers between devices, sent(): return lax.ppermute(value, axis, pairs)  26.1 us
    pallas_call x1, Pallas kernels, outer(): pl.pallas_call(outer_kernel, out_shape=shapes + [jax.ShapeDtypeStruct((CO...  3.29 us
    pallas_call x1, Pallas kernels, outer_middle(): pl.pallas_call(outer_middle_kernel, out_shape=[jax.ShapeDtypeStruct(x.sha...  2.26 us
    pallas_call x1, Pallas kernels, pack(): pl.pallas_call(pack_kernel, out_shape=[jax.ShapeDtypeStruct(s, jnp.float3...  1.93 us
    pallas_call x1, Pallas kernels, middle(): pl.pallas_call(middle_kernel, out_shape=state_shapes(*visc.shape), in_spe...  1.62 us
    pallas_call x1, Pallas kernels, inner(): pl.pallas_call(inner_kernel, out_shape=[jax.ShapeDtypeStruct(x.shape, x.d...  1.18 us
  transfers between devices with their start and end apart: 6, of which 1 were waited for; matrix products, arithmetic and copies ran while one was open for 0% of the time, Pallas kernels for 13%

profile of v7, /device:TPU:30, one launch (start us, length us, event | category | flops | bytes accessed | tf_op | source)
XLA Modules:
  0.0 37.9 jit_solution(4806202568373137004)
XLA Ops:
  0.6 0.0 copy-start.1
  0.6 0.0 copy-start
  0.7 1.9 %pack.1 = (f32[7,4,8,128]{3,2,1,0:T(8,128)S(1)}, f32[7,4,8,128]{3,2,1,0:T(8,128)S(1)}, f32[25,64,128]{2,1,0:T(8,128)S(1)}, f32[18,64,128]{2,1,0:T(8,128)S(1)}, f...) custom-call(f32[7]{0:T(128)} %wts.1, f32[3,8,64,128]{3,2,1,0:T(8,128)} %u.3, f32[3,8,64,128]{3,2,1,0:T(8,128)} %rhs.3, ...), custom_call_target="tpu_custom_call" | custom-call | bytes 4194304 | tf_op jit(solution)/shard_map/pack/pallas_call | solution.py:89
  2.6 2.4 %collective-permute-start.4 = (f32[25,64,128]{2,1,0:T(8,128)S(1)}, f32[25,64,128]{2,1,0:T(8,128)S(1)}, u32[]{:S(2)}, u32[]{:S(2)}) collective-permute-start(f32[25,64,128]{2,1,0:T(8,128)S(1)} %get-tuple-element.37), channel_id=1, source_target_pairs={{64,0},{128,64},{192,128},{256,192},{320,256},{384,320},{448,384},... | collective-permute-start | bytes 2457608 | tf_op jit(solution)/shard_map/ppermute | solution.py:465
  5.0 4.7 %collective-permute-start.5 = (f32[18,64,128]{2,1,0:T(8,128)S(1)}, f32[18,64,128]{2,1,0:T(8,128)S(1)}, u32[]{:S(2)}, u32[]{:S(2)}) collective-permute-start(f32[18,64,128]{2,1,0:T(8,128)S(1)} %get-tuple-element.38), channel_id=1, source_target_pairs={{0,64},{64,128},{128,192},{192,256},{256,320},{320,384},{384,448},... | collective-permute-start | bytes 1769480 | tf_op jit(solution)/shard_map/ppermute | solution.py:465
  9.7 1.9 %collective-permute-start = (f32[7,4,8,128]{3,2,1,0:T(8,128)S(1)}, f32[7,4,8,128]{3,2,1,0:T(8,128)S(1)}, u32[]{:S(2)}, u32[]{:S(2)}) collective-permute-start(f32[7,4,8,128]{3,2,1,0:T(8,128)S(1)} %get-tuple-element.31), channel_id=1, source_target_pairs={{0,1},{1,2},{2,3},{3,4},{4,5},{5,6},{6,7},{7,8},{8,9},{9,10},{10,1... | collective-permute-start | bytes 344072 | tf_op jit(solution)/shard_map/ppermute | solution.py:465
  11.6 10.1 %collective-permute-start.1 = (f32[7,4,8,128]{3,2,1,0:T(8,128)S(1)}, f32[7,4,8,128]{3,2,1,0:T(8,128)S(1)}, u32[]{:S(2)}, u32[]{:S(2)}) collective-permute-start(f32[7,4,8,128]{3,2,1,0:T(8,128)S(1)} %get-tuple-element.32), channel_id=1, source_target_pairs={{1,0},{2,1},{3,2},{4,3},{5,4},{6,5},{7,6},{8,7},{9,8},{10,9},{11,1... | collective-permute-start | bytes 344072 | tf_op jit(solution)/shard_map/ppermute | solution.py:465
  21.7 0.0 copy-done.1
  21.7 0.0 copy-done
  21.7 1.6 %middle.1 = (f32[3,15,88,128]{3,2,1,0:T(8,128)S(1)}, f32[3,15,88,128]{3,2,1,0:T(8,128)S(1)}, f32[3,15,72,128]{3,2,1,0:T(8,128)S(1)}, f32[15,88,128]{2,1,0:T(8,12...) custom-call(f32[15,8,128]{2,1,0:T(8,128)S(1)} %get-tuple-element.30.weight, ...), custom_call_target="tpu_custom_call" | custom-call | flops 10000000 | bytes 8388608 | tf_op jit(solution)/shard_map/middle/pallas_call | solution.py:398
  23.3 0.0 collective-permute-done.left
  23.3 0.7 %collective-permute-done.1.right = f32[7,4,8,128]{3,2,1,0:T(8,128)S(1)} collective-permute-done((f32[7,4,8,128]{3,2,1,0:T(8,128)S(1)}, f32[7,4,8,128]{3,2,1,0:T(8,128)S(1)}, u32[]{:S(2)}, u32[]{:S(2)}) %collective-permute-start.1) | collective-permute-done | bytes 114720 | tf_op jit(solution)/shard_map/ppermute | solution.py:465
  24.1 1.9 %collective-permute-start.2 = (f32[25,8,128]{2,1,0:T(8,128)S(1)}, f32[25,8,128]{2,1,0:T(8,128)S(1)}, u32[]{:S(2)}, u32[]{:S(2)}) collective-permute-start(f32[25,8,128]{2,1,0:T(8,128)S(1)} %get-tuple-element.35._), channel_id=1, source_target_pairs={{64,0},{128,64},{192,128},{256,192},{320,256},{384,320},{448,384},... | collective-permute-start | bytes 307208 | tf_op jit(solution)/shard_map/ppermute | solution.py:465
  26.0 5.1 %collective-permute-start.3 = (f32[18,8,128]{2,1,0:T(8,128)S(1)}, f32[18,8,128]{2,1,0:T(8,128)S(1)}, u32[]{:S(2)}, u32[]{:S(2)}) collective-permute-start(f32[18,8,128]{2,1,0:T(8,128)S(1)} %get-tuple-element.36), channel_id=1, source_target_pairs={{0,64},{64,128},{128,192},{192,256},{256,320},{320,384},{384,448},... | collective-permute-start | bytes 221192 | tf_op jit(solution)/shard_map/ppermute | solution.py:465
  31.1 1.2 %inner.1 = (f32[3,15,88,128]{3,2,1,0:T(8,128)S(1)}, f32[3,15,88,128]{3,2,1,0:T(8,128)S(1)}, f32[3,15,72,128]{3,2,1,0:T(8,128)S(1)}, f32[15,88,128]{2,1,0:T(8,128...) custom-call(f32[15,8,128]{2,1,0:T(8,128)S(1)} %get-tuple-element.30., ...), custom_call_target="tpu_custom_call", output_to_operand_aliasing={{0}: (4, {}), {1}: (5, {}), {2}: (6, {}), {3}: (7, {}), {4}... | custom-call | flops 10000000 | bytes 8388608 | tf_op jit(solution)/shard_map/inner/pallas_call | solution.py:411
  32.3 0.0 collective-permute-done.5.below
  32.3 0.0 collective-permute-done.4.above
  32.3 2.3 %outer_middle.1 = (f32[3,15,88,128]{3,2,1,0:T(8,128)S(1)}, f32[3,15,88,128]{3,2,1,0:T(8,128)S(1)}, f32[3,15,72,128]{3,2,1,0:T(8,128)S(1)}, f32[15,88,128]{2,1,0:...) custom-call(f32[15,8,128]{2,1,0:T(8,128)S(1)} %get-tuple-element.30., ...), custom_call_target="tpu_custom_call", output_to_operand_aliasing={{0}: (3, {}), {1}: (4, {}), {2}: (5, {}), {3}: (6, {}), {4}... | custom-call | flops 10000000 | bytes 8388608 | tf_op jit(solution)/shard_map/outer_middle/pallas_call | solution.py:425
  34.6 0.0 collective-permute-done.3.below_c
  34.6 0.0 collective-permute-done.2.above_c
  34.6 3.3 %outer.1 = (f32[3,15,88,128]{3,2,1,0:T(8,128)S(1)}, f32[3,15,88,128]{3,2,1,0:T(8,128)S(1)}, f32[3,15,72,128]{3,2,1,0:T(8,128)S(1)}, f32[15,88,128]{2,1,0:T(8,128...) custom-call(f32[15,8,128]{2,1,0:T(8,128)S(1)} %get-tuple-element.30., ...), custom_call_target="tpu_custom_call", output_to_operand_aliasing={{0}: (3, {}), {1}: (4, {}), {2}: (5, {}), {3}: (6, {}), {4}... | custom-call | flops 20000000 | bytes 16777216 | tf_op jit(solution)/shard_map/outer/pallas_call | solution.py:441
  (1 shorter events, 0.0 us)
Async XLA Ops:
  0.6 21.1 %copy-start.1 = (f32[3,8,64,128]{3,2,1,0:T(8,128)S(1)}, f32[3,8,64,128]{3,2,1,0:T(8,128)}, u32[]{:S(2)}) copy-start(f32[3,8,64,128]{3,2,1,0:T(8,128)} %rhs.3) | copy-start | bytes 2359300
  0.6 21.1 %copy-start = (f32[3,8,64,128]{3,2,1,0:T(8,128)S(1)}, f32[3,8,64,128]{3,2,1,0:T(8,128)}, u32[]{:S(2)}) copy-start(f32[3,8,64,128]{3,2,1,0:T(8,128)} %u.3) | copy-start | bytes 2359300
  2.6 29.7 %collective-permute-start.4 = (f32[25,64,128]{2,1,0:T(8,128)S(1)}, f32[25,64,128]{2,1,0:T(8,128)S(1)}, u32[]{:S(2)}, u32[]{:S(2)}) collective-permute-start(f32[25,64,128]{2,1,0:T(8,128)S(1)} %get-tuple-element.37), channel_id=1, source_target_pairs={{64,0},{128,64},{192,128},{256,192},{320,256},{384,320},{448,384},... | collective-permute-start | bytes 2457608 | tf_op jit(solution)/shard_map/ppermute | solution.py:465
  5.0 27.4 %collective-permute-start.5 = (f32[18,64,128]{2,1,0:T(8,128)S(1)}, f32[18,64,128]{2,1,0:T(8,128)S(1)}, u32[]{:S(2)}, u32[]{:S(2)}) collective-permute-start(f32[18,64,128]{2,1,0:T(8,128)S(1)} %get-tuple-element.38), channel_id=1, source_target_pairs={{0,64},{64,128},{128,192},{192,256},{256,320},{320,384},{384,448},... | collective-permute-start | bytes 1769480 | tf_op jit(solution)/shard_map/ppermute | solution.py:465
  9.7 13.7 %collective-permute-start = (f32[7,4,8,128]{3,2,1,0:T(8,128)S(1)}, f32[7,4,8,128]{3,2,1,0:T(8,128)S(1)}, u32[]{:S(2)}, u32[]{:S(2)}) collective-permute-start(f32[7,4,8,128]{3,2,1,0:T(8,128)S(1)} %get-tuple-element.31), channel_id=1, source_target_pairs={{0,1},{1,2},{2,3},{3,4},{4,5},{5,6},{6,7},{7,8},{8,9},{9,10},{10,1... | collective-permute-start | bytes 344072 | tf_op jit(solution)/shard_map/ppermute | solution.py:465
  11.6 12.4 %collective-permute-start.1 = (f32[7,4,8,128]{3,2,1,0:T(8,128)S(1)}, f32[7,4,8,128]{3,2,1,0:T(8,128)S(1)}, u32[]{:S(2)}, u32[]{:S(2)}) collective-permute-start(f32[7,4,8,128]{3,2,1,0:T(8,128)S(1)} %get-tuple-element.32), channel_id=1, source_target_pairs={{1,0},{2,1},{3,2},{4,3},{5,4},{6,5},{7,6},{8,7},{9,8},{10,9},{11,1... | collective-permute-start | bytes 344072 | tf_op jit(solution)/shard_map/ppermute | solution.py:465
  24.1 10.5 %collective-permute-start.2 = (f32[25,8,128]{2,1,0:T(8,128)S(1)}, f32[25,8,128]{2,1,0:T(8,128)S(1)}, u32[]{:S(2)}, u32[]{:S(2)}) collective-permute-start(f32[25,8,128]{2,1,0:T(8,128)S(1)} %get-tuple-element.35._), channel_id=1, source_target_pairs={{64,0},{128,64},{192,128},{256,192},{320,256},{384,320},{448,384},... | collective-permute-start | bytes 307208 | tf_op jit(solution)/shard_map/ppermute | solution.py:465
  26.0 8.6 %collective-permute-start.3 = (f32[18,8,128]{2,1,0:T(8,128)S(1)}, f32[18,8,128]{2,1,0:T(8,128)S(1)}, u32[]{:S(2)}, u32[]{:S(2)}) collective-permute-start(f32[18,8,128]{2,1,0:T(8,128)S(1)} %get-tuple-element.36), channel_id=1, source_target_pairs={{0,64},{64,128},{128,192},{192,256},{256,320},{320,384},{384,448},... | collective-permute-start | bytes 221192 | tf_op jit(solution)/shard_map/ppermute | solution.py:465
